TPU v7x, 256 devices: a whole 4x4x8 slice. The times are simulated.
256 devices in a mesh: island: 4 (over z_hi, core), fsdp: 64 (over y, x, z_lo).
Axes of the slice: x: 4, y: 4, z: 8 (z_hi: 2, z_lo: 4; z = z_hi * 4 + z_lo), core: 2. Of those that a mesh axis runs over, the one named last changes fastest.
Arguments:
- activations: bfloat16 [131072, 8192], P(('island', 'fsdp')), may hold values from -6 to 6
- out_grads: bfloat16 [131072, 512], P(('island', 'fsdp')), may hold values from -0.03125 to 0.03125
- drift: float32 [4, 8192, 512], P('island', 'fsdp'), may hold values from -4 to 4
- moment_one: float32 [4, 8192, 512], P('island', 'fsdp'), may hold values from -4 to 4
- moment_two: float32 [4, 8192, 512], P('island', 'fsdp'), may hold values from 0.1 to 2
- base: float32 [8192, 512], P('fsdp'), may hold values from -6 to 6
- outer_moment: float32 [8192, 512], P('fsdp'), may hold values from -4 to 4
Outputs:
- new_base: float32 [8192, 512], P('fsdp')
- new_outer: float32 [8192, 512], P('fsdp')
- band: float32 [2048, 128], P('fsdp')
- new_one: float32 [4, 8192, 512], P('island', 'fsdp')
- new_two: float32 [4, 8192, 512], P('island', 'fsdp')
All inputs are finite; a program needn't handle non-finite values.
Results may differ from a plain program's by a relative error of at most 0.0003.
Values may be sent and summed in bfloat16 or wider, within the bound.
No kernel may reach another device: no remote copies, remote signals or barrier semaphores. Data moves between devices by JAX's collectives and lax.ppermute only.
A program may use at most 128 MiB of HBM per device.

v0:
```python
import math

import jax
import jax.numpy as jnp
from jax import lax
from jax.sharding import PartitionSpec as P


def dct_band():
    freq = jnp.arange(16, dtype=jnp.float32)[:, None]
    place = jnp.arange(64, dtype=jnp.float32)[None, :]
    table = math.sqrt(2.0 / 64.0) * jnp.cos(math.pi * (2.0 * place + 1.0) * freq / 128.0)
    scale = jnp.where(jnp.arange(16)[:, None] == 0, 1.0 / math.sqrt(2.0), 1.0).astype(jnp.float32)
    return table * scale


def block_basis(width):
    return jnp.kron(jnp.eye(width // 64, dtype=jnp.float32), dct_band())


def inverse_band(band_part, left_basis, right_basis):
    hp = lax.Precision.HIGHEST
    inner = jnp.dot(left_basis.T, band_part, precision=hp)
    return jnp.dot(inner, right_basis, precision=hp)


def local(activations, out_grads, drift, moment_one, moment_two, base, outer_moment):
    hp = lax.Precision.HIGHEST
    row_count = drift.shape[1]
    col_count = drift.shape[2]
    grad = lax.psum_scatter(
        lax.dot_general(
            activations, out_grads, (((0,), (0,)), ((), ())), preferred_element_type=jnp.float32
        ),
        "fsdp",
        scatter_dimension=0,
        tiled=True,
    )
    first = 0.8 * moment_one[0] + 0.2 * grad
    second = 0.95 * moment_two[0] + 0.05 * grad * grad
    step = first / (1.0 - 0.8**10) / (jnp.sqrt(second / (1.0 - 0.95**10)) + 1e-08)
    theta = base + drift[0]
    delta = base - (theta - 0.3 * (step + 0.1 * theta))
    left_basis = block_basis(row_count)
    right_basis = block_basis(col_count)
    coeff = jnp.dot(jnp.dot(left_basis, delta, precision=hp), right_basis.T, precision=hp)
    groups = lax.axis_size("island")
    band = lax.psum(coeff, "island") / groups
    smooth = inverse_band(band, left_basis, right_basis)
    new_outer = 0.9 * outer_moment + smooth
    new_base = base - 0.7 * (smooth + 0.9 * new_outer)
    return (new_base, new_outer, band, first[None], second[None])


def solution(mesh):
    in_specs = (
        P(("island", "fsdp"), None),
        P(("island", "fsdp"), None),
        P("island", "fsdp", None),
        P("island", "fsdp", None),
        P("island", "fsdp", None),
        P("fsdp", None),
        P("fsdp", None),
    )
    out_specs = (
        P("fsdp", None),
        P("fsdp", None),
        P("fsdp", None),
        P("island", "fsdp", None),
        P("island", "fsdp", None),
    )
    return jax.shard_map(local, mesh=mesh, in_specs=in_specs, out_specs=out_specs, check_vma=False)
```

profile of v0, /device:TPU:1, one launch (start us, length us, event | category | flops | bytes accessed | tf_op | source)
XLA Modules:
  0.0 484.7 jit_solution(17023477894298770603)
XLA Ops:
  7.2 0.0 copy-start
  7.2 0.0 reduce-scatter.2.cloned.1.call-start
  7.2 1.0 copy-done
  8.2 11.7 %fusion.31 = f32[8192,512]{1,0:T(8,128)} fusion(bf16[512,8192]{1,0:T(8,128)(2,1)} %param.7, bf16[512,512]{1,0:T(8,128)(2,1)S(1)} %copy-done), kind=kOutput, calls=%fused_computation.43 | convolution fusion | flops 4294967296 | bytes 25690112 | tf_op jit(solution)/shard_map/dot_general | solution.py:32
  19.9 0.0 copy-start.4
  19.9 0.0 reduce-scatter.2.cloned.1.call-update
  20.0 0.1 cosine_multiply_fusion
  20.0 0.1 broadcast_multiply_fusion.1
  20.1 0.1 mul.245
  20.2 0.1 broadcast_multiply_fusion
  20.3 0.1 mul.264
  20.5 390.9 %reduce-scatter.2.cloned.1.call-done = f32[128,512]{1,0:T(8,128)} async-done(((f32[8192,512]{1,0:T(8,128)}), f32[128,512]{1,0:T(8,128)}) %reduce-scatter.2.cloned.1.call-update) | async-done | bytes 262160 | tf_op jit(solution)/shard_map/reduce_scatter | solution.py:31
  411.3 0.0 copy-done.1
  411.3 0.0 copy-done.2
  411.3 0.0 copy-done.3
  411.3 1.4 fusion.1
  412.8 0.4 fusion.32
  413.2 61.4 %psum.7 = f32[32,128]{1,0:T(8,128)S(1)} all-reduce(f32[32,128]{1,0:T(8,128)S(1)} %fusion.32), channel_id=1, replica_groups=mesh['island'=4,'fsdp'=64] {'island'}, use_global_device_ids=true, to_apply=%region_1.2 | all-reduce | flops 4096 | bytes 32768 | tf_op jit(solution)/shard_map/psum | solution.py:48
  474.5 0.0 copy-start.5
  474.5 0.3 fusion.33
  474.8 0.0 copy-done.4
  474.8 1.2 multiply_subtract_fusion
  476.0 1.8 fusion.18
  477.9 0.0 copy-done.5
  (10 shorter events, 0.0 us)
Async XLA Ops:
  7.2 1.0 copy-start
  7.2 404.2 %reduce-scatter.2.cloned.1.call-start = ((), (), s32[]{:S(2)}) async-start(), calls=%async_computation.1 | async-start | bytes 17039360 | tf_op jit(solution)/shard_map/reduce_scatter | solution.py:31
  19.9 391.5 %copy-start.1 = (f32[1,128,512]{2,1,0:T(8,128)S(1)}, f32[1,128,512]{2,1,0:T(8,128)}, u32[]{:S(2)}) copy-start(f32[1,128,512]{2,1,0:T(8,128)} %param.10) | copy-start | bytes 786436
  19.9 391.5 %copy-start.2 = (f32[1,128,512]{2,1,0:T(8,128)S(1)}, f32[1,128,512]{2,1,0:T(8,128)}, u32[]{:S(2)}) copy-start(f32[1,128,512]{2,1,0:T(8,128)} %param.11) | copy-start | bytes 786436
  19.9 391.5 %copy-start.3 = (f32[128,512]{1,0:T(8,128)S(1)}, f32[128,512]{1,0:T(8,128)}, u32[]{:S(2)}) copy-start(f32[128,512]{1,0:T(8,128)} %param.12) | copy-start | bytes 786436
  19.9 391.5 %copy-start.6 = (f32[1,128,512]{2,1,0:T(8,128)S(1)}, f32[1,128,512]{2,1,0:T(8,128)}, u32[]{:S(2)}) copy-start(f32[1,128,512]{2,1,0:T(8,128)} %param.9) | copy-start | bytes 786436
  19.9 455.0 %copy-start.4 = (f32[128,512]{1,0:T(8,128)S(1)}, f32[128,512]{1,0:T(8,128)}, u32[]{:S(2)}) copy-start(f32[128,512]{1,0:T(8,128)} %param.13) | copy-start | bytes 786436
  474.5 3.3 copy-start.5
Sparse Core Ops, SparseCore 0:
  20.0 391.2 reduce-scatter.1
where the time goes:
time: 485 us
  waiting for transfers between devices  391 us (81%)
  blocking collectives  61.4 us (13%)
  matrix products  14.9 us (3%)
  between operations  14.1 us (3%)
    reduce_scatter x1, waiting for transfers between devices, local(): lax.psum_scatter(lax.dot_general(activations, out_grads, (((0,), (0,)), (...  391 us
    psum x1, blocking collectives, local(): band = lax.psum(coeff, 'island') / groups  61.4 us
    dot_general x1, matrix products, local(): lax.dot_general(activations, out_grads, (((0,), (0,)), ((), ())), preferr...  11.7 us
  transfers between devices with their start and end apart: 1, of which 1 were waited for; matrix products, arithmetic and copies ran while one was open for 0% of the time, Pallas kernels for 0%

commit v1 on v0

--- a/solution.py
+++ b/solution.py
@@ -4,6 +4,8 @@
 import jax.numpy as jnp
 from jax import lax
 from jax.sharding import PartitionSpec as P
+
+RING = 4
 
 
 def dct_band():
@@ -18,24 +20,93 @@
     return jnp.kron(jnp.eye(width // 64, dtype=jnp.float32), dct_band())
 
 
-def inverse_band(band_part, left_basis, right_basis):
-    hp = lax.Precision.HIGHEST
-    inner = jnp.dot(left_basis.T, band_part, precision=hp)
-    return jnp.dot(inner, right_basis, precision=hp)
+def place_index(y, x, z):
+    return ((y % RING) * RING + x % RING) * RING + z % RING
+
+
+def shift(value, dy=0, dx=0, dz=0):
+    pairs = [
+        (place_index(y, x, z), place_index(y + dy, x + dx, z + dz))
+        for y in range(RING)
+        for x in range(RING)
+        for z in range(RING)
+    ]
+    return lax.ppermute(value, "fsdp", pairs)
+
+
+def narrow(value):
+    return value.astype(jnp.float16)
+
+
+def wide(value):
+    return value.astype(jnp.float32)
+
+
+def pick(blocks, y, x):
+    if isinstance(y, slice):
+        return lax.dynamic_index_in_dim(blocks[y], x, 1, keepdims=False)
+    return lax.dynamic_index_in_dim(blocks[:, x], y, 0, keepdims=False)
+
+
+def first_ring(take, place, send):
+    low, high = slice(0, 2), slice(2, 4)
+    up = send(narrow(jnp.concatenate([take(2, low), take(1, high)])), 1)
+    down = send(narrow(jnp.concatenate([take(3, low), take(2, high)])), -1)
+    last_up = send(narrow(take(1, low) + wide(up[low])), 1)
+    last_down = send(narrow(take(3, high) + wide(down[high])), -1)
+    return jnp.concatenate(
+        [
+            take(0, low) + wide(down[low]) + wide(last_up),
+            take(0, high) + wide(up[high]) + wide(last_down),
+        ]
+    )
+
+
+def second_ring(total, place, send):
+    out = lax.dynamic_index_in_dim(total, place, 0, keepdims=False)
+    for step in (2, 1, 3):
+        block = lax.dynamic_index_in_dim(total, (place + step) & 3, 0, keepdims=False)
+        out = out + wide(send(narrow(block), step))
+    return out
+
+
+def scattered_grad(activations, out_grads):
+    place = lax.axis_index("fsdp").astype(jnp.uint32)
+    y, x = place >> 4, (place >> 2) & 3
+    cut = out_grads.shape[1] // 2
+    dims = (((0,), (0,)), ((), ()))
+
+    def blocks(part):
+        full = lax.dot_general(activations, part, dims, preferred_element_type=jnp.float32)
+        return full.reshape(RING, RING, 512, cut)
+
+    left, right = blocks(out_grads[:, :cut]), blocks(out_grads[:, cut:])
+    left = first_ring(
+        lambda d, half: pick(left, half, (x + d) & 3), x, lambda v, d: shift(v, dx=d)
+    )
+    right = first_ring(
+        lambda d, half: pick(right, (y + d) & 3, half), y, lambda v, d: shift(v, dy=d)
+    )
+    left = second_ring(left, y, lambda v, d: shift(v, dy=d))
+    right = second_ring(right, x, lambda v, d: shift(v, dx=d))
+    both = narrow(jnp.concatenate([left, right], axis=1))
+    groups = [[place_index(k // 4, k, z) for z in range(RING)] for k in range(16)]
+    both = lax.all_to_all(both, "fsdp", 0, 0, axis_index_groups=groups, tiled=True)
+    return wide(both.reshape(RING, 128, 2 * cut)).sum(0)
+
+
+def island_sum(value):
+    total = value
+    for flip in (2, 3, 1):
+        total = total + lax.ppermute(value, "island", [(k, k ^ flip) for k in range(4)])
+    return total
 
 
 def local(activations, out_grads, drift, moment_one, moment_two, base, outer_moment):
     hp = lax.Precision.HIGHEST
     row_count = drift.shape[1]
     col_count = drift.shape[2]
-    grad = lax.psum_scatter(
-        lax.dot_general(
-            activations, out_grads, (((0,), (0,)), ((), ())), preferred_element_type=jnp.float32
-        ),
-        "fsdp",
-        scatter_dimension=0,
-        tiled=True,
-    )
+    grad = scattered_grad(activations, out_grads)
     first = 0.8 * moment_one[0] + 0.2 * grad
     second = 0.95 * moment_two[0] + 0.05 * grad * grad
     step = first / (1.0 - 0.8**10) / (jnp.sqrt(second / (1.0 - 0.95**10)) + 1e-08)
@@ -44,9 +115,10 @@
     left_basis = block_basis(row_count)
     right_basis = block_basis(col_count)
     coeff = jnp.dot(jnp.dot(left_basis, delta, precision=hp), right_basis.T, precision=hp)
-    groups = lax.axis_size("island")
-    band = lax.psum(coeff, "island") / groups
-    smooth = inverse_band(band, left_basis, right_basis)
+    band = island_sum(coeff) / lax.axis_size("island")
+    smooth = jnp.dot(
+        jnp.dot(left_basis.T, band, precision=hp), right_basis, precision=hp
+    )
     new_outer = 0.9 * outer_moment + smooth
     new_base = base - 0.7 * (smooth + 0.9 * new_outer)
     return (new_base, new_outer, band, first[None], second[None])

time: 485 us -> 135 us (0.28)
  waiting for transfers between devices: 391 us -> 43.2 us
  blocking collectives: 61.4 us -> 0 us
  starting transfers between devices: 0.04 us -> 42.9 us
  other arithmetic: 2.12 us -> 19.8 us
  between operations: 14.1 us -> 0.93 us
  local copies, waits for them, and re-layouts: 1.25 us -> 8.71 us
    reduce_scatter x1 -> x0, waiting for transfers between devices: 391 us -> none  [local(): lax.psum_scatter(lax.dot_general(activations, out_grads, (((0,), (0,)), (...]
    psum x1 -> x0, blocking collectives: 61.4 us -> none  [local(): band = lax.psum(coeff, 'island') / groups]
    ppermute x0 -> x17, starting transfers between devices: none -> 37.3 us  [the longest x14 18.9 us: shift(): return lax.ppermute(value, 'fsdp', pairs)]
    ppermute x0 -> x17, waiting for transfers between devices: none -> 34.5 us  [the longest x14 33.7 us: shift(): return lax.ppermute(value, 'fsdp', pairs)]
    add x0 -> x5, other arithmetic: none -> 9.3 us  [the longest x2 5.44 us: first_ring(): take(0, high) + wide(up[high]) + wide(last_down)]
    all_to_all x0 -> x1, waiting for transfers between devices: none -> 8.63 us  [scattered_grad(): lax.all_to_all(both, 'fsdp', 0, 0, axis_index_groups=groups, tiled=True)]
    all_to_all x0 -> x1, starting transfers between devices: none -> 5.63 us  [scattered_grad(): lax.all_to_all(both, 'fsdp', 0, 0, axis_index_groups=groups, tiled=True)]
    concatenate x0 -> x5, other arithmetic: none -> 5.29 us  [the longest x2 2.46 us: first_ring(): up = send(narrow(jnp.concatenate([take(2, low), take(1, high)])), 1)]
  transfers between devices with their start and end apart: 1 -> 18, of which waited for: 1 -> 12; matrix products, arithmetic and copies ran while one was open for 0% -> 23% of each run, Pallas kernels for 0% -> 0%
where the time goes in v1:
time: 135 us; the launch traced here: 133 us
  waiting for transfers between devices  43.2 us (32%)
  starting transfers between devices  42.9 us (32%)
  other arithmetic  19.8 us (15%)
  matrix products  17.2 us (13%)
  local copies, waits for them, and re-layouts  8.71 us (6%)
    ppermute x14, waiting for transfers between devices, shift(): return lax.ppermute(value, 'fsdp', pairs)  33.7 us
    ppermute x14, starting transfers between devices, shift(): return lax.ppermute(value, 'fsdp', pairs)  18.9 us
    ppermute x3, starting transfers between devices, island_sum(): lax.ppermute(value, 'island', [(k, k ^ flip) for k in range(4)])  18.4 us
    dot_general x2, matrix products, blocks(): lax.dot_general(activations, part, dims, preferred_element_type=jnp.float32)  14.8 us
    all_to_all x1, waiting for transfers between devices, scattered_grad(): lax.all_to_all(both, 'fsdp', 0, 0, axis_index_groups=groups, tiled=True)  8.63 us
    all_to_all x1, starting transfers between devices, scattered_grad(): lax.all_to_all(both, 'fsdp', 0, 0, axis_index_groups=groups, tiled=True)  5.63 us
    add x2, other arithmetic, first_ring(): take(0, high) + wide(up[high]) + wide(last_down)  5.44 us
    slice x1, local copies, waits for them, and re-layouts, pick(): return lax.dynamic_index_in_dim(blocks[:, x], y, 0, keepdims=False)  4.01 us
  transfers between devices with their start and end apart: 18, of which 12 were waited for; matrix products, arithmetic and copies ran while one was open for 23% of the time, Pallas kernels for 0%

profile of v1, /device:TPU:1, one launch (start us, length us, event | category | flops | bytes accessed | tf_op | source)
XLA Modules:
  0.0 132.7 jit_solution(21548653861757870)
XLA Ops:
  0.6 5.8 %fusion.57 = f32[8192,256]{1,0:T(8,128)S(1)} fusion(bf16[512,8192]{1,0:T(8,128)(2,1)} %param.7, bf16[512,512]{1,0:T(8,128)(2,1)} %param.8), kind=kOutput, calls=%fused_computation.102 | convolution fusion | flops 2147483648 | bytes 17039360 | tf_op jit(solution)/shard_map/dot_general | solution.py:80
  7.3 1.6 %pad_maximum_fusion = f16[4,512,256]{2,1,0:T(8,128)(2,1)} fusion(f16[2,512,256]{2,1,0:T(8,128)(2,1)S(1)} %get-tuple-element.34, f16[2,512,256]{2,1,0:T(8,128)(2,1)S(1)} %get-tuple-element.11), kind=kLoop, calls=%fused_computation.16 | loop fusion | flops 524288 | bytes 2097152 | tf_op jit(solution)/shard_map/concatenate | solution.py:54
  10.5 3.3 %collective-permute-start = (f16[4,512,256]{2,1,0:T(8,128)(2,1)}, f16[4,512,256]{2,1,0:T(8,128)(2,1)S(1)}, u32[]{:S(2)}, u32[]{:S(2)}) collective-permute-start(f16[4,512,256]{2,1,0:T(8,128)(2,1)} %pad_maximum_fusion), channel_id=1, source_target_pairs={{0,12},{1,13},{2,14},{3,15},{4,0},{5,1},{6,2},{7,3},{8,4},{9,5},{1... | collective-permute-start | bytes 3145736 | tf_op jit(solution)/shard_map/ppermute | solution.py:34
  13.8 9.1 %fusion.55 = f32[8192,256]{1,0:T(8,128)} fusion(bf16[512,8192]{1,0:T(8,128)(2,1)} %param.7, bf16[512,512]{1,0:T(8,128)(2,1)S(1)} %copy-done.5), kind=kOutput, calls=%fused_computation.100 | convolution fusion | flops 2147483648 | bytes 17039360 | tf_op jit(solution)/shard_map/dot_general | solution.py:80
  22.9 4.0 %fusion.88 = (f32[4,2,512,256]{3,2,1,0:T(8,128)S(1)}, f32[4,2,512,256]{3,2,1,0:T(8,128)S(1)}) fusion(f32[4,4,512,256]{3,2,1,0:T(8,128)} %bitcast.132), kind=kLoop, calls=%fused_computation.140 | loop fusion | bytes 16777216 | tf_op jit(solution)/shard_map/slice | solution.py:48
  28.8 2.7 %collective-permute-start.7 = (f16[4,512,256]{2,1,0:T(8,128)(2,1)S(1)}, f16[4,512,256]{2,1,0:T(8,128)(2,1)S(1)}, u32[]{:S(2)}, u32[]{:S(2)}) collective-permute-start(f16[4,512,256]{2,1,0:T(8,128)(2,1)S(1)} %pad_maximum_fusion.2), channel_id=1, source_target_pairs={{0,48},{1,49},{2,50},{3,51},{4,52},{5,53},{6,54},{7,55},{8,56},{9,... | collective-permute-start | bytes 3145736 | tf_op jit(solution)/shard_map/ppermute | solution.py:34
  34.1 1.9 %collective-permute-done = f16[4,512,256]{2,1,0:T(8,128)(2,1)S(1)} collective-permute-done((f16[4,512,256]{2,1,0:T(8,128)(2,1)}, f16[4,512,256]{2,1,0:T(8,128)(2,1)S(1)}, u32[]{:S(2)}, u32[]{:S(2)}) %collective-permute-start) | collective-permute-done | bytes 1048608 | tf_op jit(solution)/shard_map/ppermute | solution.py:34
  36.0 2.2 %fusion.4 = f16[2,512,256]{2,1,0:T(8,128)(2,1)} fusion(f32[2,4,512,256]{3,2,1,0:T(8,128)} %bitcast.137, u32[]{:T(128)S(6)} %and.21, f16[4,512,256]{2,1,0:T(8,128)(2,1)S(1)} %collective-permute-done), kind=kLoop, calls=%fused_computation.32 | loop fusion | flops 786432 | bytes 2097156 | tf_op jit(solution)/shard_map/convert_element_type | solution.py:38
  38.1 3.3 %collective-permute-start.3 = (f16[2,512,256]{2,1,0:T(8,128)(2,1)}, f16[2,512,256]{2,1,0:T(8,128)(2,1)}, u32[]{:S(2)}, u32[]{:S(2)}) collective-permute-start(f16[2,512,256]{2,1,0:T(8,128)(2,1)} %fusion.4), channel_id=1, source_target_pairs={{0,12},{1,13},{2,14},{3,15},{4,0},{5,1},{6,2},{7,3},{8,4},{9,5},{1... | collective-permute-start | bytes 1572872 | tf_op jit(solution)/shard_map/ppermute | solution.py:34
  41.4 11.6 %collective-permute-done.7 = f16[4,512,256]{2,1,0:T(8,128)(2,1)S(1)} collective-permute-done((f16[4,512,256]{2,1,0:T(8,128)(2,1)S(1)}, f16[4,512,256]{2,1,0:T(8,128)(2,1)S(1)}, u32[]{:S(2)}, u32[]{:S(2)}) %collective-permute-start.7) | collective-permute-done | bytes 1048608 | tf_op jit(solution)/shard_map/ppermute | solution.py:34
  54.1 3.4 %collective-permute-start.10 = (f16[2,512,256]{2,1,0:T(8,128)(2,1)}, f16[2,512,256]{2,1,0:T(8,128)(2,1)}, u32[]{:S(2)}, u32[]{:S(2)}) collective-permute-start(f16[2,512,256]{2,1,0:T(8,128)(2,1)} %fusion), channel_id=1, source_target_pairs={{0,48},{1,49},{2,50},{3,51},{4,52},{5,53},{6,54},{7,55},{8,56},{9,... | collective-permute-start | bytes 1572872 | tf_op jit(solution)/shard_map/ppermute | solution.py:34
  58.7 3.1 %fusion.5 = (f32[2,512,256]{2,1,0:T(8,128)S(1)}, f16[2,512,256]{2,1,0:T(8,128)(2,1)}) fusion(f16[2,512,256]{2,1,0:T(8,128)(2,1)} %collective-permute-done.3, f32[2,4,512,256]{3,2,1,0:T(8,128)} %bitcast.138, u32[]{:T(128)S(6)} %and.20, f16[4,512,256]{2,1,0:T(8,128)(2,1)} %copy-done.4, f32[2,4,512,256]{3,2,1,0:T(8,128)} %bitcast.134, u32[]{:T(128)S(6)} %and.46), kind=kLoop, calls=%fused_computation.34 | loop fusion | flops 1835008 | bytes 5242888 | tf_op jit(solution)/shard_map/add | solution.py:60
  61.9 5.3 %collective-permute-done.10 = f16[2,512,256]{2,1,0:T(8,128)(2,1)} collective-permute-done((f16[2,512,256]{2,1,0:T(8,128)(2,1)}, f16[2,512,256]{2,1,0:T(8,128)(2,1)}, u32[]{:S(2)}, u32[]{:S(2)}) %collective-permute-start.10) | collective-permute-done | bytes 524320 | tf_op jit(solution)/shard_map/ppermute | solution.py:34
  67.1 2.3 %fusion.1 = (f32[2,512,256]{2,1,0:T(8,128)S(1)}, f16[2,512,256]{2,1,0:T(8,128)(2,1)S(1)}) fusion(f16[2,512,256]{2,1,0:T(8,128)(2,1)} %collective-permute-done.10, f32[4,2,512,256]{3,2,1,0:T(8,128)} %copy-done.3, u32[]{:T(128)S(6)} %and.50, f16[4,512,256]{2,1,0:T(8,128)(2,1)} %collective-permute-done.8, f32[4,2,512,256]{3,2,1,0:T(8,128)} %copy-done.1, u32[]{:T(128)S(6)} %and.48), kind=kLoop, calls=%fused_computation.26 | loop fusion | flops 1835008 | bytes 5242888 | tf_op jit(solution)/shard_map/add | solution.py:60
  69.6 5.2 %collective-permute-done.2 = f16[2,512,256]{2,1,0:T(8,128)(2,1)} collective-permute-done((f16[2,512,256]{2,1,0:T(8,128)(2,1)}, f16[2,512,256]{2,1,0:T(8,128)(2,1)}, u32[]{:S(2)}, u32[]{:S(2)}) %collective-permute-start.2) | collective-permute-done | bytes 524320 | tf_op jit(solution)/shard_map/ppermute | solution.py:34
  77.6 2.7 %collective-permute-start.6 = (f16[512,256]{1,0:T(8,128)(2,1)S(1)}, f16[512,256]{1,0:T(8,128)(2,1)S(1)}, u32[]{:S(2)}, u32[]{:S(2)}) collective-permute-start(f16[512,256]{1,0:T(8,128)(2,1)S(1)} %get-tuple-element.21), channel_id=1, source_target_pairs={{0,48},{1,49},{2,50},{3,51},{4,52},{5,53},{6,54},{7,55},{8,56},{9,... | collective-permute-start | bytes 786440 | tf_op jit(solution)/shard_map/ppermute | solution.py:34
  80.3 2.1 %collective-permute-done.9 = f16[2,512,256]{2,1,0:T(8,128)(2,1)S(1)} collective-permute-done((f16[2,512,256]{2,1,0:T(8,128)(2,1)S(1)}, f16[2,512,256]{2,1,0:T(8,128)(2,1)S(1)}, u32[]{:S(2)}, u32[]{:S(2)}) %collective-permute-start.9) | collective-permute-done | bytes 524320 | tf_op jit(solution)/shard_map/ppermute | solution.py:34
  85.7 2.9 %collective-permute-done.4 = f16[512,256]{1,0:T(8,128)(2,1)S(1)} collective-permute-done((f16[512,256]{1,0:T(8,128)(2,1)S(1)}, f16[512,256]{1,0:T(8,128)(2,1)S(1)}, u32[]{:S(2)}, u32[]{:S(2)}) %collective-permute-start.4) | collective-permute-done | bytes 262176 | tf_op jit(solution)/shard_map/ppermute | solution.py:34
  89.5 2.2 %collective-permute-done.5 = f16[512,256]{1,0:T(8,128)(2,1)S(1)} collective-permute-done((f16[512,256]{1,0:T(8,128)(2,1)S(1)}, f16[512,256]{1,0:T(8,128)(2,1)S(1)}, u32[]{:S(2)}, u32[]{:S(2)}) %collective-permute-start.5) | collective-permute-done | bytes 262176 | tf_op jit(solution)/shard_map/ppermute | solution.py:34
  92.0 2.1 %collective-permute-done.12 = f16[512,256]{1,0:T(8,128)(2,1)S(1)} collective-permute-done((f16[512,256]{1,0:T(8,128)(2,1)S(1)}, f16[512,256]{1,0:T(8,128)(2,1)S(1)}, u32[]{:S(2)}, u32[]{:S(2)}) %collective-permute-start.12) | collective-permute-done | bytes 262176 | tf_op jit(solution)/shard_map/ppermute | solution.py:34
  95.3 5.6 %all-to-all-start = ((f16[4,128,512]{2,1,0:T(8,128)(2,1)}), f16[4,128,512]{2,1,0:T(8,128)(2,1)S(1)}, u32[]{:S(2)}, u32[]{:S(2)}) async-start(f16[4,128,512]{2,1,0:T(8,128)(2,1)} %pad_maximum_fusion.4), calls=%async_computation | async-start | bytes 1048576 | tf_op jit(solution)/shard_map/all_to_all | solution.py:94
  101.4 8.6 %all-to-all-done = f16[4,128,512]{2,1,0:T(8,128)(2,1)S(1)} async-done(((f16[4,128,512]{2,1,0:T(8,128)(2,1)}), f16[4,128,512]{2,1,0:T(8,128)(2,1)S(1)}, u32[]{:S(2)}, u32[]{:S(2)}) %all-to-all-start) | async-done | bytes 524320 | tf_op jit(solution)/shard_map/all_to_all | solution.py:94
  111.1 4.8 %collective-permute-start.14 = (f32[32,128]{1,0:T(8,128)S(1)}, f32[32,128]{1,0:T(8,128)S(1)}, u32[]{:S(2)}, u32[]{:S(2)}) collective-permute-start(f32[32,128]{1,0:T(8,128)S(1)} %fusion.89), channel_id=1, source_target_pairs={{0,128},{64,192},{128,0},{192,64},{1,129},{65,193},{129,1},{193,65... | collective-permute-start | bytes 49160 | tf_op jit(solution)/shard_map/ppermute | solution.py:101
  115.9 13.6 %collective-permute-start.15 = (f32[32,128]{1,0:T(8,128)S(1)}, f32[32,128]{1,0:T(8,128)S(1)}, u32[]{:S(2)}, u32[]{:S(2)}) collective-permute-start(f32[32,128]{1,0:T(8,128)S(1)} %fusion.89), channel_id=1, source_target_pairs={{0,192},{64,128},{128,64},{192,0},{1,193},{65,129},{129,65},{193,1... | collective-permute-start | bytes 49160 | tf_op jit(solution)/shard_map/ppermute | solution.py:101
  (73 shorter events, 22.2 us)
Async XLA Ops:
  10.5 25.5 %collective-permute-start = (f16[4,512,256]{2,1,0:T(8,128)(2,1)}, f16[4,512,256]{2,1,0:T(8,128)(2,1)S(1)}, u32[]{:S(2)}, u32[]{:S(2)}) collective-permute-start(f16[4,512,256]{2,1,0:T(8,128)(2,1)} %pad_maximum_fusion), channel_id=1, source_target_pairs={{0,12},{1,13},{2,14},{3,15},{4,0},{5,1},{6,2},{7,3},{8,4},{9,5},{1... | collective-permute-start | bytes 3145736 | tf_op jit(solution)/shard_map/ppermute | solution.py:34
  26.9 26.2 %copy-start.3 = (f32[4,2,512,256]{3,2,1,0:T(8,128)}, f32[4,2,512,256]{3,2,1,0:T(8,128)S(1)}, u32[]{:S(2)}) copy-start(f32[4,2,512,256]{3,2,1,0:T(8,128)S(1)} %get-tuple-element.9) | copy-start | bytes 12582916
  28.8 24.2 %collective-permute-start.7 = (f16[4,512,256]{2,1,0:T(8,128)(2,1)S(1)}, f16[4,512,256]{2,1,0:T(8,128)(2,1)S(1)}, u32[]{:S(2)}, u32[]{:S(2)}) collective-permute-start(f16[4,512,256]{2,1,0:T(8,128)(2,1)S(1)} %pad_maximum_fusion.2), channel_id=1, source_target_pairs={{0,48},{1,49},{2,50},{3,51},{4,52},{5,53},{6,54},{7,55},{8,56},{9,... | collective-permute-start | bytes 3145736 | tf_op jit(solution)/shard_map/ppermute | solution.py:34
  32.8 24.9 %collective-permute-start.1 = (f16[4,512,256]{2,1,0:T(8,128)(2,1)}, f16[4,512,256]{2,1,0:T(8,128)(2,1)S(1)}, u32[]{:S(2)}, u32[]{:S(2)}) collective-permute-start(f16[4,512,256]{2,1,0:T(8,128)(2,1)} %pad_maximum_fusion.1), channel_id=1, source_target_pairs={{0,4},{1,5},{2,6},{3,7},{4,8},{5,9},{6,10},{7,11},{8,12},{9,13},{1... | collective-permute-start | bytes 3145736 | tf_op jit(solution)/shard_map/ppermute | solution.py:34
  34.0 27.8 %collective-permute-start.8 = (f16[4,512,256]{2,1,0:T(8,128)(2,1)}, f16[4,512,256]{2,1,0:T(8,128)(2,1)}, u32[]{:S(2)}, u32[]{:S(2)}) collective-permute-start(f16[4,512,256]{2,1,0:T(8,128)(2,1)} %pad_maximum_fusion.3), channel_id=1, source_target_pairs={{0,16},{1,17},{2,18},{3,19},{4,20},{5,21},{6,22},{7,23},{8,24},{9,... | collective-permute-start | bytes 3145736 | tf_op jit(solution)/shard_map/ppermute | solution.py:34
  38.1 20.6 %collective-permute-start.3 = (f16[2,512,256]{2,1,0:T(8,128)(2,1)}, f16[2,512,256]{2,1,0:T(8,128)(2,1)}, u32[]{:S(2)}, u32[]{:S(2)}) collective-permute-start(f16[2,512,256]{2,1,0:T(8,128)(2,1)} %fusion.4), channel_id=1, source_target_pairs={{0,12},{1,13},{2,14},{3,15},{4,0},{5,1},{6,2},{7,3},{8,4},{9,5},{1... | collective-permute-start | bytes 1572872 | tf_op jit(solution)/shard_map/ppermute | solution.py:34
  54.1 13.1 %collective-permute-start.10 = (f16[2,512,256]{2,1,0:T(8,128)(2,1)}, f16[2,512,256]{2,1,0:T(8,128)(2,1)}, u32[]{:S(2)}, u32[]{:S(2)}) collective-permute-start(f16[2,512,256]{2,1,0:T(8,128)(2,1)} %fusion), channel_id=1, source_target_pairs={{0,48},{1,49},{2,50},{3,51},{4,52},{5,53},{6,54},{7,55},{8,56},{9,... | collective-permute-start | bytes 1572872 | tf_op jit(solution)/shard_map/ppermute | solution.py:34
  61.8 12.9 %collective-permute-start.2 = (f16[2,512,256]{2,1,0:T(8,128)(2,1)}, f16[2,512,256]{2,1,0:T(8,128)(2,1)}, u32[]{:S(2)}, u32[]{:S(2)}) collective-permute-start(f16[2,512,256]{2,1,0:T(8,128)(2,1)} %get-tuple-element.26), channel_id=1, source_target_pairs={{0,4},{1,5},{2,6},{3,7},{4,8},{5,9},{6,10},{7,11},{8,12},{9,13},{1... | collective-permute-start | bytes 1572872 | tf_op jit(solution)/shard_map/ppermute | solution.py:34
  69.5 12.9 %collective-permute-start.9 = (f16[2,512,256]{2,1,0:T(8,128)(2,1)S(1)}, f16[2,512,256]{2,1,0:T(8,128)(2,1)S(1)}, u32[]{:S(2)}, u32[]{:S(2)}) collective-permute-start(f16[2,512,256]{2,1,0:T(8,128)(2,1)S(1)} %get-tuple-element.28), channel_id=1, source_target_pairs={{0,16},{1,17},{2,18},{3,19},{4,20},{5,21},{6,22},{7,23},{8,24},{9,... | collective-permute-start | bytes 1572872 | tf_op jit(solution)/shard_map/ppermute | solution.py:34
  76.6 12.1 %collective-permute-start.4 = (f16[512,256]{1,0:T(8,128)(2,1)S(1)}, f16[512,256]{1,0:T(8,128)(2,1)S(1)}, u32[]{:S(2)}, u32[]{:S(2)}) collective-permute-start(f16[512,256]{1,0:T(8,128)(2,1)S(1)} %get-tuple-element.19), channel_id=1, source_target_pairs={{0,32},{1,33},{2,34},{3,35},{4,36},{5,37},{6,38},{7,39},{8,40},{9,... | collective-permute-start | bytes 786440 | tf_op jit(solution)/shard_map/ppermute | solution.py:34
  77.6 14.1 %collective-permute-start.5 = (f16[512,256]{1,0:T(8,128)(2,1)S(1)}, f16[512,256]{1,0:T(8,128)(2,1)S(1)}, u32[]{:S(2)}, u32[]{:S(2)}) collective-permute-start(f16[512,256]{1,0:T(8,128)(2,1)S(1)} %get-tuple-element.20), channel_id=1, source_target_pairs={{0,16},{1,17},{2,18},{3,19},{4,20},{5,21},{6,22},{7,23},{8,24},{9,... | collective-permute-start | bytes 786440 | tf_op jit(solution)/shard_map/ppermute | solution.py:34
  77.6 14.1 %collective-permute-start.6 = (f16[512,256]{1,0:T(8,128)(2,1)S(1)}, f16[512,256]{1,0:T(8,128)(2,1)S(1)}, u32[]{:S(2)}, u32[]{:S(2)}) collective-permute-start(f16[512,256]{1,0:T(8,128)(2,1)S(1)} %get-tuple-element.21), channel_id=1, source_target_pairs={{0,48},{1,49},{2,50},{3,51},{4,52},{5,53},{6,54},{7,55},{8,56},{9,... | collective-permute-start | bytes 786440 | tf_op jit(solution)/shard_map/ppermute | solution.py:34
  84.2 7.8 %collective-permute-start.11 = (f16[512,256]{1,0:T(8,128)(2,1)S(1)}, f16[512,256]{1,0:T(8,128)(2,1)S(1)}, u32[]{:S(2)}, u32[]{:S(2)}) collective-permute-start(f16[512,256]{1,0:T(8,128)(2,1)S(1)} %get-tuple-element.22), channel_id=1, source_target_pairs={{0,8},{1,9},{2,10},{3,11},{4,12},{5,13},{6,14},{7,15},{8,0},{9,1},... | collective-permute-start | bytes 786440 | tf_op jit(solution)/shard_map/ppermute | solution.py:34
  84.8 9.3 %collective-permute-start.12 = (f16[512,256]{1,0:T(8,128)(2,1)S(1)}, f16[512,256]{1,0:T(8,128)(2,1)S(1)}, u32[]{:S(2)}, u32[]{:S(2)}) collective-permute-start(f16[512,256]{1,0:T(8,128)(2,1)S(1)} %get-tuple-element.23), channel_id=1, source_target_pairs={{0,4},{1,5},{2,6},{3,7},{4,8},{5,9},{6,10},{7,11},{8,12},{9,13},{1... | collective-permute-start | bytes 786440 | tf_op jit(solution)/shard_map/ppermute | solution.py:34
  88.6 5.5 %collective-permute-start.13 = (f16[512,256]{1,0:T(8,128)(2,1)S(1)}, f16[512,256]{1,0:T(8,128)(2,1)S(1)}, u32[]{:S(2)}, u32[]{:S(2)}) collective-permute-start(f16[512,256]{1,0:T(8,128)(2,1)S(1)} %get-tuple-element.24), channel_id=1, source_target_pairs={{0,12},{1,13},{2,14},{3,15},{4,0},{5,1},{6,2},{7,3},{8,4},{9,5},{1... | collective-permute-start | bytes 786440 | tf_op jit(solution)/shard_map/ppermute | solution.py:34
  91.9 18.2 %copy-start.6 = (f32[1,128,512]{2,1,0:T(8,128)S(1)}, f32[1,128,512]{2,1,0:T(8,128)}, u32[]{:S(2)}) copy-start(f32[1,128,512]{2,1,0:T(8,128)} %param.11) | copy-start | bytes 786436
  91.9 18.2 %copy-start.7 = (f32[1,128,512]{2,1,0:T(8,128)S(1)}, f32[1,128,512]{2,1,0:T(8,128)}, u32[]{:S(2)}) copy-start(f32[1,128,512]{2,1,0:T(8,128)} %param.10) | copy-start | bytes 786436
  91.9 18.2 %copy-start.8 = (f32[128,512]{1,0:T(8,128)S(1)}, f32[128,512]{1,0:T(8,128)}, u32[]{:S(2)}) copy-start(f32[128,512]{1,0:T(8,128)} %param.12) | copy-start | bytes 786436
  92.0 18.2 %copy-start.11 = (f32[1,128,512]{2,1,0:T(8,128)S(1)}, f32[1,128,512]{2,1,0:T(8,128)}, u32[]{:S(2)}) copy-start(f32[1,128,512]{2,1,0:T(8,128)} %param.9) | copy-start | bytes 786436
  94.4 37.1 %copy-start.9 = (f32[128,512]{1,0:T(8,128)S(1)}, f32[128,512]{1,0:T(8,128)}, u32[]{:S(2)}) copy-start(f32[128,512]{1,0:T(8,128)} %param.13) | copy-start | bytes 786436
  95.3 14.8 %all-to-all-start = ((f16[4,128,512]{2,1,0:T(8,128)(2,1)}), f16[4,128,512]{2,1,0:T(8,128)(2,1)S(1)}, u32[]{:S(2)}, u32[]{:S(2)}) async-start(f16[4,128,512]{2,1,0:T(8,128)(2,1)} %pad_maximum_fusion.4), calls=%async_computation | async-start | bytes 1048576 | tf_op jit(solution)/shard_map/all_to_all | solution.py:94
  111.1 19.3 %collective-permute-start.14 = (f32[32,128]{1,0:T(8,128)S(1)}, f32[32,128]{1,0:T(8,128)S(1)}, u32[]{:S(2)}, u32[]{:S(2)}) collective-permute-start(f32[32,128]{1,0:T(8,128)S(1)} %fusion.89), channel_id=1, source_target_pairs={{0,128},{64,192},{128,0},{192,64},{1,129},{65,193},{129,1},{193,65... | collective-permute-start | bytes 49160 | tf_op jit(solution)/shard_map/ppermute | solution.py:101
  115.9 15.3 %collective-permute-start.15 = (f32[32,128]{1,0:T(8,128)S(1)}, f32[32,128]{1,0:T(8,128)S(1)}, u32[]{:S(2)}, u32[]{:S(2)}) collective-permute-start(f32[32,128]{1,0:T(8,128)S(1)} %fusion.89), channel_id=1, source_target_pairs={{0,192},{64,128},{128,64},{192,0},{1,193},{65,129},{129,65},{193,1... | collective-permute-start | bytes 49160 | tf_op jit(solution)/shard_map/ppermute | solution.py:101
  129.4 1.7 %collective-permute-start.16 = (f32[32,128]{1,0:T(8,128)S(1)}, f32[32,128]{1,0:T(8,128)S(1)}, u32[]{:S(2)}, u32[]{:S(2)}) collective-permute-start(f32[32,128]{1,0:T(8,128)S(1)} %fusion.89), channel_id=1, source_target_pairs={{0,64},{64,0},{128,192},{192,128},{1,65},{65,1},{129,193},{193,129... | collective-permute-start | bytes 49160 | tf_op jit(solution)/shard_map/ppermute | solution.py:101
  (6 other events, 17.1 us)

commit v2 on v0

v2 whole, which is shorter than its diff:
```python
import functools
import math

import jax
import jax.numpy as jnp
import numpy as np
from jax import lax
from jax.experimental import pallas as pl
from jax.experimental.pallas import tpu as pltpu
from jax.sharding import PartitionSpec as P

RING = 4
HIGHEST = lax.Precision.HIGHEST


def block_basis(width):
    freq, place = np.arange(16.0)[:, None], np.arange(64.0)[None, :]
    table = math.sqrt(2.0 / 64.0) * np.cos(math.pi * (2.0 * place + 1.0) * freq / 128.0)
    table[0] /= math.sqrt(2.0)
    return np.kron(np.eye(width // 64), table).astype(np.float32)


def place_index(y, x, z):
    return ((y % RING) * RING + x % RING) * RING + z % RING


def shift(value, dy=0, dx=0, dz=0):
    pairs = [
        (place_index(y, x, z), place_index(y + dy, x + dx, z + dz))
        for y in range(RING)
        for x in range(RING)
        for z in range(RING)
    ]
    return lax.ppermute(value, "fsdp", pairs)


def narrow(value):
    return value.astype(jnp.float16)


def wide(value):
    return value.astype(jnp.float32)


def product_kernel(roles, a_ref, g_ref, *refs):
    outs, (held, flipped, raw, sems, g_sem) = refs[:4], refs[4:]
    width = held.shape[2]
    cut = flipped.shape[0] // 2
    place = lax.axis_index("fsdp")
    y, x = place >> 4, (place >> 2) & 3

    def named(half, role, j):
        low, high = roles[role]
        d = high + (low - high) * (j < 2)
        return ((y + j) & 3, (x + d) & 3) if half == 0 else ((y + d) & 3, (x + j) & 3)

    def fetch(spot):
        block = spot[0] * 4 + spot[1]
        start = pl.multiple_of(block * width, width)
        return pltpu.make_async_copy(
            a_ref.at[:, pl.ds(start, width)], held.at[block], sems.at[block]
        )

    def left(do):
        for role in range(2):
            for j in range(4):
                do(named(0, role, j))

    def rest(do):
        seen = {(j, roles[r][j // 2]) for r in range(2) for j in range(4)}
        for role in range(2):
            for j in range(4):
                if (roles[role][j // 2], j) not in seen:
                    do(named(1, role, j))

    bring = pltpu.make_async_copy(g_ref, raw, g_sem)
    bring.start()
    left(lambda spot: fetch(spot).start())
    rest(lambda spot: fetch(spot).start())
    bring.wait()
    flipped[...] = raw[...].T
    for half in range(2):
        part = flipped[:cut] if half == 0 else flipped[cut:]
        if half == 1:
            rest(lambda spot: fetch(spot).wait())

        def multiply(j, carry):
            spots = [named(half, role, j) for role in range(2)]
            if half == 0:
                for spot in spots:
                    fetch(spot).wait()
            for role, spot in enumerate(spots):
                block = held[spot[0] * 4 + spot[1]]
                product = jnp.dot(part, block, preferred_element_type=jnp.float32)
                for z in range(RING):
                    outs[2 * half + role][j, z] = product[:, z * 128 : (z + 1) * 128]
            return carry

        lax.fori_loop(0, RING, multiply, 0)


def products(activations, out_grads, roles):
    depth, rows = activations.shape
    count = RING * RING
    cut = out_grads.shape[1] // 2
    part = jax.ShapeDtypeStruct((RING, RING, cut, rows // count // RING), jnp.float32)
    return pl.pallas_call(
        functools.partial(product_kernel, roles),
        in_specs=[pl.BlockSpec(memory_space=pl.ANY)] * 2,
        out_specs=[pl.BlockSpec(memory_space=pltpu.VMEM)] * 4,
        out_shape=[part] * 4,
        scratch_shapes=[
            pltpu.VMEM((count, depth, rows // count), activations.dtype),
            pltpu.VMEM(out_grads.shape[::-1], out_grads.dtype),
            pltpu.VMEM(out_grads.shape, out_grads.dtype),
            pltpu.SemaphoreType.DMA((count,)),
            pltpu.SemaphoreType.DMA,
        ],
        compiler_params=pltpu.CompilerParams(vmem_limit_bytes=50 << 20),
        cost_estimate=pl.CostEstimate(
            flops=2 * rows * cut * depth, bytes_accessed=depth * rows * 2, transcendentals=0
        ),
    )(activations, out_grads)


def scattered_grad(activations, out_grads):
    sends = products(activations, out_grads, ((2, 1), (3, 2)))
    keeps = products(activations, out_grads, ((1, 3), (0, 0)))

    def along(path, value, d):
        return shift(value, dx=d) if path == 0 else shift(value, dy=d)

    def across(path, value, d):
        return shift(value, dy=d) if path == 0 else shift(value, dx=d)

    up = [along(p, narrow(sends[2 * p]), 1) for p in (0, 1)]
    down = [along(p, narrow(sends[2 * p + 1]), -1) for p in (0, 1)]
    sums = []
    for p in (0, 1):
        near, own = keeps[2 * p], keeps[2 * p + 1]
        low = along(p, narrow(near[:2] + wide(up[p][:2])), 1)
        high = along(p, narrow(near[2:] + wide(down[p][2:])), -1)
        low = own[:2] + wide(down[p][:2]) + wide(low)
        high = own[2:] + wide(up[p][2:]) + wide(high)
        total = low[0]
        for value, d in ((high[0], 2), (low[1], 1), (high[1], 3)):
            total = total + wide(across(p, narrow(value), d))
        sums.append(total)
    both = narrow(jnp.concatenate(sums, axis=1))
    groups = [[place_index(k // 4, k, z) for z in range(RING)] for k in range(16)]
    both = lax.all_to_all(both, "fsdp", 0, 0, axis_index_groups=groups, tiled=True)
    return wide(both).sum(0)


def step_kernel(grad_ref, drift, one, two, base, rows, cols, new_one, new_two, coeff):
    grad = grad_ref[...].T
    first = 0.8 * one[...] + 0.2 * grad
    second = 0.95 * two[...] + 0.05 * grad * grad
    new_one[...] = first
    new_two[...] = second
    step = first / (1.0 - 0.8**10) / (jnp.sqrt(second / (1.0 - 0.95**10)) + 1e-08)
    theta = base[...] + drift[...]
    delta = base[...] - (theta - 0.3 * (step + 0.1 * theta))
    inner = jnp.dot(rows[...], delta, precision=HIGHEST, preferred_element_type=jnp.float32)
    coeff[...] = lax.dot_general(
        inner, cols[...], (((1,), (1,)), ((), ())), precision=HIGHEST,
        preferred_element_type=jnp.float32,
    )


def outer_kernel(coeffs, base, moment, rows, cols, new_base, new_outer, band_ref):
    band = jnp.sum(coeffs[...], axis=0) / coeffs.shape[0]
    band_ref[...] = band
    inner = lax.dot_general(
        rows[...], band, (((0,), (0,)), ((), ())), precision=HIGHEST,
        preferred_element_type=jnp.float32,
    )
    smooth = jnp.dot(inner, cols[...], precision=HIGHEST, preferred_element_type=jnp.float32)
    outer = 0.9 * moment[...] + smooth
    new_outer[...] = outer
    new_base[...] = base[...] - 0.7 * (smooth + 0.9 * outer)


def on_chip(kernel, shapes, *args):
    return pl.pallas_call(
        kernel,
        in_specs=[pl.BlockSpec(memory_space=pltpu.VMEM)] * len(args),
        out_specs=[pl.BlockSpec(memory_space=pltpu.VMEM)] * len(shapes),
        out_shape=[jax.ShapeDtypeStruct(shape, jnp.float32) for shape in shapes],
    )(*args)


def every_island(value):
    return lax.all_gather(value, "island")


def local(activations, out_grads, drift, moment_one, moment_two, base, outer_moment):
    rows, cols = block_basis(drift.shape[1]), block_basis(drift.shape[2])
    grad = scattered_grad(activations, out_grads)
    full, small = drift.shape[1:], (rows.shape[0], cols.shape[0])
    first, second, coeff = on_chip(
        step_kernel, [full, full, small],
        grad, drift[0], moment_one[0], moment_two[0], base, rows, cols,
    )
    new_base, new_outer, band = on_chip(
        outer_kernel, [full, full, small], every_island(coeff), base, outer_moment, rows, cols
    )
    return (new_base, new_outer, band, first[None], second[None])


def solution(mesh):
    in_specs = (
        P(("island", "fsdp"), None),
        P(("island", "fsdp"), None),
        P("island", "fsdp", None),
        P("island", "fsdp", None),
        P("island", "fsdp", None),
        P("fsdp", None),
        P("fsdp", None),
    )
    out_specs = (
        P("fsdp", None),
        P("fsdp", None),
        P("fsdp", None),
        P("island", "fsdp", None),
        P("island", "fsdp", None),
    )
    return jax.shard_map(local, mesh=mesh, in_specs=in_specs, out_specs=out_specs, check_vma=False)
```

time: 485 us -> 110 us (0.23)
  waiting for transfers between devices: 391 us -> 27 us
  blocking collectives: 61.4 us -> 31.7 us
  starting transfers between devices: 0.04 us -> 23.8 us
  Pallas kernels: 0 us -> 20.8 us
  matrix products: 14.9 us -> 0 us
  between operations: 14.1 us -> 0.81 us
    reduce_scatter x1 -> x0, waiting for transfers between devices: 391 us -> none  [local(): lax.psum_scatter(lax.dot_general(activations, out_grads, (((0,), (0,)), (...]
    psum x1 -> x0, blocking collectives: 61.4 us -> none  [local(): band = lax.psum(coeff, 'island') / groups]
    ppermute x0 -> x14, waiting for transfers between devices: none -> 27 us  [shift(): return lax.ppermute(value, 'fsdp', pairs)]
    ppermute x0 -> x14, starting transfers between devices: none -> 23.8 us  [shift(): return lax.ppermute(value, 'fsdp', pairs)]
    pallas_call x0 -> x4, Pallas kernels: none -> 20.8 us  [the longest x2 15.3 us: products(): pl.pallas_call(functools.partial(product_kernel, roles), in_specs=[pl.Blo...]
    all_gather x0 -> x1, blocking collectives: none -> 17.2 us  [every_island(): return lax.all_gather(value, 'island')]
    dot_general x5 -> x0, matrix products: 14.9 us -> none  [the longest x1 11.7 us: local(): lax.dot_general(activations, out_grads, (((0,), (0,)), ((), ())), preferr...]
    all_to_all x0 -> x1, blocking collectives: none -> 14.5 us  [scattered_grad(): lax.all_to_all(both, 'fsdp', 0, 0, axis_index_groups=groups, tiled=True)]
  transfers between devices with their start and end apart: 1 -> 14, of which waited for: 1 -> 10; matrix products, arithmetic and copies ran while one was open for 0% -> 2% of each run, Pallas kernels for 0% -> 7%
where the time goes in v2:
time: 110 us; the launch traced here: 109 us
  blocking collectives  31.7 us (29%)
  waiting for transfers between devices  27 us (25%)
  starting transfers between devices  23.8 us (22%)
  Pallas kernels  20.8 us (19%)
  other arithmetic  3.77 us (3%)
  local copies, waits for them, and re-layouts  1.27 us (1%)
    ppermute x14, waiting for transfers between devices, shift(): return lax.ppermute(value, 'fsdp', pairs)  27 us
    ppermute x14, starting transfers between devices, shift(): return lax.ppermute(value, 'fsdp', pairs)  23.8 us
    all_gather x1, blocking collectives, every_island(): return lax.all_gather(value, 'island')  17.2 us
    pallas_call x2, Pallas kernels, products(): pl.pallas_call(functools.partial(product_kernel, roles), in_specs=[pl.Blo...  15.3 us
    all_to_all x1, blocking collectives, scattered_grad(): lax.all_to_all(both, 'fsdp', 0, 0, axis_index_groups=groups, tiled=True)  14.5 us
    pallas_call x2, Pallas kernels, on_chip(): pl.pallas_call(kernel, in_specs=[pl.BlockSpec(memory_space=pltpu.VMEM)] *...  5.47 us
  transfers between devices with their start and end apart: 14, of which 10 were waited for; matrix products, arithmetic and copies ran while one was open for 2% of the time, Pallas kernels for 7%

profile of v2, /device:TPU:1, one launch (start us, length us, event | category | flops | bytes accessed | tf_op | source)
XLA Modules:
  0.0 109.2 jit_solution(14471781884134612736)
XLA Ops:
  0.6 1.0 copy-done
  1.7 7.7 %shard_map.129 = (f32[4,4,256,128]{3,2,1,0:T(8,128)S(1)}, f32[4,4,256,128]{3,2,1,0:T(8,128)}, f32[4,4,256,128]{3,2,1,0:T(8,128)}, f32[4,4,256,128]{3,2,1,0:T(8,128)}) custom-call(bf16[512,8192]{1,0:T(8,128)(2,1)} %a_ref.3, bf16[512,512]{1,0:T(8,128)(2,1)S(1)} %copy-done), custom_call_target="tpu_custom_call" | custom-call | flops 2147483648 | bytes 8388608 | tf_op jit(solution)/shard_map/pallas_call | solution.py:107
  9.6 2.1 %collective-permute-start.1 = (f16[4,4,256,128]{3,2,1,0:T(8,128)(2,1)S(1)}, f16[4,4,256,128]{3,2,1,0:T(8,128)(2,1)S(1)}, u32[]{:S(2)}, u32[]{:S(2)}) collective-permute-start(f16[4,4,256,128]{3,2,1,0:T(8,128)(2,1)S(1)} %convert_element_type.108), channel_id=1, source_target_pairs={{0,4},{1,5},{2,6},{3,7},{4,8},{5,9},{6,10},{7,11},{8,12},{9,13},{1... | collective-permute-start | bytes 3145736 | tf_op jit(solution)/shard_map/ppermute | solution.py:34
  11.9 2.6 %collective-permute-start = (f16[4,4,256,128]{3,2,1,0:T(8,128)(2,1)S(1)}, f16[4,4,256,128]{3,2,1,0:T(8,128)(2,1)S(1)}, u32[]{:S(2)}, u32[]{:S(2)}) collective-permute-start(f16[4,4,256,128]{3,2,1,0:T(8,128)(2,1)S(1)} %convert_element_type.106), channel_id=1, source_target_pairs={{0,12},{1,13},{2,14},{3,15},{4,0},{5,1},{6,2},{7,3},{8,4},{9,5},{1... | collective-permute-start | bytes 3145736 | tf_op jit(solution)/shard_map/ppermute | solution.py:34
  14.8 1.4 %collective-permute-start.8 = (f16[4,4,256,128]{3,2,1,0:T(8,128)(2,1)S(1)}, f16[4,4,256,128]{3,2,1,0:T(8,128)(2,1)S(1)}, u32[]{:S(2)}, u32[]{:S(2)}) collective-permute-start(f16[4,4,256,128]{3,2,1,0:T(8,128)(2,1)S(1)} %convert_element_type.124), channel_id=1, source_target_pairs={{0,16},{1,17},{2,18},{3,19},{4,20},{5,21},{6,22},{7,23},{8,24},{9,... | collective-permute-start | bytes 3145736 | tf_op jit(solution)/shard_map/ppermute | solution.py:34
  16.4 1.5 %collective-permute-start.7 = (f16[4,4,256,128]{3,2,1,0:T(8,128)(2,1)S(1)}, f16[4,4,256,128]{3,2,1,0:T(8,128)(2,1)S(1)}, u32[]{:S(2)}, u32[]{:S(2)}) collective-permute-start(f16[4,4,256,128]{3,2,1,0:T(8,128)(2,1)S(1)} %convert_element_type.122), channel_id=1, source_target_pairs={{0,48},{1,49},{2,50},{3,51},{4,52},{5,53},{6,54},{7,55},{8,56},{9,... | collective-permute-start | bytes 3145736 | tf_op jit(solution)/shard_map/ppermute | solution.py:34
  17.9 7.7 %shard_map.128 = (f32[4,4,256,128]{3,2,1,0:T(8,128)S(1)}, f32[4,4,256,128]{3,2,1,0:T(8,128)}, f32[4,4,256,128]{3,2,1,0:T(8,128)}, f32[4,4,256,128]{3,2,1,0:T(8,128)}) custom-call(bf16[512,8192]{1,0:T(8,128)(2,1)} %a_ref.3, bf16[512,512]{1,0:T(8,128)(2,1)S(1)} %copy-done), custom_call_target="tpu_custom_call" | custom-call | flops 2147483648 | bytes 8388608 | tf_op jit(solution)/shard_map/pallas_call | solution.py:107
  25.6 8.0 %collective-permute-done.1 = f16[4,4,256,128]{3,2,1,0:T(8,128)(2,1)S(1)} collective-permute-done((f16[4,4,256,128]{3,2,1,0:T(8,128)(2,1)S(1)}, f16[4,4,256,128]{3,2,1,0:T(8,128)(2,1)S(1)}, u32[]{:S(2)}, u32[]{:S(2)}) %collective-permute-start.1) | collective-permute-done | bytes 1048608 | tf_op jit(solution)/shard_map/ppermute | solution.py:34
  33.6 1.8 %collective-permute-done = f16[4,4,256,128]{3,2,1,0:T(8,128)(2,1)S(1)} collective-permute-done((f16[4,4,256,128]{3,2,1,0:T(8,128)(2,1)S(1)}, f16[4,4,256,128]{3,2,1,0:T(8,128)(2,1)S(1)}, u32[]{:S(2)}, u32[]{:S(2)}) %collective-permute-start) | collective-permute-done | bytes 1048608 | tf_op jit(solution)/shard_map/ppermute | solution.py:34
  35.7 3.5 %collective-permute-start.3 = (f16[2,4,256,128]{3,2,1,0:T(8,128)(2,1)S(1)}, f16[2,4,256,128]{3,2,1,0:T(8,128)(2,1)S(1)}, u32[]{:S(2)}, u32[]{:S(2)}) collective-permute-start(f16[2,4,256,128]{3,2,1,0:T(8,128)(2,1)S(1)} %get-tuple-element.35), channel_id=1, source_target_pairs={{0,12},{1,13},{2,14},{3,15},{4,0},{5,1},{6,2},{7,3},{8,4},{9,5},{1... | collective-permute-start | bytes 1572872 | tf_op jit(solution)/shard_map/ppermute | solution.py:34
  40.3 3.2 %collective-permute-start.10 = (f16[2,4,256,128]{3,2,1,0:T(8,128)(2,1)S(1)}, f16[2,4,256,128]{3,2,1,0:T(8,128)(2,1)S(1)}, u32[]{:S(2)}, u32[]{:S(2)}) collective-permute-start(f16[2,4,256,128]{3,2,1,0:T(8,128)(2,1)S(1)} %get-tuple-element.39), channel_id=1, source_target_pairs={{0,48},{1,49},{2,50},{3,51},{4,52},{5,53},{6,54},{7,55},{8,56},{9,... | collective-permute-start | bytes 1572872 | tf_op jit(solution)/shard_map/ppermute | solution.py:34
  43.4 4.5 %collective-permute-done.3 = f16[2,4,256,128]{3,2,1,0:T(8,128)(2,1)S(1)} collective-permute-done((f16[2,4,256,128]{3,2,1,0:T(8,128)(2,1)S(1)}, f16[2,4,256,128]{3,2,1,0:T(8,128)(2,1)S(1)}, u32[]{:S(2)}, u32[]{:S(2)}) %collective-permute-start.3) | collective-permute-done | bytes 524320 | tf_op jit(solution)/shard_map/ppermute | solution.py:34
  47.9 3.1 %collective-permute-done.2 = f16[2,4,256,128]{3,2,1,0:T(8,128)(2,1)S(1)} collective-permute-done((f16[2,4,256,128]{3,2,1,0:T(8,128)(2,1)S(1)}, f16[2,4,256,128]{3,2,1,0:T(8,128)(2,1)S(1)}, u32[]{:S(2)}, u32[]{:S(2)}) %collective-permute-start.2) | collective-permute-done | bytes 524320 | tf_op jit(solution)/shard_map/ppermute | solution.py:34
  51.6 3.3 %collective-permute-start.5 = (f16[4,256,128]{2,1,0:T(8,128)(2,1)S(1)}, f16[4,256,128]{2,1,0:T(8,128)(2,1)S(1)}, u32[]{:S(2)}, u32[]{:S(2)}) collective-permute-start(f16[4,256,128]{2,1,0:T(8,128)(2,1)S(1)} %fusion.8), channel_id=1, source_target_pairs={{0,16},{1,17},{2,18},{3,19},{4,20},{5,21},{6,22},{7,23},{8,24},{9,... | collective-permute-start | bytes 786440 | tf_op jit(solution)/shard_map/ppermute | solution.py:34
  55.0 2.7 %collective-permute-start.4 = (f16[4,256,128]{2,1,0:T(8,128)(2,1)S(1)}, f16[4,256,128]{2,1,0:T(8,128)(2,1)S(1)}, u32[]{:S(2)}, u32[]{:S(2)}) collective-permute-start(f16[4,256,128]{2,1,0:T(8,128)(2,1)S(1)} %get-tuple-element.41), channel_id=1, source_target_pairs={{0,32},{1,33},{2,34},{3,35},{4,36},{5,37},{6,38},{7,39},{8,40},{9,... | collective-permute-start | bytes 786440 | tf_op jit(solution)/shard_map/ppermute | solution.py:34
  57.8 1.1 collective-permute-start.6
  59.5 1.5 %collective-permute-start.11 = (f16[4,256,128]{2,1,0:T(8,128)(2,1)S(1)}, f16[4,256,128]{2,1,0:T(8,128)(2,1)S(1)}, u32[]{:S(2)}, u32[]{:S(2)}) collective-permute-start(f16[4,256,128]{2,1,0:T(8,128)(2,1)S(1)} %get-tuple-element.43), channel_id=1, source_target_pairs={{0,8},{1,9},{2,10},{3,11},{4,12},{5,13},{6,14},{7,15},{8,0},{9,1},... | collective-permute-start | bytes 786440 | tf_op jit(solution)/shard_map/ppermute | solution.py:34
  61.1 2.1 %collective-permute-done.5 = f16[4,256,128]{2,1,0:T(8,128)(2,1)S(1)} collective-permute-done((f16[4,256,128]{2,1,0:T(8,128)(2,1)S(1)}, f16[4,256,128]{2,1,0:T(8,128)(2,1)S(1)}, u32[]{:S(2)}, u32[]{:S(2)}) %collective-permute-start.5) | collective-permute-done | bytes 262176 | tf_op jit(solution)/shard_map/ppermute | solution.py:34
  64.0 2.5 %collective-permute-done.4 = f16[4,256,128]{2,1,0:T(8,128)(2,1)S(1)} collective-permute-done((f16[4,256,128]{2,1,0:T(8,128)(2,1)S(1)}, f16[4,256,128]{2,1,0:T(8,128)(2,1)S(1)}, u32[]{:S(2)}, u32[]{:S(2)}) %collective-permute-start.4) | collective-permute-done | bytes 262176 | tf_op jit(solution)/shard_map/ppermute | solution.py:34
  66.9 3.1 %collective-permute-done.12 = f16[4,256,128]{2,1,0:T(8,128)(2,1)S(1)} collective-permute-done((f16[4,256,128]{2,1,0:T(8,128)(2,1)S(1)}, f16[4,256,128]{2,1,0:T(8,128)(2,1)S(1)}, u32[]{:S(2)}, u32[]{:S(2)}) %collective-permute-start.12) | collective-permute-done | bytes 262176 | tf_op jit(solution)/shard_map/ppermute | solution.py:34
  71.3 14.5 %all_to_all.5 = f16[4,512,128]{2,1,0:T(8,128)(2,1)S(1)} all-to-all(f16[4,512,128]{2,1,0:T(8,128)(2,1)S(1)} %pad_maximum_fusion), channel_id=1, replica_groups={{0,1,2,3},{4,5,6,7},{8,9,10,11},{12,13,14,15},{16,17,18,19},{20,21,22,2..., dimensions={0} | all-to-all | bytes 1048576 | tf_op jit(solution)/shard_map/all_to_all | solution.py:151
  86.6 2.9 %shard_map.130 = (f32[128,512]{1,0:T(8,128)}, f32[128,512]{1,0:T(8,128)}, f32[32,128]{1,0:T(8,128)}) custom-call(f32[512,128]{1,0:T(8,128)} %convert_reduce_fusion.grad_ref, f32[128,512]{1,0:T(8,128)} %bitcast.38, f32[128,512]{1,0:T(8,128)} %bitcast.39, f32[128,512]{1,0:T(8,128)} %bitcast.40, f32[128,512]{1,0:T(8,128)} %base.3, ...), custom_call_target="tpu_custom_call" | custom-call | tf_op jit(solution)/shard_map/pallas_call | solution.py:185
  89.4 17.2 %all-gather = f32[128,128]{1,0:T(8,128)} all-gather(f32[32,128]{1,0:T(8,128)} %get-tuple-element.27), channel_id=2, replica_groups=mesh['island'=4,'fsdp'=64] {'island'}, dimensions={0}, use_global_device_ids=true | all-gather | bytes 81920 | tf_op jit(solution)/shard_map/all_gather | solution.py:194
  106.6 2.6 %shard_map.131 = (f32[128,512]{1,0:T(8,128)}, f32[128,512]{1,0:T(8,128)}, f32[32,128]{1,0:T(8,128)}) custom-call(f32[4,32,128]{2,1,0:T(8,128)} %bitcast.41, f32[128,512]{1,0:T(8,128)} %base.3, f32[128,512]{1,0:T(8,128)} %moment.1, f32[32,128]{1,0:T(8,128)} %constant.6.clone.rows, f32[128,512]{1,0:T(8,128)} %constant.7.clone.cols), custom_call_target="tpu_custom_call" | custom-call | tf_op jit(solution)/shard_map/pallas_call | solution.py:185
  (40 shorter events, 6.7 us)
Async XLA Ops:
  0.6 1.0 copy-start
  9.4 2.4 %copy-start.3 = (f32[4,4,256,128]{3,2,1,0:T(8,128)S(1)}, f32[4,4,256,128]{3,2,1,0:T(8,128)}, u32[]{:S(2)}) copy-start(f32[4,4,256,128]{3,2,1,0:T(8,128)} %get-tuple-element.20) | copy-start | bytes 6291460
  9.6 5.0 %copy-start.2 = (f32[4,4,256,128]{3,2,1,0:T(8,128)S(1)}, f32[4,4,256,128]{3,2,1,0:T(8,128)}, u32[]{:S(2)}) copy-start(f32[4,4,256,128]{3,2,1,0:T(8,128)} %get-tuple-element.26) | copy-start | bytes 6291460
  9.6 24.0 %collective-permute-start.1 = (f16[4,4,256,128]{3,2,1,0:T(8,128)(2,1)S(1)}, f16[4,4,256,128]{3,2,1,0:T(8,128)(2,1)S(1)}, u32[]{:S(2)}, u32[]{:S(2)}) collective-permute-start(f16[4,4,256,128]{3,2,1,0:T(8,128)(2,1)S(1)} %convert_element_type.108), channel_id=1, source_target_pairs={{0,4},{1,5},{2,6},{3,7},{4,8},{5,9},{6,10},{7,11},{8,12},{9,13},{1... | collective-permute-start | bytes 3145736 | tf_op jit(solution)/shard_map/ppermute | solution.py:34
  11.9 4.2 %copy-start.1 = (f32[4,4,256,128]{3,2,1,0:T(8,128)S(1)}, f32[4,4,256,128]{3,2,1,0:T(8,128)}, u32[]{:S(2)}) copy-start(f32[4,4,256,128]{3,2,1,0:T(8,128)} %get-tuple-element.24) | copy-start | bytes 6291460
  11.9 23.5 %collective-permute-start = (f16[4,4,256,128]{3,2,1,0:T(8,128)(2,1)S(1)}, f16[4,4,256,128]{3,2,1,0:T(8,128)(2,1)S(1)}, u32[]{:S(2)}, u32[]{:S(2)}) collective-permute-start(f16[4,4,256,128]{3,2,1,0:T(8,128)(2,1)S(1)} %convert_element_type.106), channel_id=1, source_target_pairs={{0,12},{1,13},{2,14},{3,15},{4,0},{5,1},{6,2},{7,3},{8,4},{9,5},{1... | collective-permute-start | bytes 3145736 | tf_op jit(solution)/shard_map/ppermute | solution.py:34
  14.8 24.4 %collective-permute-start.8 = (f16[4,4,256,128]{3,2,1,0:T(8,128)(2,1)S(1)}, f16[4,4,256,128]{3,2,1,0:T(8,128)(2,1)S(1)}, u32[]{:S(2)}, u32[]{:S(2)}) collective-permute-start(f16[4,4,256,128]{3,2,1,0:T(8,128)(2,1)S(1)} %convert_element_type.124), channel_id=1, source_target_pairs={{0,16},{1,17},{2,18},{3,19},{4,20},{5,21},{6,22},{7,23},{8,24},{9,... | collective-permute-start | bytes 3145736 | tf_op jit(solution)/shard_map/ppermute | solution.py:34
  16.4 23.5 %collective-permute-start.7 = (f16[4,4,256,128]{3,2,1,0:T(8,128)(2,1)S(1)}, f16[4,4,256,128]{3,2,1,0:T(8,128)(2,1)S(1)}, u32[]{:S(2)}, u32[]{:S(2)}) collective-permute-start(f16[4,4,256,128]{3,2,1,0:T(8,128)(2,1)S(1)} %convert_element_type.122), channel_id=1, source_target_pairs={{0,48},{1,49},{2,50},{3,51},{4,52},{5,53},{6,54},{7,55},{8,56},{9,... | collective-permute-start | bytes 3145736 | tf_op jit(solution)/shard_map/ppermute | solution.py:34
  35.4 4.5 %copy-start.4 = (f32[4,4,256,128]{3,2,1,0:T(8,128)S(1)}, f32[4,4,256,128]{3,2,1,0:T(8,128)}, u32[]{:S(2)}) copy-start(f32[4,4,256,128]{3,2,1,0:T(8,128)} %get-tuple-element.25) | copy-start | bytes 6291460
  35.7 12.2 %collective-permute-start.3 = (f16[2,4,256,128]{3,2,1,0:T(8,128)(2,1)S(1)}, f16[2,4,256,128]{3,2,1,0:T(8,128)(2,1)S(1)}, u32[]{:S(2)}, u32[]{:S(2)}) collective-permute-start(f16[2,4,256,128]{3,2,1,0:T(8,128)(2,1)S(1)} %get-tuple-element.35), channel_id=1, source_target_pairs={{0,12},{1,13},{2,14},{3,15},{4,0},{5,1},{6,2},{7,3},{8,4},{9,5},{1... | collective-permute-start | bytes 1572872 | tf_op jit(solution)/shard_map/ppermute | solution.py:34
  39.2 11.8 %collective-permute-start.2 = (f16[2,4,256,128]{3,2,1,0:T(8,128)(2,1)S(1)}, f16[2,4,256,128]{3,2,1,0:T(8,128)(2,1)S(1)}, u32[]{:S(2)}, u32[]{:S(2)}) collective-permute-start(f16[2,4,256,128]{3,2,1,0:T(8,128)(2,1)S(1)} %get-tuple-element.36), channel_id=1, source_target_pairs={{0,4},{1,5},{2,6},{3,7},{4,8},{5,9},{6,10},{7,11},{8,12},{9,13},{1... | collective-permute-start | bytes 1572872 | tf_op jit(solution)/shard_map/ppermute | solution.py:34
  39.9 11.2 %copy-start.6 = (f32[4,4,256,128]{3,2,1,0:T(8,128)S(1)}, f32[4,4,256,128]{3,2,1,0:T(8,128)}, u32[]{:S(2)}) copy-start(f32[4,4,256,128]{3,2,1,0:T(8,128)} %get-tuple-element.19) | copy-start | bytes 6291460
  40.3 18.6 %collective-permute-start.10 = (f16[2,4,256,128]{3,2,1,0:T(8,128)(2,1)S(1)}, f16[2,4,256,128]{3,2,1,0:T(8,128)(2,1)S(1)}, u32[]{:S(2)}, u32[]{:S(2)}) collective-permute-start(f16[2,4,256,128]{3,2,1,0:T(8,128)(2,1)S(1)} %get-tuple-element.39), channel_id=1, source_target_pairs={{0,48},{1,49},{2,50},{3,51},{4,52},{5,53},{6,54},{7,55},{8,56},{9,... | collective-permute-start | bytes 1572872 | tf_op jit(solution)/shard_map/ppermute | solution.py:34
  43.4 15.4 %collective-permute-start.9 = (f16[2,4,256,128]{3,2,1,0:T(8,128)(2,1)S(1)}, f16[2,4,256,128]{3,2,1,0:T(8,128)(2,1)S(1)}, u32[]{:S(2)}, u32[]{:S(2)}) collective-permute-start(f16[2,4,256,128]{3,2,1,0:T(8,128)(2,1)S(1)} %get-tuple-element.40), channel_id=1, source_target_pairs={{0,16},{1,17},{2,18},{3,19},{4,20},{5,21},{6,22},{7,23},{8,24},{9,... | collective-permute-start | bytes 1572872 | tf_op jit(solution)/shard_map/ppermute | solution.py:34
  51.0 7.8 %copy-start.5 = (f32[4,4,256,128]{3,2,1,0:T(8,128)S(1)}, f32[4,4,256,128]{3,2,1,0:T(8,128)}, u32[]{:S(2)}) copy-start(f32[4,4,256,128]{3,2,1,0:T(8,128)} %get-tuple-element.23) | copy-start | bytes 6291460
  51.6 11.6 %collective-permute-start.5 = (f16[4,256,128]{2,1,0:T(8,128)(2,1)S(1)}, f16[4,256,128]{2,1,0:T(8,128)(2,1)S(1)}, u32[]{:S(2)}, u32[]{:S(2)}) collective-permute-start(f16[4,256,128]{2,1,0:T(8,128)(2,1)S(1)} %fusion.8), channel_id=1, source_target_pairs={{0,16},{1,17},{2,18},{3,19},{4,20},{5,21},{6,22},{7,23},{8,24},{9,... | collective-permute-start | bytes 786440 | tf_op jit(solution)/shard_map/ppermute | solution.py:34
  55.0 11.4 %collective-permute-start.4 = (f16[4,256,128]{2,1,0:T(8,128)(2,1)S(1)}, f16[4,256,128]{2,1,0:T(8,128)(2,1)S(1)}, u32[]{:S(2)}, u32[]{:S(2)}) collective-permute-start(f16[4,256,128]{2,1,0:T(8,128)(2,1)S(1)} %get-tuple-element.41), channel_id=1, source_target_pairs={{0,32},{1,33},{2,34},{3,35},{4,36},{5,37},{6,38},{7,39},{8,40},{9,... | collective-permute-start | bytes 786440 | tf_op jit(solution)/shard_map/ppermute | solution.py:34
  57.8 9.0 %collective-permute-start.6 = (f16[4,256,128]{2,1,0:T(8,128)(2,1)S(1)}, f16[4,256,128]{2,1,0:T(8,128)(2,1)S(1)}, u32[]{:S(2)}, u32[]{:S(2)}) collective-permute-start(f16[4,256,128]{2,1,0:T(8,128)(2,1)S(1)} %get-tuple-element.42), channel_id=1, source_target_pairs={{0,48},{1,49},{2,50},{3,51},{4,52},{5,53},{6,54},{7,55},{8,56},{9,... | collective-permute-start | bytes 786440 | tf_op jit(solution)/shard_map/ppermute | solution.py:34
  59.3 10.7 %collective-permute-start.12 = (f16[4,256,128]{2,1,0:T(8,128)(2,1)S(1)}, f16[4,256,128]{2,1,0:T(8,128)(2,1)S(1)}, u32[]{:S(2)}, u32[]{:S(2)}) collective-permute-start(f16[4,256,128]{2,1,0:T(8,128)(2,1)S(1)} %fusion.9), channel_id=1, source_target_pairs={{0,4},{1,5},{2,6},{3,7},{4,8},{5,9},{6,10},{7,11},{8,12},{9,13},{1... | collective-permute-start | bytes 786440 | tf_op jit(solution)/shard_map/ppermute | solution.py:34
  59.5 10.4 %collective-permute-start.11 = (f16[4,256,128]{2,1,0:T(8,128)(2,1)S(1)}, f16[4,256,128]{2,1,0:T(8,128)(2,1)S(1)}, u32[]{:S(2)}, u32[]{:S(2)}) collective-permute-start(f16[4,256,128]{2,1,0:T(8,128)(2,1)S(1)} %get-tuple-element.43), channel_id=1, source_target_pairs={{0,8},{1,9},{2,10},{3,11},{4,12},{5,13},{6,14},{7,15},{8,0},{9,1},... | collective-permute-start | bytes 786440 | tf_op jit(solution)/shard_map/ppermute | solution.py:34
  63.2 7.7 %collective-permute-start.13 = (f16[4,256,128]{2,1,0:T(8,128)(2,1)S(1)}, f16[4,256,128]{2,1,0:T(8,128)(2,1)S(1)}, u32[]{:S(2)}, u32[]{:S(2)}) collective-permute-start(f16[4,256,128]{2,1,0:T(8,128)(2,1)S(1)} %get-tuple-element.44), channel_id=1, source_target_pairs={{0,12},{1,13},{2,14},{3,15},{4,0},{5,1},{6,2},{7,3},{8,4},{9,5},{1... | collective-permute-start | bytes 786440 | tf_op jit(solution)/shard_map/ppermute | solution.py:34

commit v3 on v2

--- a/solution.py
+++ b/solution.py
@@ -10,6 +10,7 @@
 from jax.sharding import PartitionSpec as P
 
 RING = 4
+SCALE = 8.0
 HIGHEST = lax.Precision.HIGHEST
 
 
@@ -42,12 +43,12 @@
     return value.astype(jnp.float32)
 
 
-def product_kernel(roles, a_ref, g_ref, *refs):
+def product_kernel(roles, unroll, a_ref, g_ref, *refs):
     outs, (held, flipped, raw, sems, g_sem) = refs[:4], refs[4:]
     width = held.shape[2]
     cut = flipped.shape[0] // 2
     place = lax.axis_index("fsdp")
-    y, x = place >> 4, (place >> 2) & 3
+    y, x, z = place >> 4, (place >> 2) & 3, place & 3
 
     def named(half, role, j):
         low, high = roles[role]
@@ -78,7 +79,7 @@
     left(lambda spot: fetch(spot).start())
     rest(lambda spot: fetch(spot).start())
     bring.wait()
-    flipped[...] = raw[...].T
+    flipped[...] = raw[...].T * SCALE
     for half in range(2):
         part = flipped[:cut] if half == 0 else flipped[cut:]
         if half == 1:
@@ -92,20 +93,20 @@
             for role, spot in enumerate(spots):
                 block = held[spot[0] * 4 + spot[1]]
                 product = jnp.dot(part, block, preferred_element_type=jnp.float32)
-                for z in range(RING):
-                    outs[2 * half + role][j, z] = product[:, z * 128 : (z + 1) * 128]
+                for k in range(RING):
+                    outs[2 * half + role][j, k ^ z] = product[:, k * 128 : (k + 1) * 128]
             return carry
 
-        lax.fori_loop(0, RING, multiply, 0)
-
-
-def products(activations, out_grads, roles):
+        lax.fori_loop(0, RING, multiply, 0, unroll=unroll)
+
+
+def products(activations, out_grads, roles, unroll):
     depth, rows = activations.shape
     count = RING * RING
     cut = out_grads.shape[1] // 2
     part = jax.ShapeDtypeStruct((RING, RING, cut, rows // count // RING), jnp.float32)
     return pl.pallas_call(
-        functools.partial(product_kernel, roles),
+        functools.partial(product_kernel, roles, unroll),
         in_specs=[pl.BlockSpec(memory_space=pl.ANY)] * 2,
         out_specs=[pl.BlockSpec(memory_space=pltpu.VMEM)] * 4,
         out_shape=[part] * 4,
@@ -116,7 +117,7 @@
             pltpu.SemaphoreType.DMA((count,)),
             pltpu.SemaphoreType.DMA,
         ],
-        compiler_params=pltpu.CompilerParams(vmem_limit_bytes=50 << 20),
+        compiler_params=pltpu.CompilerParams(vmem_limit_bytes=44 << 20),
         cost_estimate=pl.CostEstimate(
             flops=2 * rows * cut * depth, bytes_accessed=depth * rows * 2, transcendentals=0
         ),
@@ -124,8 +125,8 @@
 
 
 def scattered_grad(activations, out_grads):
-    sends = products(activations, out_grads, ((2, 1), (3, 2)))
-    keeps = products(activations, out_grads, ((1, 3), (0, 0)))
+    sends = products(activations, out_grads, ((2, 1), (3, 2)), RING)
+    keeps = products(activations, out_grads, ((1, 3), (0, 0)), 1)
 
     def along(path, value, d):
         return shift(value, dx=d) if path == 0 else shift(value, dy=d)
@@ -145,19 +146,25 @@
         total = low[0]
         for value, d in ((high[0], 2), (low[1], 1), (high[1], 3)):
             total = total + wide(across(p, narrow(value), d))
-        sums.append(total)
-    both = narrow(jnp.concatenate(sums, axis=1))
-    groups = [[place_index(k // 4, k, z) for z in range(RING)] for k in range(16)]
-    both = lax.all_to_all(both, "fsdp", 0, 0, axis_index_groups=groups, tiled=True)
-    return wide(both).sum(0)
-
-
-def step_kernel(grad_ref, drift, one, two, base, rows, cols, new_one, new_two, coeff):
-    grad = grad_ref[...].T
-    first = 0.8 * one[...] + 0.2 * grad
-    second = 0.95 * two[...] + 0.05 * grad * grad
-    new_one[...] = first
-    new_two[...] = second
+        part = total[0]
+        for flip in (2, 3, 1):
+            pairs = [(k, k ^ flip) for k in range(RING**3)]
+            part = part + wide(lax.ppermute(narrow(total[flip]), "fsdp", pairs))
+        sums.append(part)
+    return sums
+
+
+def moments(left, right, one, two):
+    grad = jnp.concatenate([left[...], right[...]]).T * (1.0 / SCALE)
+    return 0.8 * one[...] + 0.2 * grad, 0.95 * two[...] + 0.05 * grad * grad
+
+
+def moment_kernel(left, right, one, two, new_one, new_two):
+    new_one[...], new_two[...] = moments(left, right, one, two)
+
+
+def band_kernel(left, right, one, two, drift, base, rows, cols, coeff):
+    first, second = moments(left, right, one, two)
     step = first / (1.0 - 0.8**10) / (jnp.sqrt(second / (1.0 - 0.95**10)) + 1e-08)
     theta = base[...] + drift[...]
     delta = base[...] - (theta - 0.3 * (step + 0.1 * theta))
@@ -168,8 +175,8 @@
     )
 
 
-def outer_kernel(coeffs, base, moment, rows, cols, new_base, new_outer, band_ref):
-    band = jnp.sum(coeffs[...], axis=0) / coeffs.shape[0]
+def outer_kernel(here, there, base, moment, rows, cols, new_base, new_outer, band_ref):
+    band = (here[...] + there[...]) / 4.0
     band_ref[...] = band
     inner = lax.dot_general(
         rows[...], band, (((0,), (0,)), ((), ())), precision=HIGHEST,
@@ -190,20 +197,21 @@
     )(*args)
 
 
-def every_island(value):
-    return lax.all_gather(value, "island")
+def flipped_island(value, flip):
+    return lax.ppermute(value, "island", [(k, k ^ flip) for k in range(4)])
 
 
 def local(activations, out_grads, drift, moment_one, moment_two, base, outer_moment):
     rows, cols = block_basis(drift.shape[1]), block_basis(drift.shape[2])
-    grad = scattered_grad(activations, out_grads)
+    left, right = scattered_grad(activations, out_grads)
     full, small = drift.shape[1:], (rows.shape[0], cols.shape[0])
-    first, second, coeff = on_chip(
-        step_kernel, [full, full, small],
-        grad, drift[0], moment_one[0], moment_two[0], base, rows, cols,
-    )
+    state = left, right, moment_one[0], moment_two[0]
+    (coeff,) = on_chip(band_kernel, [small], *state, drift[0], base, rows, cols)
+    chip = coeff + flipped_island(coeff, 1)
+    there = flipped_island(chip, 2)
+    first, second = on_chip(moment_kernel, [full, full], *state)
     new_base, new_outer, band = on_chip(
-        outer_kernel, [full, full, small], every_island(coeff), base, outer_moment, rows, cols
+        outer_kernel, [full, full, small], chip, there, base, outer_moment, rows, cols
     )
     return (new_base, new_outer, band, first[None], second[None])
 

time: 110 us -> 96.5 us (0.88)
  blocking collectives: 31.7 us -> 0 us
  starting transfers between devices: 23.8 us -> 40.5 us
  waiting for transfers between devices: 27 us -> 29.6 us
  Pallas kernels: 20.8 us -> 18.6 us
    ppermute x0 -> x8, starting transfers between devices: none -> 17.7 us  [the longest x2 8.94 us: flipped_island(): return lax.ppermute(value, 'island', [(k, k ^ flip) for k in range(4)])]
    all_gather x1 -> x0, blocking collectives: 17.2 us -> none  [every_island(): return lax.all_gather(value, 'island')]
    all_to_all x1 -> x0, blocking collectives: 14.5 us -> none  [scattered_grad(): lax.all_to_all(both, 'fsdp', 0, 0, axis_index_groups=groups, tiled=True)]
    ppermute x0 -> x8, waiting for transfers between devices: none -> 5.78 us  [the longest x6 4.73 us: scattered_grad(): part = part + wide(lax.ppermute(narrow(total[flip]), 'fsdp', pairs))]
    pallas_call x2, Pallas kernels: 15.3 us -> 11 us  [products(): pl.pallas_call(functools.partial(product_kernel, roles, unroll), in_specs...]
    ppermute x14, waiting for transfers between devices: 27 us -> 23.9 us  [shift(): return lax.ppermute(value, 'fsdp', pairs)]
    add x0 -> x5, other arithmetic: none -> 2.9 us  [the longest x2 1.37 us: scattered_grad(): part = part + wide(lax.ppermute(narrow(total[flip]), 'fsdp', pairs))]
    pallas_call x2 -> x3, Pallas kernels: 5.47 us -> 7.6 us  [on_chip(): pl.pallas_call(kernel, in_specs=[pl.BlockSpec(memory_space=pltpu.VMEM)] *...]
  transfers between devices with their start and end apart: 14 -> 22, of which waited for: 10 -> 9; matrix products, arithmetic and copies ran while one was open for 2% -> 4% of each run, Pallas kernels for 7% -> 8%
where the time goes in v3:
time: 96.5 us; the launch traced here: 96.2 us
  starting transfers between devices  40.5 us (42%)
  waiting for transfers between devices  29.6 us (31%)
  Pallas kernels  18.6 us (19%)
  other arithmetic  4.77 us (5%)
  local copies, waits for them, and re-layouts  1.93 us (2%)
    ppermute x14, waiting for transfers between devices, shift(): return lax.ppermute(value, 'fsdp', pairs)  23.9 us
    ppermute x14, starting transfers between devices, shift(): return lax.ppermute(value, 'fsdp', pairs)  22.8 us
    pallas_call x2, Pallas kernels, products(): pl.pallas_call(functools.partial(product_kernel, roles, unroll), in_specs...  11 us
    ppermute x2, starting transfers between devices, flipped_island(): return lax.ppermute(value, 'island', [(k, k ^ flip) for k in range(4)])  8.94 us
    ppermute x6, starting transfers between devices, scattered_grad(): part = part + wide(lax.ppermute(narrow(total[flip]), 'fsdp', pairs))  8.74 us
    pallas_call x3, Pallas kernels, on_chip(): pl.pallas_call(kernel, in_specs=[pl.BlockSpec(memory_space=pltpu.VMEM)] *...  7.6 us
    ppermute x6, waiting for transfers between devices, scattered_grad(): part = part + wide(lax.ppermute(narrow(total[flip]), 'fsdp', pairs))  4.73 us
  transfers between devices with their start and end apart: 22, of which 9 were waited for; matrix products, arithmetic and copies ran while one was open for 4% of the time, Pallas kernels for 8%

profile of v3, /device:TPU:1, one launch (start us, length us, event | category | flops | bytes accessed | tf_op | source)
XLA Modules:
  0.0 96.2 jit_solution(13855715241059493648)
XLA Ops:
  1.7 5.2 %shard_map.129 = (f32[4,4,256,128]{3,2,1,0:T(8,128)S(1)}, f32[4,4,256,128]{3,2,1,0:T(8,128)S(1)}, f32[4,4,256,128]{3,2,1,0:T(8,128)S(1)}, f32[4,4,256,128]{3,2,1,0:T(8,128)S(1)}) custom-call(bf16[512,8192]{1,0:T(8,128)(2,1)} %a_ref.3, bf16[512,512]{1,0:T(8,128)(2,1)S(1)} %copy-done), custom_call_target="tpu_custom_call" | custom-call | flops 2147483648 | bytes 8388608 | tf_op jit(solution)/shard_map/pallas_call | solution.py:108
  7.1 2.1 %collective-permute-start.1 = (f16[4,4,256,128]{3,2,1,0:T(8,128)(2,1)S(1)}, f16[4,4,256,128]{3,2,1,0:T(8,128)(2,1)S(1)}, u32[]{:S(2)}, u32[]{:S(2)}) collective-permute-start(f16[4,4,256,128]{3,2,1,0:T(8,128)(2,1)S(1)} %convert_element_type.146), channel_id=1, source_target_pairs={{0,4},{1,5},{2,6},{3,7},{4,8},{5,9},{6,10},{7,11},{8,12},{9,13},{1... | collective-permute-start | bytes 3145736 | tf_op jit(solution)/shard_map/ppermute | solution.py:35
  11.0 1.6 %collective-permute-start.11 = (f16[4,4,256,128]{3,2,1,0:T(8,128)(2,1)S(1)}, f16[4,4,256,128]{3,2,1,0:T(8,128)(2,1)S(1)}, u32[]{:S(2)}, u32[]{:S(2)}) collective-permute-start(f16[4,4,256,128]{3,2,1,0:T(8,128)(2,1)S(1)} %convert_element_type.168), channel_id=1, source_target_pairs={{0,16},{1,17},{2,18},{3,19},{4,20},{5,21},{6,22},{7,23},{8,24},{9,... | collective-permute-start | bytes 3145736 | tf_op jit(solution)/shard_map/ppermute | solution.py:35
  12.8 1.5 %collective-permute-start.10 = (f16[4,4,256,128]{3,2,1,0:T(8,128)(2,1)S(1)}, f16[4,4,256,128]{3,2,1,0:T(8,128)(2,1)S(1)}, u32[]{:S(2)}, u32[]{:S(2)}) collective-permute-start(f16[4,4,256,128]{3,2,1,0:T(8,128)(2,1)S(1)} %convert_element_type.166), channel_id=1, source_target_pairs={{0,48},{1,49},{2,50},{3,51},{4,52},{5,53},{6,54},{7,55},{8,56},{9,... | collective-permute-start | bytes 3145736 | tf_op jit(solution)/shard_map/ppermute | solution.py:35
  14.3 5.8 %shard_map.128 = (f32[4,4,256,128]{3,2,1,0:T(8,128)S(1)}, f32[4,4,256,128]{3,2,1,0:T(8,128)S(1)}, f32[4,4,256,128]{3,2,1,0:T(8,128)S(1)}, f32[4,4,256,128]{3,2,1,0:T(8,128)S(1)}) custom-call(bf16[512,8192]{1,0:T(8,128)(2,1)} %a_ref.3, bf16[512,512]{1,0:T(8,128)(2,1)S(1)} %copy-done), custom_call_target="tpu_custom_call" | custom-call | flops 2147483648 | bytes 8388608 | tf_op jit(solution)/shard_map/pallas_call | solution.py:108
  20.1 10.9 %collective-permute-done.1 = f16[4,4,256,128]{3,2,1,0:T(8,128)(2,1)S(1)} collective-permute-done((f16[4,4,256,128]{3,2,1,0:T(8,128)(2,1)S(1)}, f16[4,4,256,128]{3,2,1,0:T(8,128)(2,1)S(1)}, u32[]{:S(2)}, u32[]{:S(2)}) %collective-permute-start.1) | collective-permute-done | bytes 1048608 | tf_op jit(solution)/shard_map/ppermute | solution.py:35
  31.0 1.9 %collective-permute-done = f16[4,4,256,128]{3,2,1,0:T(8,128)(2,1)S(1)} collective-permute-done((f16[4,4,256,128]{3,2,1,0:T(8,128)(2,1)S(1)}, f16[4,4,256,128]{3,2,1,0:T(8,128)(2,1)S(1)}, u32[]{:S(2)}, u32[]{:S(2)}) %collective-permute-start) | collective-permute-done | bytes 1048608 | tf_op jit(solution)/shard_map/ppermute | solution.py:35
  33.2 1.6 %collective-permute-start.2 = (f16[2,4,256,128]{3,2,1,0:T(8,128)(2,1)S(1)}, f16[2,4,256,128]{3,2,1,0:T(8,128)(2,1)S(1)}, u32[]{:S(2)}, u32[]{:S(2)}) collective-permute-start(f16[2,4,256,128]{3,2,1,0:T(8,128)(2,1)S(1)} %get-tuple-element.41), channel_id=1, source_target_pairs={{0,4},{1,5},{2,6},{3,7},{4,8},{5,9},{6,10},{7,11},{8,12},{9,13},{1... | collective-permute-start | bytes 1572872 | tf_op jit(solution)/shard_map/ppermute | solution.py:35
  36.3 1.7 %collective-permute-start.12 = (f16[2,4,256,128]{3,2,1,0:T(8,128)(2,1)S(1)}, f16[2,4,256,128]{3,2,1,0:T(8,128)(2,1)S(1)}, u32[]{:S(2)}, u32[]{:S(2)}) collective-permute-start(f16[2,4,256,128]{3,2,1,0:T(8,128)(2,1)S(1)} %get-tuple-element.37), channel_id=1, source_target_pairs={{0,16},{1,17},{2,18},{3,19},{4,20},{5,21},{6,22},{7,23},{8,24},{9,... | collective-permute-start | bytes 1572872 | tf_op jit(solution)/shard_map/ppermute | solution.py:35
  38.1 1.5 %collective-permute-start.13 = (f16[2,4,256,128]{3,2,1,0:T(8,128)(2,1)S(1)}, f16[2,4,256,128]{3,2,1,0:T(8,128)(2,1)S(1)}, u32[]{:S(2)}, u32[]{:S(2)}) collective-permute-start(f16[2,4,256,128]{3,2,1,0:T(8,128)(2,1)S(1)} %get-tuple-element.38), channel_id=1, source_target_pairs={{0,48},{1,49},{2,50},{3,51},{4,52},{5,53},{6,54},{7,55},{8,56},{9,... | collective-permute-start | bytes 1572872 | tf_op jit(solution)/shard_map/ppermute | solution.py:35
  39.6 6.2 %collective-permute-done.2 = f16[2,4,256,128]{3,2,1,0:T(8,128)(2,1)S(1)} collective-permute-done((f16[2,4,256,128]{3,2,1,0:T(8,128)(2,1)S(1)}, f16[2,4,256,128]{3,2,1,0:T(8,128)(2,1)S(1)}, u32[]{:S(2)}, u32[]{:S(2)}) %collective-permute-start.2) | collective-permute-done | bytes 524320 | tf_op jit(solution)/shard_map/ppermute | solution.py:35
  46.5 1.9 %collective-permute-start.5 = (f16[4,256,128]{2,1,0:T(8,128)(2,1)S(1)}, f16[4,256,128]{2,1,0:T(8,128)(2,1)S(1)}, u32[]{:S(2)}, u32[]{:S(2)}) collective-permute-start(f16[4,256,128]{2,1,0:T(8,128)(2,1)S(1)} %fusion.6), channel_id=1, source_target_pairs={{0,16},{1,17},{2,18},{3,19},{4,20},{5,21},{6,22},{7,23},{8,24},{9,... | collective-permute-start | bytes 786440 | tf_op jit(solution)/shard_map/ppermute | solution.py:35
  48.5 2.7 %collective-permute-start.4 = (f16[4,256,128]{2,1,0:T(8,128)(2,1)S(1)}, f16[4,256,128]{2,1,0:T(8,128)(2,1)S(1)}, u32[]{:S(2)}, u32[]{:S(2)}) collective-permute-start(f16[4,256,128]{2,1,0:T(8,128)(2,1)S(1)} %get-tuple-element.45), channel_id=1, source_target_pairs={{0,32},{1,33},{2,34},{3,35},{4,36},{5,37},{6,38},{7,39},{8,40},{9,... | collective-permute-start | bytes 786440 | tf_op jit(solution)/shard_map/ppermute | solution.py:35
  53.5 3.2 %collective-permute-start.14 = (f16[4,256,128]{2,1,0:T(8,128)(2,1)S(1)}, f16[4,256,128]{2,1,0:T(8,128)(2,1)S(1)}, u32[]{:S(2)}, u32[]{:S(2)}) collective-permute-start(f16[4,256,128]{2,1,0:T(8,128)(2,1)S(1)} %get-tuple-element.43), channel_id=1, source_target_pairs={{0,8},{1,9},{2,10},{3,11},{4,12},{5,13},{6,14},{7,15},{8,0},{9,1},... | collective-permute-start | bytes 786440 | tf_op jit(solution)/shard_map/ppermute | solution.py:35
  57.4 4.6 %collective-permute-done.4 = f16[4,256,128]{2,1,0:T(8,128)(2,1)S(1)} collective-permute-done((f16[4,256,128]{2,1,0:T(8,128)(2,1)S(1)}, f16[4,256,128]{2,1,0:T(8,128)(2,1)S(1)}, u32[]{:S(2)}, u32[]{:S(2)}) %collective-permute-start.4) | collective-permute-done | bytes 262176 | tf_op jit(solution)/shard_map/ppermute | solution.py:35
  62.2 3.1 %collective-permute-start.7 = (f16[256,128]{1,0:T(8,128)(2,1)S(1)}, f16[256,128]{1,0:T(8,128)(2,1)S(1)}, u32[]{:S(2)}, u32[]{:S(2)}) collective-permute-start(f16[256,128]{1,0:T(8,128)(2,1)S(1)} %get-tuple-element.50), channel_id=1, source_target_pairs={{0,2},{1,3},{2,0},{3,1},{4,6},{5,7},{6,4},{7,5},{8,10},{9,11},{10,... | collective-permute-start | bytes 196616 | tf_op jit(solution)/shard_map/ppermute | solution.py:152
  65.3 1.6 %collective-permute-start.9 = (f16[256,128]{1,0:T(8,128)(2,1)S(1)}, f16[256,128]{1,0:T(8,128)(2,1)S(1)}, u32[]{:S(2)}, u32[]{:S(2)}) collective-permute-start(f16[256,128]{1,0:T(8,128)(2,1)S(1)} %get-tuple-element.51), channel_id=1, source_target_pairs={{0,1},{1,0},{2,3},{3,2},{4,5},{5,4},{6,7},{7,6},{8,9},{9,8},{10,11... | collective-permute-start | bytes 196616 | tf_op jit(solution)/shard_map/ppermute | solution.py:152
  68.4 2.4 %collective-permute-start.19 = (f16[256,128]{1,0:T(8,128)(2,1)S(1)}, f16[256,128]{1,0:T(8,128)(2,1)S(1)}, u32[]{:S(2)}, u32[]{:S(2)}) collective-permute-start(f16[256,128]{1,0:T(8,128)(2,1)S(1)} %get-tuple-element.48), channel_id=1, source_target_pairs={{0,1},{1,0},{2,3},{3,2},{4,5},{5,4},{6,7},{7,6},{8,9},{9,8},{10,11... | collective-permute-start | bytes 196616 | tf_op jit(solution)/shard_map/ppermute | solution.py:152
  74.0 2.6 %collective-permute-done.18 = f16[256,128]{1,0:T(8,128)(2,1)S(1)} collective-permute-done((f16[256,128]{1,0:T(8,128)(2,1)S(1)}, f16[256,128]{1,0:T(8,128)(2,1)S(1)}, u32[]{:S(2)}, u32[]{:S(2)}) %collective-permute-start.18) | collective-permute-done | bytes 65568 | tf_op jit(solution)/shard_map/ppermute | solution.py:152
  77.3 2.9 %shard_map.130 = f32[32,128]{1,0:T(8,128)} custom-call(f32[256,128]{1,0:T(8,128)} %fusion.13.left, f32[256,128]{1,0:T(8,128)} %fusion.10.right, f32[128,512]{1,0:T(8,128)} %bitcast.63, f32[128,512]{1,0:T(8,128)} %bitcast.65, f32[128,512]{1,0:T(8,128)} %bitcast.67, f32[128,512]{1,0:T(8,128)} %base.3, f32[32,128]{1,0:T(8,128)} %constant.4.clone.rows, ...), custom_call_target="tpu_custom_call" | custom-call | tf_op jit(solution)/shard_map/pallas_call | solution.py:192
  80.2 4.4 %collective-permute-start.20 = (f32[32,128]{1,0:T(8,128)}, f32[32,128]{1,0:T(8,128)S(1)}, u32[]{:S(2)}, u32[]{:S(2)}) collective-permute-start(f32[32,128]{1,0:T(8,128)} %shard_map.130), channel_id=1, source_target_pairs={{0,64},{64,0},{128,192},{192,128},{1,65},{65,1},{129,193},{193,129... | collective-permute-start | bytes 49160 | tf_op jit(solution)/shard_map/ppermute | solution.py:201
  86.4 4.5 %collective-permute-start.21 = (f32[32,128]{1,0:T(8,128)S(1)}, f32[32,128]{1,0:T(8,128)S(1)}, u32[]{:S(2)}, u32[]{:S(2)}) collective-permute-start(f32[32,128]{1,0:T(8,128)S(1)} %add.99.here), channel_id=1, source_target_pairs={{0,128},{64,192},{128,0},{192,64},{1,129},{65,193},{129,1},{193,65... | collective-permute-start | bytes 49160 | tf_op jit(solution)/shard_map/ppermute | solution.py:201
  90.9 2.1 %shard_map.132 = (f32[128,512]{1,0:T(8,128)}, f32[128,512]{1,0:T(8,128)}) custom-call(f32[256,128]{1,0:T(8,128)} %fusion.13.left, f32[256,128]{1,0:T(8,128)} %fusion.10.right, f32[128,512]{1,0:T(8,128)} %bitcast.64, f32[128,512]{1,0:T(8,128)} %bitcast.66), custom_call_target="tpu_custom_call" | custom-call | tf_op jit(solution)/shard_map/pallas_call | solution.py:192
  93.6 2.6 %shard_map.131 = (f32[128,512]{1,0:T(8,128)}, f32[128,512]{1,0:T(8,128)}, f32[32,128]{1,0:T(8,128)}) custom-call(f32[32,128]{1,0:T(8,128)} %copy-done.1, f32[32,128]{1,0:T(8,128)} %copy-done.2, f32[128,512]{1,0:T(8,128)} %base.3, f32[128,512]{1,0:T(8,128)} %moment.1, f32[32,128]{1,0:T(8,128)} %constant.4.clone.rows, f32[128,512]{1,0:T(8,128)} %constant.5.clone.cols), custom_call_target="tpu_custom_call" | custom-call | tf_op jit(solution)/shard_map/pallas_call | solution.py:192
  (50 shorter events, 16.9 us)
Async XLA Ops:
  0.6 1.0 %copy-start = (bf16[512,512]{1,0:T(8,128)(2,1)S(1)}, bf16[512,512]{1,0:T(8,128)(2,1)}, u32[]{:S(2)}) copy-start(bf16[512,512]{1,0:T(8,128)(2,1)} %g_ref.3) | copy-start | bytes 1572868
  7.1 24.0 %collective-permute-start.1 = (f16[4,4,256,128]{3,2,1,0:T(8,128)(2,1)S(1)}, f16[4,4,256,128]{3,2,1,0:T(8,128)(2,1)S(1)}, u32[]{:S(2)}, u32[]{:S(2)}) collective-permute-start(f16[4,4,256,128]{3,2,1,0:T(8,128)(2,1)S(1)} %convert_element_type.146), channel_id=1, source_target_pairs={{0,4},{1,5},{2,6},{3,7},{4,8},{5,9},{6,10},{7,11},{8,12},{9,13},{1... | collective-permute-start | bytes 3145736 | tf_op jit(solution)/shard_map/ppermute | solution.py:35
  9.4 23.5 %collective-permute-start = (f16[4,4,256,128]{3,2,1,0:T(8,128)(2,1)S(1)}, f16[4,4,256,128]{3,2,1,0:T(8,128)(2,1)S(1)}, u32[]{:S(2)}, u32[]{:S(2)}) collective-permute-start(f16[4,4,256,128]{3,2,1,0:T(8,128)(2,1)S(1)} %convert_element_type.144), channel_id=1, source_target_pairs={{0,12},{1,13},{2,14},{3,15},{4,0},{5,1},{6,2},{7,3},{8,4},{9,5},{1... | collective-permute-start | bytes 3145736 | tf_op jit(solution)/shard_map/ppermute | solution.py:35
  11.0 25.0 %collective-permute-start.11 = (f16[4,4,256,128]{3,2,1,0:T(8,128)(2,1)S(1)}, f16[4,4,256,128]{3,2,1,0:T(8,128)(2,1)S(1)}, u32[]{:S(2)}, u32[]{:S(2)}) collective-permute-start(f16[4,4,256,128]{3,2,1,0:T(8,128)(2,1)S(1)} %convert_element_type.168), channel_id=1, source_target_pairs={{0,16},{1,17},{2,18},{3,19},{4,20},{5,21},{6,22},{7,23},{8,24},{9,... | collective-permute-start | bytes 3145736 | tf_op jit(solution)/shard_map/ppermute | solution.py:35
  12.8 23.2 %collective-permute-start.10 = (f16[4,4,256,128]{3,2,1,0:T(8,128)(2,1)S(1)}, f16[4,4,256,128]{3,2,1,0:T(8,128)(2,1)S(1)}, u32[]{:S(2)}, u32[]{:S(2)}) collective-permute-start(f16[4,4,256,128]{3,2,1,0:T(8,128)(2,1)S(1)} %convert_element_type.166), channel_id=1, source_target_pairs={{0,48},{1,49},{2,50},{3,51},{4,52},{5,53},{6,54},{7,55},{8,56},{9,... | collective-permute-start | bytes 3145736 | tf_op jit(solution)/shard_map/ppermute | solution.py:35
  33.2 12.6 %collective-permute-start.2 = (f16[2,4,256,128]{3,2,1,0:T(8,128)(2,1)S(1)}, f16[2,4,256,128]{3,2,1,0:T(8,128)(2,1)S(1)}, u32[]{:S(2)}, u32[]{:S(2)}) collective-permute-start(f16[2,4,256,128]{3,2,1,0:T(8,128)(2,1)S(1)} %get-tuple-element.41), channel_id=1, source_target_pairs={{0,4},{1,5},{2,6},{3,7},{4,8},{5,9},{6,10},{7,11},{8,12},{9,13},{1... | collective-permute-start | bytes 1572872 | tf_op jit(solution)/shard_map/ppermute | solution.py:35
  34.8 11.3 %collective-permute-start.3 = (f16[2,4,256,128]{3,2,1,0:T(8,128)(2,1)S(1)}, f16[2,4,256,128]{3,2,1,0:T(8,128)(2,1)S(1)}, u32[]{:S(2)}, u32[]{:S(2)}) collective-permute-start(f16[2,4,256,128]{3,2,1,0:T(8,128)(2,1)S(1)} %get-tuple-element.42), channel_id=1, source_target_pairs={{0,12},{1,13},{2,14},{3,15},{4,0},{5,1},{6,2},{7,3},{8,4},{9,5},{1... | collective-permute-start | bytes 1572872 | tf_op jit(solution)/shard_map/ppermute | solution.py:35
  36.3 16.0 %collective-permute-start.12 = (f16[2,4,256,128]{3,2,1,0:T(8,128)(2,1)S(1)}, f16[2,4,256,128]{3,2,1,0:T(8,128)(2,1)S(1)}, u32[]{:S(2)}, u32[]{:S(2)}) collective-permute-start(f16[2,4,256,128]{3,2,1,0:T(8,128)(2,1)S(1)} %get-tuple-element.37), channel_id=1, source_target_pairs={{0,16},{1,17},{2,18},{3,19},{4,20},{5,21},{6,22},{7,23},{8,24},{9,... | collective-permute-start | bytes 1572872 | tf_op jit(solution)/shard_map/ppermute | solution.py:35
  38.1 14.2 %collective-permute-start.13 = (f16[2,4,256,128]{3,2,1,0:T(8,128)(2,1)S(1)}, f16[2,4,256,128]{3,2,1,0:T(8,128)(2,1)S(1)}, u32[]{:S(2)}, u32[]{:S(2)}) collective-permute-start(f16[2,4,256,128]{3,2,1,0:T(8,128)(2,1)S(1)} %get-tuple-element.38), channel_id=1, source_target_pairs={{0,48},{1,49},{2,50},{3,51},{4,52},{5,53},{6,54},{7,55},{8,56},{9,... | collective-permute-start | bytes 1572872 | tf_op jit(solution)/shard_map/ppermute | solution.py:35
  46.5 10.2 %collective-permute-start.5 = (f16[4,256,128]{2,1,0:T(8,128)(2,1)S(1)}, f16[4,256,128]{2,1,0:T(8,128)(2,1)S(1)}, u32[]{:S(2)}, u32[]{:S(2)}) collective-permute-start(f16[4,256,128]{2,1,0:T(8,128)(2,1)S(1)} %fusion.6), channel_id=1, source_target_pairs={{0,16},{1,17},{2,18},{3,19},{4,20},{5,21},{6,22},{7,23},{8,24},{9,... | collective-permute-start | bytes 786440 | tf_op jit(solution)/shard_map/ppermute | solution.py:35
  48.5 13.5 %collective-permute-start.4 = (f16[4,256,128]{2,1,0:T(8,128)(2,1)S(1)}, f16[4,256,128]{2,1,0:T(8,128)(2,1)S(1)}, u32[]{:S(2)}, u32[]{:S(2)}) collective-permute-start(f16[4,256,128]{2,1,0:T(8,128)(2,1)S(1)} %get-tuple-element.45), channel_id=1, source_target_pairs={{0,32},{1,33},{2,34},{3,35},{4,36},{5,37},{6,38},{7,39},{8,40},{9,... | collective-permute-start | bytes 786440 | tf_op jit(solution)/shard_map/ppermute | solution.py:35
  51.2 10.8 %collective-permute-start.6 = (f16[4,256,128]{2,1,0:T(8,128)(2,1)S(1)}, f16[4,256,128]{2,1,0:T(8,128)(2,1)S(1)}, u32[]{:S(2)}, u32[]{:S(2)}) collective-permute-start(f16[4,256,128]{2,1,0:T(8,128)(2,1)S(1)} %get-tuple-element.46), channel_id=1, source_target_pairs={{0,48},{1,49},{2,50},{3,51},{4,52},{5,53},{6,54},{7,55},{8,56},{9,... | collective-permute-start | bytes 786440 | tf_op jit(solution)/shard_map/ppermute | solution.py:35
  52.8 14.1 %collective-permute-start.15 = (f16[4,256,128]{2,1,0:T(8,128)(2,1)S(1)}, f16[4,256,128]{2,1,0:T(8,128)(2,1)S(1)}, u32[]{:S(2)}, u32[]{:S(2)}) collective-permute-start(f16[4,256,128]{2,1,0:T(8,128)(2,1)S(1)} %fusion.7), channel_id=1, source_target_pairs={{0,4},{1,5},{2,6},{3,7},{4,8},{5,9},{6,10},{7,11},{8,12},{9,13},{1... | collective-permute-start | bytes 786440 | tf_op jit(solution)/shard_map/ppermute | solution.py:35
  53.5 13.4 %collective-permute-start.14 = (f16[4,256,128]{2,1,0:T(8,128)(2,1)S(1)}, f16[4,256,128]{2,1,0:T(8,128)(2,1)S(1)}, u32[]{:S(2)}, u32[]{:S(2)}) collective-permute-start(f16[4,256,128]{2,1,0:T(8,128)(2,1)S(1)} %get-tuple-element.43), channel_id=1, source_target_pairs={{0,8},{1,9},{2,10},{3,11},{4,12},{5,13},{6,14},{7,15},{8,0},{9,1},... | collective-permute-start | bytes 786440 | tf_op jit(solution)/shard_map/ppermute | solution.py:35
  56.8 10.2 %collective-permute-start.16 = (f16[4,256,128]{2,1,0:T(8,128)(2,1)S(1)}, f16[4,256,128]{2,1,0:T(8,128)(2,1)S(1)}, u32[]{:S(2)}, u32[]{:S(2)}) collective-permute-start(f16[4,256,128]{2,1,0:T(8,128)(2,1)S(1)} %get-tuple-element.44), channel_id=1, source_target_pairs={{0,12},{1,13},{2,14},{3,15},{4,0},{5,1},{6,2},{7,3},{8,4},{9,5},{1... | collective-permute-start | bytes 786440 | tf_op jit(solution)/shard_map/ppermute | solution.py:35
  62.2 8.6 %collective-permute-start.7 = (f16[256,128]{1,0:T(8,128)(2,1)S(1)}, f16[256,128]{1,0:T(8,128)(2,1)S(1)}, u32[]{:S(2)}, u32[]{:S(2)}) collective-permute-start(f16[256,128]{1,0:T(8,128)(2,1)S(1)} %get-tuple-element.50), channel_id=1, source_target_pairs={{0,2},{1,3},{2,0},{3,1},{4,6},{5,7},{6,4},{7,5},{8,10},{9,11},{10,... | collective-permute-start | bytes 196616 | tf_op jit(solution)/shard_map/ppermute | solution.py:152
  65.3 5.9 %collective-permute-start.9 = (f16[256,128]{1,0:T(8,128)(2,1)S(1)}, f16[256,128]{1,0:T(8,128)(2,1)S(1)}, u32[]{:S(2)}, u32[]{:S(2)}) collective-permute-start(f16[256,128]{1,0:T(8,128)(2,1)S(1)} %get-tuple-element.51), channel_id=1, source_target_pairs={{0,1},{1,0},{2,3},{3,2},{4,5},{5,4},{6,7},{7,6},{8,9},{9,8},{10,11... | collective-permute-start | bytes 196616 | tf_op jit(solution)/shard_map/ppermute | solution.py:152
  66.9 5.6 %collective-permute-start.8 = (f16[256,128]{1,0:T(8,128)(2,1)S(1)}, f16[256,128]{1,0:T(8,128)(2,1)S(1)}, u32[]{:S(2)}, u32[]{:S(2)}) collective-permute-start(f16[256,128]{1,0:T(8,128)(2,1)S(1)} %get-tuple-element.52), channel_id=1, source_target_pairs={{0,3},{1,2},{2,1},{3,0},{4,7},{5,6},{6,5},{7,4},{8,11},{9,10},{10,... | collective-permute-start | bytes 196616 | tf_op jit(solution)/shard_map/ppermute | solution.py:152
  67.1 6.1 %collective-permute-start.17 = (f16[256,128]{1,0:T(8,128)(2,1)S(1)}, f16[256,128]{1,0:T(8,128)(2,1)S(1)}, u32[]{:S(2)}, u32[]{:S(2)}) collective-permute-start(f16[256,128]{1,0:T(8,128)(2,1)S(1)} %get-tuple-element.47), channel_id=1, source_target_pairs={{0,2},{1,3},{2,0},{3,1},{4,6},{5,7},{6,4},{7,5},{8,10},{9,11},{10,... | collective-permute-start | bytes 196616 | tf_op jit(solution)/shard_map/ppermute | solution.py:152
  68.4 5.7 %collective-permute-start.19 = (f16[256,128]{1,0:T(8,128)(2,1)S(1)}, f16[256,128]{1,0:T(8,128)(2,1)S(1)}, u32[]{:S(2)}, u32[]{:S(2)}) collective-permute-start(f16[256,128]{1,0:T(8,128)(2,1)S(1)} %get-tuple-element.48), channel_id=1, source_target_pairs={{0,1},{1,0},{2,3},{3,2},{4,5},{5,4},{6,7},{7,6},{8,9},{9,8},{10,11... | collective-permute-start | bytes 196616 | tf_op jit(solution)/shard_map/ppermute | solution.py:152
  70.8 5.8 %collective-permute-start.18 = (f16[256,128]{1,0:T(8,128)(2,1)S(1)}, f16[256,128]{1,0:T(8,128)(2,1)S(1)}, u32[]{:S(2)}, u32[]{:S(2)}) collective-permute-start(f16[256,128]{1,0:T(8,128)(2,1)S(1)} %get-tuple-element.49), channel_id=1, source_target_pairs={{0,3},{1,2},{2,1},{3,0},{4,7},{5,6},{6,5},{7,4},{8,11},{9,10},{10,... | collective-permute-start | bytes 196616 | tf_op jit(solution)/shard_map/ppermute | solution.py:152
  80.2 5.5 %collective-permute-start.20 = (f32[32,128]{1,0:T(8,128)}, f32[32,128]{1,0:T(8,128)S(1)}, u32[]{:S(2)}, u32[]{:S(2)}) collective-permute-start(f32[32,128]{1,0:T(8,128)} %shard_map.130), channel_id=1, source_target_pairs={{0,64},{64,0},{128,192},{192,128},{1,65},{65,1},{129,193},{193,129... | collective-permute-start | bytes 49160 | tf_op jit(solution)/shard_map/ppermute | solution.py:201
  86.4 6.6 %copy-start.1 = (f32[32,128]{1,0:T(8,128)}, f32[32,128]{1,0:T(8,128)S(1)}, u32[]{:S(2)}) copy-start(f32[32,128]{1,0:T(8,128)S(1)} %add.99.here) | copy-start | bytes 49156
  86.4 6.6 %collective-permute-start.21 = (f32[32,128]{1,0:T(8,128)S(1)}, f32[32,128]{1,0:T(8,128)S(1)}, u32[]{:S(2)}, u32[]{:S(2)}) collective-permute-start(f32[32,128]{1,0:T(8,128)S(1)} %add.99.here), channel_id=1, source_target_pairs={{0,128},{64,192},{128,0},{192,64},{1,129},{65,193},{129,1},{193,65... | collective-permute-start | bytes 49160 | tf_op jit(solution)/shard_map/ppermute | solution.py:201
  (1 other events, 0.6 us)

commit v4 on v3

--- a/solution.py
+++ b/solution.py
@@ -194,6 +194,7 @@
         in_specs=[pl.BlockSpec(memory_space=pltpu.VMEM)] * len(args),
         out_specs=[pl.BlockSpec(memory_space=pltpu.VMEM)] * len(shapes),
         out_shape=[jax.ShapeDtypeStruct(shape, jnp.float32) for shape in shapes],
+        compiler_params=pltpu.CompilerParams(vmem_limit_bytes=8 << 20),
     )(*args)
 
 

time: 96.5 us -> 91.1 us (0.944)
  Pallas kernels: 18.6 us -> 14.3 us
  other arithmetic: 4.77 us -> 2.74 us
  waiting for transfers between devices: 29.6 us -> 31.2 us
    pallas_call x3, Pallas kernels: 7.6 us -> 3.27 us  [on_chip(): pl.pallas_call(kernel, in_specs=[pl.BlockSpec(memory_space=pltpu.VMEM)] *...]
    add x2, other arithmetic: 1.37 us -> 0.06 us  [scattered_grad(): part = part + wide(lax.ppermute(narrow(total[flip]), 'fsdp', pairs))]
  transfers between devices with their start and end apart: 22 -> 22, of which waited for: 9 -> 11; matrix products, arithmetic and copies ran while one was open for 4% -> 3% of each run, Pallas kernels for 8% -> 7%
where the time goes in v4:
time: 91.1 us; the launch traced here: 90.9 us
  starting transfers between devices  40.5 us (44%)
  waiting for transfers between devices  31.2 us (34%)
  Pallas kernels  14.3 us (16%)
  other arithmetic  2.74 us (3%)
  local copies, waits for them, and re-layouts  1.38 us (2%)
    ppermute x14, waiting for transfers between devices, shift(): return lax.ppermute(value, 'fsdp', pairs)  23.9 us
    ppermute x14, starting transfers between devices, shift(): return lax.ppermute(value, 'fsdp', pairs)  22.8 us
    pallas_call x2, Pallas kernels, products(): pl.pallas_call(functools.partial(product_kernel, roles, unroll), in_specs...  11 us
    ppermute x2, starting transfers between devices, flipped_island(): return lax.ppermute(value, 'island', [(k, k ^ flip) for k in range(4)])  8.97 us
    ppermute x6, starting transfers between devices, scattered_grad(): part = part + wide(lax.ppermute(narrow(total[flip]), 'fsdp', pairs))  8.73 us
    ppermute x6, waiting for transfers between devices, scattered_grad(): part = part + wide(lax.ppermute(narrow(total[flip]), 'fsdp', pairs))  5.37 us
    pallas_call x3, Pallas kernels, on_chip(): pl.pallas_call(kernel, in_specs=[pl.BlockSpec(memory_space=pltpu.VMEM)] *...  3.27 us
    ppermute x2, waiting for transfers between devices, flipped_island(): return lax.ppermute(value, 'island', [(k, k ^ flip) for k in range(4)])  1.92 us
  transfers between devices with their start and end apart: 22, of which 11 were waited for; matrix products, arithmetic and copies ran while one was open for 3% of the time, Pallas kernels for 7%

profile of v4, /device:TPU:1, one launch (start us, length us, event | category | flops | bytes accessed | tf_op | source)
XLA Modules:
  0.0 90.9 jit_solution(18096709197580530711)
XLA Ops:
  1.7 5.2 %shard_map.129 = (f32[4,4,256,128]{3,2,1,0:T(8,128)S(1)}, f32[4,4,256,128]{3,2,1,0:T(8,128)S(1)}, f32[4,4,256,128]{3,2,1,0:T(8,128)S(1)}, f32[4,4,256,128]{3,2,1,0:T(8,128)S(1)}) custom-call(bf16[512,8192]{1,0:T(8,128)(2,1)} %a_ref.3, bf16[512,512]{1,0:T(8,128)(2,1)S(1)} %copy-done), custom_call_target="tpu_custom_call" | custom-call | flops 2147483648 | bytes 8388608 | tf_op jit(solution)/shard_map/pallas_call | solution.py:108
  7.1 2.1 %collective-permute-start.1 = (f16[4,4,256,128]{3,2,1,0:T(8,128)(2,1)S(1)}, f16[4,4,256,128]{3,2,1,0:T(8,128)(2,1)S(1)}, u32[]{:S(2)}, u32[]{:S(2)}) collective-permute-start(f16[4,4,256,128]{3,2,1,0:T(8,128)(2,1)S(1)} %convert_element_type.146), channel_id=1, source_target_pairs={{0,4},{1,5},{2,6},{3,7},{4,8},{5,9},{6,10},{7,11},{8,12},{9,13},{1... | collective-permute-start | bytes 3145736 | tf_op jit(solution)/shard_map/ppermute | solution.py:35
  9.4 1.4 %collective-permute-start = (f16[4,4,256,128]{3,2,1,0:T(8,128)(2,1)S(1)}, f16[4,4,256,128]{3,2,1,0:T(8,128)(2,1)S(1)}, u32[]{:S(2)}, u32[]{:S(2)}) collective-permute-start(f16[4,4,256,128]{3,2,1,0:T(8,128)(2,1)S(1)} %convert_element_type.144), channel_id=1, source_target_pairs={{0,12},{1,13},{2,14},{3,15},{4,0},{5,1},{6,2},{7,3},{8,4},{9,5},{1... | collective-permute-start | bytes 3145736 | tf_op jit(solution)/shard_map/ppermute | solution.py:35
  11.0 1.6 %collective-permute-start.11 = (f16[4,4,256,128]{3,2,1,0:T(8,128)(2,1)S(1)}, f16[4,4,256,128]{3,2,1,0:T(8,128)(2,1)S(1)}, u32[]{:S(2)}, u32[]{:S(2)}) collective-permute-start(f16[4,4,256,128]{3,2,1,0:T(8,128)(2,1)S(1)} %convert_element_type.168), channel_id=1, source_target_pairs={{0,16},{1,17},{2,18},{3,19},{4,20},{5,21},{6,22},{7,23},{8,24},{9,... | collective-permute-start | bytes 3145736 | tf_op jit(solution)/shard_map/ppermute | solution.py:35
  12.8 1.5 %collective-permute-start.10 = (f16[4,4,256,128]{3,2,1,0:T(8,128)(2,1)S(1)}, f16[4,4,256,128]{3,2,1,0:T(8,128)(2,1)S(1)}, u32[]{:S(2)}, u32[]{:S(2)}) collective-permute-start(f16[4,4,256,128]{3,2,1,0:T(8,128)(2,1)S(1)} %convert_element_type.166), channel_id=1, source_target_pairs={{0,48},{1,49},{2,50},{3,51},{4,52},{5,53},{6,54},{7,55},{8,56},{9,... | collective-permute-start | bytes 3145736 | tf_op jit(solution)/shard_map/ppermute | solution.py:35
  14.3 5.8 %shard_map.128 = (f32[4,4,256,128]{3,2,1,0:T(8,128)S(1)}, f32[4,4,256,128]{3,2,1,0:T(8,128)S(1)}, f32[4,4,256,128]{3,2,1,0:T(8,128)S(1)}, f32[4,4,256,128]{3,2,1,0:T(8,128)S(1)}) custom-call(bf16[512,8192]{1,0:T(8,128)(2,1)} %a_ref.3, bf16[512,512]{1,0:T(8,128)(2,1)S(1)} %copy-done), custom_call_target="tpu_custom_call" | custom-call | flops 2147483648 | bytes 8388608 | tf_op jit(solution)/shard_map/pallas_call | solution.py:108
  20.1 10.9 %collective-permute-done.1 = f16[4,4,256,128]{3,2,1,0:T(8,128)(2,1)S(1)} collective-permute-done((f16[4,4,256,128]{3,2,1,0:T(8,128)(2,1)S(1)}, f16[4,4,256,128]{3,2,1,0:T(8,128)(2,1)S(1)}, u32[]{:S(2)}, u32[]{:S(2)}) %collective-permute-start.1) | collective-permute-done | bytes 1048608 | tf_op jit(solution)/shard_map/ppermute | solution.py:35
  31.0 1.9 %collective-permute-done = f16[4,4,256,128]{3,2,1,0:T(8,128)(2,1)S(1)} collective-permute-done((f16[4,4,256,128]{3,2,1,0:T(8,128)(2,1)S(1)}, f16[4,4,256,128]{3,2,1,0:T(8,128)(2,1)S(1)}, u32[]{:S(2)}, u32[]{:S(2)}) %collective-permute-start) | collective-permute-done | bytes 1048608 | tf_op jit(solution)/shard_map/ppermute | solution.py:35
  33.2 1.6 %collective-permute-start.2 = (f16[2,4,256,128]{3,2,1,0:T(8,128)(2,1)S(1)}, f16[2,4,256,128]{3,2,1,0:T(8,128)(2,1)S(1)}, u32[]{:S(2)}, u32[]{:S(2)}) collective-permute-start(f16[2,4,256,128]{3,2,1,0:T(8,128)(2,1)S(1)} %get-tuple-element.41), channel_id=1, source_target_pairs={{0,4},{1,5},{2,6},{3,7},{4,8},{5,9},{6,10},{7,11},{8,12},{9,13},{1... | collective-permute-start | bytes 1572872 | tf_op jit(solution)/shard_map/ppermute | solution.py:35
  36.3 1.7 %collective-permute-start.12 = (f16[2,4,256,128]{3,2,1,0:T(8,128)(2,1)S(1)}, f16[2,4,256,128]{3,2,1,0:T(8,128)(2,1)S(1)}, u32[]{:S(2)}, u32[]{:S(2)}) collective-permute-start(f16[2,4,256,128]{3,2,1,0:T(8,128)(2,1)S(1)} %get-tuple-element.37), channel_id=1, source_target_pairs={{0,16},{1,17},{2,18},{3,19},{4,20},{5,21},{6,22},{7,23},{8,24},{9,... | collective-permute-start | bytes 1572872 | tf_op jit(solution)/shard_map/ppermute | solution.py:35
  38.1 1.5 %collective-permute-start.13 = (f16[2,4,256,128]{3,2,1,0:T(8,128)(2,1)S(1)}, f16[2,4,256,128]{3,2,1,0:T(8,128)(2,1)S(1)}, u32[]{:S(2)}, u32[]{:S(2)}) collective-permute-start(f16[2,4,256,128]{3,2,1,0:T(8,128)(2,1)S(1)} %get-tuple-element.38), channel_id=1, source_target_pairs={{0,48},{1,49},{2,50},{3,51},{4,52},{5,53},{6,54},{7,55},{8,56},{9,... | collective-permute-start | bytes 1572872 | tf_op jit(solution)/shard_map/ppermute | solution.py:35
  39.6 6.2 %collective-permute-done.2 = f16[2,4,256,128]{3,2,1,0:T(8,128)(2,1)S(1)} collective-permute-done((f16[2,4,256,128]{3,2,1,0:T(8,128)(2,1)S(1)}, f16[2,4,256,128]{3,2,1,0:T(8,128)(2,1)S(1)}, u32[]{:S(2)}, u32[]{:S(2)}) %collective-permute-start.2) | collective-permute-done | bytes 524320 | tf_op jit(solution)/shard_map/ppermute | solution.py:35
  46.5 1.9 %collective-permute-start.5 = (f16[4,256,128]{2,1,0:T(8,128)(2,1)S(1)}, f16[4,256,128]{2,1,0:T(8,128)(2,1)S(1)}, u32[]{:S(2)}, u32[]{:S(2)}) collective-permute-start(f16[4,256,128]{2,1,0:T(8,128)(2,1)S(1)} %fusion.6), channel_id=1, source_target_pairs={{0,16},{1,17},{2,18},{3,19},{4,20},{5,21},{6,22},{7,23},{8,24},{9,... | collective-permute-start | bytes 786440 | tf_op jit(solution)/shard_map/ppermute | solution.py:35
  48.5 2.7 %collective-permute-start.4 = (f16[4,256,128]{2,1,0:T(8,128)(2,1)S(1)}, f16[4,256,128]{2,1,0:T(8,128)(2,1)S(1)}, u32[]{:S(2)}, u32[]{:S(2)}) collective-permute-start(f16[4,256,128]{2,1,0:T(8,128)(2,1)S(1)} %get-tuple-element.45), channel_id=1, source_target_pairs={{0,32},{1,33},{2,34},{3,35},{4,36},{5,37},{6,38},{7,39},{8,40},{9,... | collective-permute-start | bytes 786440 | tf_op jit(solution)/shard_map/ppermute | solution.py:35
  53.5 3.2 %collective-permute-start.14 = (f16[4,256,128]{2,1,0:T(8,128)(2,1)S(1)}, f16[4,256,128]{2,1,0:T(8,128)(2,1)S(1)}, u32[]{:S(2)}, u32[]{:S(2)}) collective-permute-start(f16[4,256,128]{2,1,0:T(8,128)(2,1)S(1)} %get-tuple-element.43), channel_id=1, source_target_pairs={{0,8},{1,9},{2,10},{3,11},{4,12},{5,13},{6,14},{7,15},{8,0},{9,1},... | collective-permute-start | bytes 786440 | tf_op jit(solution)/shard_map/ppermute | solution.py:35
  57.4 4.6 %collective-permute-done.4 = f16[4,256,128]{2,1,0:T(8,128)(2,1)S(1)} collective-permute-done((f16[4,256,128]{2,1,0:T(8,128)(2,1)S(1)}, f16[4,256,128]{2,1,0:T(8,128)(2,1)S(1)}, u32[]{:S(2)}, u32[]{:S(2)}) %collective-permute-start.4) | collective-permute-done | bytes 262176 | tf_op jit(solution)/shard_map/ppermute | solution.py:35
  62.3 3.1 %collective-permute-start.7 = (f16[256,128]{1,0:T(8,128)(2,1)S(1)}, f16[256,128]{1,0:T(8,128)(2,1)S(1)}, u32[]{:S(2)}, u32[]{:S(2)}) collective-permute-start(f16[256,128]{1,0:T(8,128)(2,1)S(1)} %get-tuple-element.50), channel_id=1, source_target_pairs={{0,2},{1,3},{2,0},{3,1},{4,6},{5,7},{6,4},{7,5},{8,10},{9,11},{10,... | collective-permute-start | bytes 196616 | tf_op jit(solution)/shard_map/ppermute | solution.py:152
  65.3 1.6 %collective-permute-start.9 = (f16[256,128]{1,0:T(8,128)(2,1)S(1)}, f16[256,128]{1,0:T(8,128)(2,1)S(1)}, u32[]{:S(2)}, u32[]{:S(2)}) collective-permute-start(f16[256,128]{1,0:T(8,128)(2,1)S(1)} %get-tuple-element.51), channel_id=1, source_target_pairs={{0,1},{1,0},{2,3},{3,2},{4,5},{5,4},{6,7},{7,6},{8,9},{9,8},{10,11... | collective-permute-start | bytes 196616 | tf_op jit(solution)/shard_map/ppermute | solution.py:152
  68.5 2.4 %collective-permute-start.19 = (f16[256,128]{1,0:T(8,128)(2,1)S(1)}, f16[256,128]{1,0:T(8,128)(2,1)S(1)}, u32[]{:S(2)}, u32[]{:S(2)}) collective-permute-start(f16[256,128]{1,0:T(8,128)(2,1)S(1)} %get-tuple-element.48), channel_id=1, source_target_pairs={{0,1},{1,0},{2,3},{3,2},{4,5},{5,4},{6,7},{7,6},{8,9},{9,8},{10,11... | collective-permute-start | bytes 196616 | tf_op jit(solution)/shard_map/ppermute | solution.py:152
  71.3 1.3 %collective-permute-done.8 = f16[256,128]{1,0:T(8,128)(2,1)S(1)} collective-permute-done((f16[256,128]{1,0:T(8,128)(2,1)S(1)}, f16[256,128]{1,0:T(8,128)(2,1)S(1)}, u32[]{:S(2)}, u32[]{:S(2)}) %collective-permute-start.8) | collective-permute-done | bytes 65568 | tf_op jit(solution)/shard_map/ppermute | solution.py:152
  74.1 2.5 %collective-permute-done.18 = f16[256,128]{1,0:T(8,128)(2,1)S(1)} collective-permute-done((f16[256,128]{1,0:T(8,128)(2,1)S(1)}, f16[256,128]{1,0:T(8,128)(2,1)S(1)}, u32[]{:S(2)}, u32[]{:S(2)}) %collective-permute-start.18) | collective-permute-done | bytes 65568 | tf_op jit(solution)/shard_map/ppermute | solution.py:152
  77.6 4.5 %collective-permute-start.20 = (f32[32,128]{1,0:T(8,128)S(1)}, f32[32,128]{1,0:T(8,128)S(1)}, u32[]{:S(2)}, u32[]{:S(2)}) collective-permute-start(f32[32,128]{1,0:T(8,128)S(1)} %shard_map.130), channel_id=1, source_target_pairs={{0,64},{64,0},{128,192},{192,128},{1,65},{65,1},{129,193},{193,129... | collective-permute-start | bytes 49160 | tf_op jit(solution)/shard_map/ppermute | solution.py:202
  83.0 4.5 %collective-permute-start.21 = (f32[32,128]{1,0:T(8,128)S(1)}, f32[32,128]{1,0:T(8,128)S(1)}, u32[]{:S(2)}, u32[]{:S(2)}) collective-permute-start(f32[32,128]{1,0:T(8,128)S(1)} %add.99.here), channel_id=1, source_target_pairs={{0,128},{64,192},{128,0},{192,64},{1,129},{65,193},{129,1},{193,65... | collective-permute-start | bytes 49160 | tf_op jit(solution)/shard_map/ppermute | solution.py:202
  89.5 1.5 %shard_map.131 = (f32[128,512]{1,0:T(8,128)}, f32[128,512]{1,0:T(8,128)}, f32[32,128]{1,0:T(8,128)}) custom-call(f32[32,128]{1,0:T(8,128)S(1)} %add.99.here, f32[32,128]{1,0:T(8,128)S(1)} %collective-permute-done.21.there, f32[128,512]{1,0:T(8,128)S(1)} %copy-done.3, f32[128,512]{1,0:T(8,128)S(1)} %copy-done.6, f32[32,128]{1,0:T(8,128)S(1)} %copy-done.7, ...), custom_call_target="tpu_custom_call" | custom-call | tf_op jit(solution)/shard_map/pallas_call | solution.py:192
  (60 shorter events, 15.0 us)
Async XLA Ops:
  7.1 24.0 %collective-permute-start.1 = (f16[4,4,256,128]{3,2,1,0:T(8,128)(2,1)S(1)}, f16[4,4,256,128]{3,2,1,0:T(8,128)(2,1)S(1)}, u32[]{:S(2)}, u32[]{:S(2)}) collective-permute-start(f16[4,4,256,128]{3,2,1,0:T(8,128)(2,1)S(1)} %convert_element_type.146), channel_id=1, source_target_pairs={{0,4},{1,5},{2,6},{3,7},{4,8},{5,9},{6,10},{7,11},{8,12},{9,13},{1... | collective-permute-start | bytes 3145736 | tf_op jit(solution)/shard_map/ppermute | solution.py:35
  9.4 23.5 %collective-permute-start = (f16[4,4,256,128]{3,2,1,0:T(8,128)(2,1)S(1)}, f16[4,4,256,128]{3,2,1,0:T(8,128)(2,1)S(1)}, u32[]{:S(2)}, u32[]{:S(2)}) collective-permute-start(f16[4,4,256,128]{3,2,1,0:T(8,128)(2,1)S(1)} %convert_element_type.144), channel_id=1, source_target_pairs={{0,12},{1,13},{2,14},{3,15},{4,0},{5,1},{6,2},{7,3},{8,4},{9,5},{1... | collective-permute-start | bytes 3145736 | tf_op jit(solution)/shard_map/ppermute | solution.py:35
  11.0 25.0 %collective-permute-start.11 = (f16[4,4,256,128]{3,2,1,0:T(8,128)(2,1)S(1)}, f16[4,4,256,128]{3,2,1,0:T(8,128)(2,1)S(1)}, u32[]{:S(2)}, u32[]{:S(2)}) collective-permute-start(f16[4,4,256,128]{3,2,1,0:T(8,128)(2,1)S(1)} %convert_element_type.168), channel_id=1, source_target_pairs={{0,16},{1,17},{2,18},{3,19},{4,20},{5,21},{6,22},{7,23},{8,24},{9,... | collective-permute-start | bytes 3145736 | tf_op jit(solution)/shard_map/ppermute | solution.py:35
  12.8 23.2 %collective-permute-start.10 = (f16[4,4,256,128]{3,2,1,0:T(8,128)(2,1)S(1)}, f16[4,4,256,128]{3,2,1,0:T(8,128)(2,1)S(1)}, u32[]{:S(2)}, u32[]{:S(2)}) collective-permute-start(f16[4,4,256,128]{3,2,1,0:T(8,128)(2,1)S(1)} %convert_element_type.166), channel_id=1, source_target_pairs={{0,48},{1,49},{2,50},{3,51},{4,52},{5,53},{6,54},{7,55},{8,56},{9,... | collective-permute-start | bytes 3145736 | tf_op jit(solution)/shard_map/ppermute | solution.py:35
  33.2 12.6 %collective-permute-start.2 = (f16[2,4,256,128]{3,2,1,0:T(8,128)(2,1)S(1)}, f16[2,4,256,128]{3,2,1,0:T(8,128)(2,1)S(1)}, u32[]{:S(2)}, u32[]{:S(2)}) collective-permute-start(f16[2,4,256,128]{3,2,1,0:T(8,128)(2,1)S(1)} %get-tuple-element.41), channel_id=1, source_target_pairs={{0,4},{1,5},{2,6},{3,7},{4,8},{5,9},{6,10},{7,11},{8,12},{9,13},{1... | collective-permute-start | bytes 1572872 | tf_op jit(solution)/shard_map/ppermute | solution.py:35
  34.8 11.3 %collective-permute-start.3 = (f16[2,4,256,128]{3,2,1,0:T(8,128)(2,1)S(1)}, f16[2,4,256,128]{3,2,1,0:T(8,128)(2,1)S(1)}, u32[]{:S(2)}, u32[]{:S(2)}) collective-permute-start(f16[2,4,256,128]{3,2,1,0:T(8,128)(2,1)S(1)} %get-tuple-element.42), channel_id=1, source_target_pairs={{0,12},{1,13},{2,14},{3,15},{4,0},{5,1},{6,2},{7,3},{8,4},{9,5},{1... | collective-permute-start | bytes 1572872 | tf_op jit(solution)/shard_map/ppermute | solution.py:35
  36.3 16.0 %collective-permute-start.12 = (f16[2,4,256,128]{3,2,1,0:T(8,128)(2,1)S(1)}, f16[2,4,256,128]{3,2,1,0:T(8,128)(2,1)S(1)}, u32[]{:S(2)}, u32[]{:S(2)}) collective-permute-start(f16[2,4,256,128]{3,2,1,0:T(8,128)(2,1)S(1)} %get-tuple-element.37), channel_id=1, source_target_pairs={{0,16},{1,17},{2,18},{3,19},{4,20},{5,21},{6,22},{7,23},{8,24},{9,... | collective-permute-start | bytes 1572872 | tf_op jit(solution)/shard_map/ppermute | solution.py:35
  38.1 14.2 %collective-permute-start.13 = (f16[2,4,256,128]{3,2,1,0:T(8,128)(2,1)S(1)}, f16[2,4,256,128]{3,2,1,0:T(8,128)(2,1)S(1)}, u32[]{:S(2)}, u32[]{:S(2)}) collective-permute-start(f16[2,4,256,128]{3,2,1,0:T(8,128)(2,1)S(1)} %get-tuple-element.38), channel_id=1, source_target_pairs={{0,48},{1,49},{2,50},{3,51},{4,52},{5,53},{6,54},{7,55},{8,56},{9,... | collective-permute-start | bytes 1572872 | tf_op jit(solution)/shard_map/ppermute | solution.py:35
  46.5 10.2 %collective-permute-start.5 = (f16[4,256,128]{2,1,0:T(8,128)(2,1)S(1)}, f16[4,256,128]{2,1,0:T(8,128)(2,1)S(1)}, u32[]{:S(2)}, u32[]{:S(2)}) collective-permute-start(f16[4,256,128]{2,1,0:T(8,128)(2,1)S(1)} %fusion.6), channel_id=1, source_target_pairs={{0,16},{1,17},{2,18},{3,19},{4,20},{5,21},{6,22},{7,23},{8,24},{9,... | collective-permute-start | bytes 786440 | tf_op jit(solution)/shard_map/ppermute | solution.py:35
  48.5 13.5 %collective-permute-start.4 = (f16[4,256,128]{2,1,0:T(8,128)(2,1)S(1)}, f16[4,256,128]{2,1,0:T(8,128)(2,1)S(1)}, u32[]{:S(2)}, u32[]{:S(2)}) collective-permute-start(f16[4,256,128]{2,1,0:T(8,128)(2,1)S(1)} %get-tuple-element.45), channel_id=1, source_target_pairs={{0,32},{1,33},{2,34},{3,35},{4,36},{5,37},{6,38},{7,39},{8,40},{9,... | collective-permute-start | bytes 786440 | tf_op jit(solution)/shard_map/ppermute | solution.py:35
  51.2 10.8 %collective-permute-start.6 = (f16[4,256,128]{2,1,0:T(8,128)(2,1)S(1)}, f16[4,256,128]{2,1,0:T(8,128)(2,1)S(1)}, u32[]{:S(2)}, u32[]{:S(2)}) collective-permute-start(f16[4,256,128]{2,1,0:T(8,128)(2,1)S(1)} %get-tuple-element.46), channel_id=1, source_target_pairs={{0,48},{1,49},{2,50},{3,51},{4,52},{5,53},{6,54},{7,55},{8,56},{9,... | collective-permute-start | bytes 786440 | tf_op jit(solution)/shard_map/ppermute | solution.py:35
  52.8 14.2 %collective-permute-start.15 = (f16[4,256,128]{2,1,0:T(8,128)(2,1)S(1)}, f16[4,256,128]{2,1,0:T(8,128)(2,1)S(1)}, u32[]{:S(2)}, u32[]{:S(2)}) collective-permute-start(f16[4,256,128]{2,1,0:T(8,128)(2,1)S(1)} %fusion.7), channel_id=1, source_target_pairs={{0,4},{1,5},{2,6},{3,7},{4,8},{5,9},{6,10},{7,11},{8,12},{9,13},{1... | collective-permute-start | bytes 786440 | tf_op jit(solution)/shard_map/ppermute | solution.py:35
  53.5 13.4 %collective-permute-start.14 = (f16[4,256,128]{2,1,0:T(8,128)(2,1)S(1)}, f16[4,256,128]{2,1,0:T(8,128)(2,1)S(1)}, u32[]{:S(2)}, u32[]{:S(2)}) collective-permute-start(f16[4,256,128]{2,1,0:T(8,128)(2,1)S(1)} %get-tuple-element.43), channel_id=1, source_target_pairs={{0,8},{1,9},{2,10},{3,11},{4,12},{5,13},{6,14},{7,15},{8,0},{9,1},... | collective-permute-start | bytes 786440 | tf_op jit(solution)/shard_map/ppermute | solution.py:35
  56.8 10.2 %collective-permute-start.16 = (f16[4,256,128]{2,1,0:T(8,128)(2,1)S(1)}, f16[4,256,128]{2,1,0:T(8,128)(2,1)S(1)}, u32[]{:S(2)}, u32[]{:S(2)}) collective-permute-start(f16[4,256,128]{2,1,0:T(8,128)(2,1)S(1)} %get-tuple-element.44), channel_id=1, source_target_pairs={{0,12},{1,13},{2,14},{3,15},{4,0},{5,1},{6,2},{7,3},{8,4},{9,5},{1... | collective-permute-start | bytes 786440 | tf_op jit(solution)/shard_map/ppermute | solution.py:35
  62.1 14.6 %copy-start.1 = (f32[1,128,512]{2,1,0:T(8,128)S(1)}, f32[1,128,512]{2,1,0:T(8,128)}, u32[]{:S(2)}) copy-start(f32[1,128,512]{2,1,0:T(8,128)} %param.12) | copy-start | bytes 786436
  62.3 8.6 %collective-permute-start.7 = (f16[256,128]{1,0:T(8,128)(2,1)S(1)}, f16[256,128]{1,0:T(8,128)(2,1)S(1)}, u32[]{:S(2)}, u32[]{:S(2)}) collective-permute-start(f16[256,128]{1,0:T(8,128)(2,1)S(1)} %get-tuple-element.50), channel_id=1, source_target_pairs={{0,2},{1,3},{2,0},{3,1},{4,6},{5,7},{6,4},{7,5},{8,10},{9,11},{10,... | collective-permute-start | bytes 196616 | tf_op jit(solution)/shard_map/ppermute | solution.py:152
  65.3 5.9 %collective-permute-start.9 = (f16[256,128]{1,0:T(8,128)(2,1)S(1)}, f16[256,128]{1,0:T(8,128)(2,1)S(1)}, u32[]{:S(2)}, u32[]{:S(2)}) collective-permute-start(f16[256,128]{1,0:T(8,128)(2,1)S(1)} %get-tuple-element.51), channel_id=1, source_target_pairs={{0,1},{1,0},{2,3},{3,2},{4,5},{5,4},{6,7},{7,6},{8,9},{9,8},{10,11... | collective-permute-start | bytes 196616 | tf_op jit(solution)/shard_map/ppermute | solution.py:152
  67.0 5.6 %collective-permute-start.8 = (f16[256,128]{1,0:T(8,128)(2,1)S(1)}, f16[256,128]{1,0:T(8,128)(2,1)S(1)}, u32[]{:S(2)}, u32[]{:S(2)}) collective-permute-start(f16[256,128]{1,0:T(8,128)(2,1)S(1)} %get-tuple-element.52), channel_id=1, source_target_pairs={{0,3},{1,2},{2,1},{3,0},{4,7},{5,6},{6,5},{7,4},{8,11},{9,10},{10,... | collective-permute-start | bytes 196616 | tf_op jit(solution)/shard_map/ppermute | solution.py:152
  67.2 22.3 %copy-start.6 = (f32[128,512]{1,0:T(8,128)S(1)}, f32[128,512]{1,0:T(8,128)}, u32[]{:S(2)}) copy-start(f32[128,512]{1,0:T(8,128)} %moment.1) | copy-start | bytes 786436
  67.2 6.2 %collective-permute-start.17 = (f16[256,128]{1,0:T(8,128)(2,1)S(1)}, f16[256,128]{1,0:T(8,128)(2,1)S(1)}, u32[]{:S(2)}, u32[]{:S(2)}) collective-permute-start(f16[256,128]{1,0:T(8,128)(2,1)S(1)} %get-tuple-element.47), channel_id=1, source_target_pairs={{0,2},{1,3},{2,0},{3,1},{4,6},{5,7},{6,4},{7,5},{8,10},{9,11},{10,... | collective-permute-start | bytes 196616 | tf_op jit(solution)/shard_map/ppermute | solution.py:152
  68.5 5.7 %collective-permute-start.19 = (f16[256,128]{1,0:T(8,128)(2,1)S(1)}, f16[256,128]{1,0:T(8,128)(2,1)S(1)}, u32[]{:S(2)}, u32[]{:S(2)}) collective-permute-start(f16[256,128]{1,0:T(8,128)(2,1)S(1)} %get-tuple-element.48), channel_id=1, source_target_pairs={{0,1},{1,0},{2,3},{3,2},{4,5},{5,4},{6,7},{7,6},{8,9},{9,8},{10,11... | collective-permute-start | bytes 196616 | tf_op jit(solution)/shard_map/ppermute | solution.py:152
  70.8 5.8 %collective-permute-start.18 = (f16[256,128]{1,0:T(8,128)(2,1)S(1)}, f16[256,128]{1,0:T(8,128)(2,1)S(1)}, u32[]{:S(2)}, u32[]{:S(2)}) collective-permute-start(f16[256,128]{1,0:T(8,128)(2,1)S(1)} %get-tuple-element.49), channel_id=1, source_target_pairs={{0,3},{1,2},{2,1},{3,0},{4,7},{5,6},{6,5},{7,4},{8,11},{9,10},{10,... | collective-permute-start | bytes 196616 | tf_op jit(solution)/shard_map/ppermute | solution.py:152
  77.6 5.3 %collective-permute-start.20 = (f32[32,128]{1,0:T(8,128)S(1)}, f32[32,128]{1,0:T(8,128)S(1)}, u32[]{:S(2)}, u32[]{:S(2)}) collective-permute-start(f32[32,128]{1,0:T(8,128)S(1)} %shard_map.130), channel_id=1, source_target_pairs={{0,64},{64,0},{128,192},{192,128},{1,65},{65,1},{129,193},{193,129... | collective-permute-start | bytes 49160 | tf_op jit(solution)/shard_map/ppermute | solution.py:202
  83.0 6.5 %collective-permute-start.21 = (f32[32,128]{1,0:T(8,128)S(1)}, f32[32,128]{1,0:T(8,128)S(1)}, u32[]{:S(2)}, u32[]{:S(2)}) collective-permute-start(f32[32,128]{1,0:T(8,128)S(1)} %add.99.here), channel_id=1, source_target_pairs={{0,128},{64,192},{128,0},{192,64},{1,129},{65,193},{129,1},{193,65... | collective-permute-start | bytes 49160 | tf_op jit(solution)/shard_map/ppermute | solution.py:202
  (6 other events, 73.8 us)

commit v5 on v4

--- a/solution.py
+++ b/solution.py
@@ -43,114 +43,118 @@
     return value.astype(jnp.float32)
 
 
-def product_kernel(roles, unroll, a_ref, g_ref, *refs):
-    outs, (held, flipped, raw, sems, g_sem) = refs[:4], refs[4:]
+FAR_UP, FAR_DOWN = ((2, 0), (2, 1)), ((2, 2), (2, 3))
+UP, DOWN, OWN = (tuple((d, j) for j in range(RING)) for d in (1, 3, 0))
+
+
+def places(half, block):
+    return block[::-1] if half == 0 else block
+
+
+def product_kernel(plan, a_ref, g_ref, *refs):
+    outs, (held, turned, raw, sems, g_sem) = refs[: len(plan)], refs[len(plan) :]
     width = held.shape[2]
-    cut = flipped.shape[0] // 2
+    cut = turned.shape[0] // 2
     place = lax.axis_index("fsdp")
     y, x, z = place >> 4, (place >> 2) & 3, place & 3
-
-    def named(half, role, j):
-        low, high = roles[role]
-        d = high + (low - high) * (j < 2)
-        return ((y + j) & 3, (x + d) & 3) if half == 0 else ((y + d) & 3, (x + j) & 3)
-
-    def fetch(spot):
-        block = spot[0] * 4 + spot[1]
-        start = pl.multiple_of(block * width, width)
+    order = list(dict.fromkeys(places(half, block) for half, blocks in plan for block in blocks))
+
+    def fetch(slot):
+        up_y, up_x = order[slot]
+        start = pl.multiple_of((((y + up_y) & 3) * RING + ((x + up_x) & 3)) * width, width)
         return pltpu.make_async_copy(
-            a_ref.at[:, pl.ds(start, width)], held.at[block], sems.at[block]
+            a_ref.at[:, pl.ds(start, width)], held.at[slot], sems.at[slot]
         )
-
-    def left(do):
-        for role in range(2):
-            for j in range(4):
-                do(named(0, role, j))
-
-    def rest(do):
-        seen = {(j, roles[r][j // 2]) for r in range(2) for j in range(4)}
-        for role in range(2):
-            for j in range(4):
-                if (roles[role][j // 2], j) not in seen:
-                    do(named(1, role, j))
 
     bring = pltpu.make_async_copy(g_ref, raw, g_sem)
     bring.start()
-    left(lambda spot: fetch(spot).start())
-    rest(lambda spot: fetch(spot).start())
+    for slot in range(len(order)):
+        fetch(slot).start()
     bring.wait()
-    flipped[...] = raw[...].T * SCALE
-    for half in range(2):
-        part = flipped[:cut] if half == 0 else flipped[cut:]
-        if half == 1:
-            rest(lambda spot: fetch(spot).wait())
-
-        def multiply(j, carry):
-            spots = [named(half, role, j) for role in range(2)]
-            if half == 0:
-                for spot in spots:
-                    fetch(spot).wait()
-            for role, spot in enumerate(spots):
-                block = held[spot[0] * 4 + spot[1]]
-                product = jnp.dot(part, block, preferred_element_type=jnp.float32)
-                for k in range(RING):
-                    outs[2 * half + role][j, k ^ z] = product[:, k * 128 : (k + 1) * 128]
-            return carry
-
-        lax.fori_loop(0, RING, multiply, 0, unroll=unroll)
-
-
-def products(activations, out_grads, roles, unroll):
+    turned[...] = raw[...].T * SCALE
+    ready = 0
+    for out, (half, blocks) in zip(outs, plan):
+        part = turned[half * cut : (half + 1) * cut]
+        for k, block in enumerate(blocks):
+            slot = order.index(places(half, block))
+            while ready <= slot:
+                fetch(ready).wait()
+                ready += 1
+            product = jnp.dot(part, held[slot], preferred_element_type=jnp.float32)
+            for to in range(RING):
+                out[k, to ^ z] = product[:, to * 128 : (to + 1) * 128]
+
+
+def products(activations, out_grads, *kinds, vmem):
+    plan = [(half, blocks) for half in (0, 1) for blocks in kinds]
     depth, rows = activations.shape
-    count = RING * RING
-    cut = out_grads.shape[1] // 2
-    part = jax.ShapeDtypeStruct((RING, RING, cut, rows // count // RING), jnp.float32)
-    return pl.pallas_call(
-        functools.partial(product_kernel, roles, unroll),
+    width, cut = rows // RING**2, out_grads.shape[1] // 2
+    count = len({places(half, block) for half, blocks in plan for block in blocks})
+    total = sum(len(blocks) for _, blocks in plan)
+    outs = pl.pallas_call(
+        functools.partial(product_kernel, plan),
         in_specs=[pl.BlockSpec(memory_space=pl.ANY)] * 2,
-        out_specs=[pl.BlockSpec(memory_space=pltpu.VMEM)] * 4,
-        out_shape=[part] * 4,
+        out_specs=[pl.BlockSpec(memory_space=pltpu.VMEM)] * len(plan),
+        out_shape=[
+            jax.ShapeDtypeStruct((len(blocks), RING, cut, width // RING), jnp.float32)
+            for _, blocks in plan
+        ],
         scratch_shapes=[
-            pltpu.VMEM((count, depth, rows // count), activations.dtype),
+            pltpu.VMEM((count, depth, width), activations.dtype),
             pltpu.VMEM(out_grads.shape[::-1], out_grads.dtype),
             pltpu.VMEM(out_grads.shape, out_grads.dtype),
             pltpu.SemaphoreType.DMA((count,)),
             pltpu.SemaphoreType.DMA,
         ],
-        compiler_params=pltpu.CompilerParams(vmem_limit_bytes=44 << 20),
+        compiler_params=pltpu.CompilerParams(vmem_limit_bytes=vmem << 20),
         cost_estimate=pl.CostEstimate(
-            flops=2 * rows * cut * depth, bytes_accessed=depth * rows * 2, transcendentals=0
+            flops=2 * total * width * cut * depth,
+            bytes_accessed=count * depth * width * 2,
+            transcendentals=0,
         ),
     )(activations, out_grads)
+    return outs[: len(kinds)], outs[len(kinds) :]
+
+
+def block_sum(terms, k):
+    out = wide(terms[0][k])
+    for value in terms[1:]:
+        out = out + wide(value[k])
+    return out
 
 
 def scattered_grad(activations, out_grads):
-    sends = products(activations, out_grads, ((2, 1), (3, 2)), RING)
-    keeps = products(activations, out_grads, ((1, 3), (0, 0)), 1)
-
-    def along(path, value, d):
-        return shift(value, dx=d) if path == 0 else shift(value, dy=d)
-
-    def across(path, value, d):
-        return shift(value, dy=d) if path == 0 else shift(value, dx=d)
-
-    up = [along(p, narrow(sends[2 * p]), 1) for p in (0, 1)]
-    down = [along(p, narrow(sends[2 * p + 1]), -1) for p in (0, 1)]
+    halves = (0, 1)
+    far = products(activations, out_grads, FAR_UP, FAR_DOWN, vmem=49)
+    near = products(activations, out_grads, UP, DOWN, vmem=44)
+    own = products(activations, out_grads, OWN, vmem=44)
+
+    def along(half, value, d):
+        return shift(value, dx=d) if half == 0 else shift(value, dy=d)
+
+    def across(half, value, d):
+        return shift(value, dy=d) if half == 0 else shift(value, dx=d)
+
+    first = [(along(h, narrow(far[h][0]), 1), along(h, narrow(far[h][1]), -1)) for h in halves]
     sums = []
-    for p in (0, 1):
-        near, own = keeps[2 * p], keeps[2 * p + 1]
-        low = along(p, narrow(near[:2] + wide(up[p][:2])), 1)
-        high = along(p, narrow(near[2:] + wide(down[p][2:])), -1)
-        low = own[:2] + wide(down[p][:2]) + wide(low)
-        high = own[2:] + wide(up[p][2:]) + wide(high)
-        total = low[0]
-        for value, d in ((high[0], 2), (low[1], 1), (high[1], 3)):
-            total = total + wide(across(p, narrow(value), d))
-        part = total[0]
+    for h in halves:
+        up, down = near[h]
+        below, above = first[h]
+        pads = ((0, 0, 0),) * 3
+        zero = jnp.zeros((), jnp.float16)
+        up = narrow(up + wide(lax.pad(below, zero, ((0, 2, 0),) + pads)))
+        down = narrow(down + wide(lax.pad(above, zero, ((2, 0, 0),) + pads)))
+        terms = own[h][0], along(h, up, 1), along(h, down, -1)
+        sent = [across(h, narrow(block_sum(terms, d)), d) for d in (1, 3, 2)]
+        terms = [block_sum(terms, 0)] + sent
+        sent = []
         for flip in (2, 3, 1):
             pairs = [(k, k ^ flip) for k in range(RING**3)]
-            part = part + wide(lax.ppermute(narrow(total[flip]), "fsdp", pairs))
-        sums.append(part)
+            sent.append(lax.ppermute(narrow(block_sum(terms, flip)), "fsdp", pairs))
+        out = block_sum(terms, 0)
+        for value in sent:
+            out = out + wide(value)
+        sums.append(out)
     return sums
 
 

time: 91.1 us -> 88.3 us (0.969)
  waiting for transfers between devices: 31.2 us -> 27.4 us
  Pallas kernels: 14.3 us -> 16.2 us
    ppermute x14, waiting for transfers between devices: 23.9 us -> 20.9 us  [shift(): return lax.ppermute(value, 'fsdp', pairs)]
    pallas_call x2 -> x3, Pallas kernels: 11 us -> 12.9 us  [products(): pl.pallas_call(functools.partial(product_kernel, plan), in_specs=[pl.Bloc...]
    convert_element_type x8 -> x10, other arithmetic: 1.56 us -> 2.36 us  [narrow(): return value.astype(jnp.float16)]
  transfers between devices with their start and end apart: 22 -> 22, of which waited for: 11 -> 11; matrix products, arithmetic and copies ran while one was open for 3% -> 3% of each run, Pallas kernels for 7% -> 12%
where the time goes in v5:
time: 88.3 us; the launch traced here: 87.9 us
  starting transfers between devices  39.6 us (45%)
  waiting for transfers between devices  27.4 us (31%)
  Pallas kernels  16.2 us (18%)
  other arithmetic  2.77 us (3%)
  local copies, waits for them, and re-layouts  1.09 us (1%)
    ppermute x14, starting transfers between devices, shift(): return lax.ppermute(value, 'fsdp', pairs)  22.9 us
    ppermute x14, waiting for transfers between devices, shift(): return lax.ppermute(value, 'fsdp', pairs)  20.9 us
    pallas_call x3, Pallas kernels, products(): pl.pallas_call(functools.partial(product_kernel, plan), in_specs=[pl.Bloc...  12.9 us
    ppermute x2, starting transfers between devices, flipped_island(): return lax.ppermute(value, 'island', [(k, k ^ flip) for k in range(4)])  8.5 us
    ppermute x6, starting transfers between devices, scattered_grad(): sent.append(lax.ppermute(narrow(block_sum(terms, flip)), 'fsdp', pairs))  8.16 us
    ppermute x6, waiting for transfers between devices, scattered_grad(): sent.append(lax.ppermute(narrow(block_sum(terms, flip)), 'fsdp', pairs))  5.39 us
    pallas_call x3, Pallas kernels, on_chip(): pl.pallas_call(kernel, in_specs=[pl.BlockSpec(memory_space=pltpu.VMEM)] *...  3.27 us
    convert_element_type x10, other arithmetic, narrow(): return value.astype(jnp.float16)  2.36 us
  transfers between devices with their start and end apart: 22, of which 11 were waited for; matrix products, arithmetic and copies ran while one was open for 3% of the time, Pallas kernels for 12%

profile of v5, /device:TPU:1, one launch (start us, length us, event | category | flops | bytes accessed | tf_op | source)
XLA Modules:
  0.0 87.9 jit_solution(17890743814589827367)
XLA Ops:
  1.7 3.6 %shard_map.130 = (f32[2,4,256,128]{3,2,1,0:T(8,128)S(1)}, f32[2,4,256,128]{3,2,1,0:T(8,128)S(1)}, f32[2,4,256,128]{3,2,1,0:T(8,128)S(1)}, f32[2,4,256,128]{3,2,1,0:T(8,128)S(1)}) custom-call(bf16[512,8192]{1,0:T(8,128)(2,1)} %a_ref.5, bf16[512,512]{1,0:T(8,128)(2,1)S(1)} %copy-done), custom_call_target="tpu_custom_call" | custom-call | flops 1073741824 | bytes 3670016 | tf_op jit(solution)/shard_map/pallas_call | solution.py:94
  5.4 2.2 %collective-permute-start.10 = (f16[2,4,256,128]{3,2,1,0:T(8,128)(2,1)S(1)}, f16[2,4,256,128]{3,2,1,0:T(8,128)(2,1)S(1)}, u32[]{:S(2)}, u32[]{:S(2)}) collective-permute-start(f16[2,4,256,128]{3,2,1,0:T(8,128)(2,1)S(1)} %convert_element_type.291), channel_id=1, source_target_pairs={{0,16},{1,17},{2,18},{3,19},{4,20},{5,21},{6,22},{7,23},{8,24},{9,... | collective-permute-start | bytes 1572872 | tf_op jit(solution)/shard_map/ppermute | solution.py:35
  7.6 1.5 %collective-permute-start.12 = (f16[2,4,256,128]{3,2,1,0:T(8,128)(2,1)S(1)}, f16[2,4,256,128]{3,2,1,0:T(8,128)(2,1)S(1)}, u32[]{:S(2)}, u32[]{:S(2)}) collective-permute-start(f16[2,4,256,128]{3,2,1,0:T(8,128)(2,1)S(1)} %convert_element_type.295), channel_id=1, source_target_pairs={{0,48},{1,49},{2,50},{3,51},{4,52},{5,53},{6,54},{7,55},{8,56},{9,... | collective-permute-start | bytes 1572872 | tf_op jit(solution)/shard_map/ppermute | solution.py:35
  10.6 1.5 %collective-permute-start.2 = (f16[2,4,256,128]{3,2,1,0:T(8,128)(2,1)S(1)}, f16[2,4,256,128]{3,2,1,0:T(8,128)(2,1)S(1)}, u32[]{:S(2)}, u32[]{:S(2)}) collective-permute-start(f16[2,4,256,128]{3,2,1,0:T(8,128)(2,1)S(1)} %convert_element_type.260), channel_id=1, source_target_pairs={{0,12},{1,13},{2,14},{3,15},{4,0},{5,1},{6,2},{7,3},{8,4},{9,5},{1... | collective-permute-start | bytes 1572872 | tf_op jit(solution)/shard_map/ppermute | solution.py:35
  12.2 5.7 %shard_map.129 = (f32[4,4,256,128]{3,2,1,0:T(8,128)S(1)}, f32[4,4,256,128]{3,2,1,0:T(8,128)S(1)}, f32[4,4,256,128]{3,2,1,0:T(8,128)S(1)}, f32[4,4,256,128]{3,2,1,0:T(8,128)S(1)}) custom-call(bf16[512,8192]{1,0:T(8,128)(2,1)} %a_ref.5, bf16[512,512]{1,0:T(8,128)(2,1)S(1)} %copy-done.1), custom_call_target="tpu_custom_call" | custom-call | flops 2147483648 | bytes 6291456 | tf_op jit(solution)/shard_map/pallas_call | solution.py:94
  18.9 1.6 %collective-permute-start.11 = (f16[4,4,256,128]{3,2,1,0:T(8,128)(2,1)S(1)}, f16[4,4,256,128]{3,2,1,0:T(8,128)(2,1)S(1)}, u32[]{:S(2)}, u32[]{:S(2)}) collective-permute-start(f16[4,4,256,128]{3,2,1,0:T(8,128)(2,1)S(1)} %add_convert_fusion.1), channel_id=1, source_target_pairs={{0,16},{1,17},{2,18},{3,19},{4,20},{5,21},{6,22},{7,23},{8,24},{9,... | collective-permute-start | bytes 3145736 | tf_op jit(solution)/shard_map/ppermute | solution.py:35
  20.8 1.7 %collective-permute-start.13 = (f16[4,4,256,128]{3,2,1,0:T(8,128)(2,1)S(1)}, f16[4,4,256,128]{3,2,1,0:T(8,128)(2,1)S(1)}, u32[]{:S(2)}, u32[]{:S(2)}) collective-permute-start(f16[4,4,256,128]{3,2,1,0:T(8,128)(2,1)S(1)} %add_convert_fusion), channel_id=1, source_target_pairs={{0,48},{1,49},{2,50},{3,51},{4,52},{5,53},{6,54},{7,55},{8,56},{9,... | collective-permute-start | bytes 3145736 | tf_op jit(solution)/shard_map/ppermute | solution.py:35
  22.9 2.6 %collective-permute-start.1 = (f16[4,4,256,128]{3,2,1,0:T(8,128)(2,1)S(1)}, f16[4,4,256,128]{3,2,1,0:T(8,128)(2,1)S(1)}, u32[]{:S(2)}, u32[]{:S(2)}) collective-permute-start(f16[4,4,256,128]{3,2,1,0:T(8,128)(2,1)S(1)} %add_convert_fusion.3), channel_id=1, source_target_pairs={{0,4},{1,5},{2,6},{3,7},{4,8},{5,9},{6,10},{7,11},{8,12},{9,13},{1... | collective-permute-start | bytes 3145736 | tf_op jit(solution)/shard_map/ppermute | solution.py:35
  25.8 1.5 %collective-permute-start.3 = (f16[4,4,256,128]{3,2,1,0:T(8,128)(2,1)S(1)}, f16[4,4,256,128]{3,2,1,0:T(8,128)(2,1)S(1)}, u32[]{:S(2)}, u32[]{:S(2)}) collective-permute-start(f16[4,4,256,128]{3,2,1,0:T(8,128)(2,1)S(1)} %add_convert_fusion.2), channel_id=1, source_target_pairs={{0,12},{1,13},{2,14},{3,15},{4,0},{5,1},{6,2},{7,3},{8,4},{9,5},{1... | collective-permute-start | bytes 3145736 | tf_op jit(solution)/shard_map/ppermute | solution.py:35
  27.3 3.6 %shard_map.128 = (f32[4,4,256,128]{3,2,1,0:T(8,128)S(1)}, f32[4,4,256,128]{3,2,1,0:T(8,128)S(1)}) custom-call(bf16[512,8192]{1,0:T(8,128)(2,1)} %a_ref.5, bf16[512,512]{1,0:T(8,128)(2,1)S(1)} %copy-done.1), custom_call_target="tpu_custom_call" | custom-call | flops 1073741824 | bytes 3670016 | tf_op jit(solution)/shard_map/pallas_call | solution.py:94
  30.9 11.7 %collective-permute-done.11 = f16[4,4,256,128]{3,2,1,0:T(8,128)(2,1)S(1)} collective-permute-done((f16[4,4,256,128]{3,2,1,0:T(8,128)(2,1)S(1)}, f16[4,4,256,128]{3,2,1,0:T(8,128)(2,1)S(1)}, u32[]{:S(2)}, u32[]{:S(2)}) %collective-permute-start.11) | collective-permute-done | bytes 1048608 | tf_op jit(solution)/shard_map/ppermute | solution.py:35
  44.1 2.9 %collective-permute-start.14 = (f16[4,256,128]{2,1,0:T(8,128)(2,1)S(1)}, f16[4,256,128]{2,1,0:T(8,128)(2,1)S(1)}, u32[]{:S(2)}, u32[]{:S(2)}) collective-permute-start(f16[4,256,128]{2,1,0:T(8,128)(2,1)S(1)} %get-tuple-element.35), channel_id=1, source_target_pairs={{0,4},{1,5},{2,6},{3,7},{4,8},{5,9},{6,10},{7,11},{8,12},{9,13},{1... | collective-permute-start | bytes 786440 | tf_op jit(solution)/shard_map/ppermute | solution.py:35
  46.9 1.4 %collective-permute-start.15 = (f16[4,256,128]{2,1,0:T(8,128)(2,1)S(1)}, f16[4,256,128]{2,1,0:T(8,128)(2,1)S(1)}, u32[]{:S(2)}, u32[]{:S(2)}) collective-permute-start(f16[4,256,128]{2,1,0:T(8,128)(2,1)S(1)} %get-tuple-element.37), channel_id=1, source_target_pairs={{0,12},{1,13},{2,14},{3,15},{4,0},{5,1},{6,2},{7,3},{8,4},{9,5},{1... | collective-permute-start | bytes 786440 | tf_op jit(solution)/shard_map/ppermute | solution.py:35
  48.3 1.7 %collective-permute-start.16 = (f16[4,256,128]{2,1,0:T(8,128)(2,1)S(1)}, f16[4,256,128]{2,1,0:T(8,128)(2,1)S(1)}, u32[]{:S(2)}, u32[]{:S(2)}) collective-permute-start(f16[4,256,128]{2,1,0:T(8,128)(2,1)S(1)} %get-tuple-element.36), channel_id=1, source_target_pairs={{0,8},{1,9},{2,10},{3,11},{4,12},{5,13},{6,14},{7,15},{8,0},{9,1},... | collective-permute-start | bytes 786440 | tf_op jit(solution)/shard_map/ppermute | solution.py:35
  50.6 2.8 %collective-permute-start.5 = (f16[4,256,128]{2,1,0:T(8,128)(2,1)S(1)}, f16[4,256,128]{2,1,0:T(8,128)(2,1)S(1)}, u32[]{:S(2)}, u32[]{:S(2)}) collective-permute-start(f16[4,256,128]{2,1,0:T(8,128)(2,1)S(1)} %get-tuple-element.41), channel_id=1, source_target_pairs={{0,48},{1,49},{2,50},{3,51},{4,52},{5,53},{6,54},{7,55},{8,56},{9,... | collective-permute-start | bytes 786440 | tf_op jit(solution)/shard_map/ppermute | solution.py:35
  55.2 5.8 %collective-permute-done.16 = f16[4,256,128]{2,1,0:T(8,128)(2,1)S(1)} collective-permute-done((f16[4,256,128]{2,1,0:T(8,128)(2,1)S(1)}, f16[4,256,128]{2,1,0:T(8,128)(2,1)S(1)}, u32[]{:S(2)}, u32[]{:S(2)}) %collective-permute-start.16) | collective-permute-done | bytes 262176 | tf_op jit(solution)/shard_map/ppermute | solution.py:35
  61.1 3.1 %collective-permute-start.17 = (f16[256,128]{1,0:T(8,128)(2,1)S(1)}, f16[256,128]{1,0:T(8,128)(2,1)S(1)}, u32[]{:S(2)}, u32[]{:S(2)}) collective-permute-start(f16[256,128]{1,0:T(8,128)(2,1)S(1)} %get-tuple-element.43), channel_id=1, source_target_pairs={{0,2},{1,3},{2,0},{3,1},{4,6},{5,7},{6,4},{7,5},{8,10},{9,11},{10,... | collective-permute-start | bytes 196616 | tf_op jit(solution)/shard_map/ppermute | solution.py:153
  64.2 1.4 %collective-permute-start.18 = (f16[256,128]{1,0:T(8,128)(2,1)S(1)}, f16[256,128]{1,0:T(8,128)(2,1)S(1)}, u32[]{:S(2)}, u32[]{:S(2)}) collective-permute-start(f16[256,128]{1,0:T(8,128)(2,1)S(1)} %get-tuple-element.45), channel_id=1, source_target_pairs={{0,3},{1,2},{2,1},{3,0},{4,7},{5,6},{6,5},{7,4},{8,11},{9,10},{10,... | collective-permute-start | bytes 196616 | tf_op jit(solution)/shard_map/ppermute | solution.py:153
  65.9 2.0 %collective-permute-start.7 = (f16[256,128]{1,0:T(8,128)(2,1)S(1)}, f16[256,128]{1,0:T(8,128)(2,1)S(1)}, u32[]{:S(2)}, u32[]{:S(2)}) collective-permute-start(f16[256,128]{1,0:T(8,128)(2,1)S(1)} %get-tuple-element.46), channel_id=1, source_target_pairs={{0,2},{1,3},{2,0},{3,1},{4,6},{5,7},{6,4},{7,5},{8,10},{9,11},{10,... | collective-permute-start | bytes 196616 | tf_op jit(solution)/shard_map/ppermute | solution.py:153
  67.9 1.4 %collective-permute-start.8 = (f16[256,128]{1,0:T(8,128)(2,1)S(1)}, f16[256,128]{1,0:T(8,128)(2,1)S(1)}, u32[]{:S(2)}, u32[]{:S(2)}) collective-permute-start(f16[256,128]{1,0:T(8,128)(2,1)S(1)} %get-tuple-element.48), channel_id=1, source_target_pairs={{0,3},{1,2},{2,1},{3,0},{4,7},{5,6},{6,5},{7,4},{8,11},{9,10},{10,... | collective-permute-start | bytes 196616 | tf_op jit(solution)/shard_map/ppermute | solution.py:153
  70.1 3.7 %collective-permute-done.7 = f16[256,128]{1,0:T(8,128)(2,1)S(1)} collective-permute-done((f16[256,128]{1,0:T(8,128)(2,1)S(1)}, f16[256,128]{1,0:T(8,128)(2,1)S(1)}, u32[]{:S(2)}, u32[]{:S(2)}) %collective-permute-start.7) | collective-permute-done | bytes 65568 | tf_op jit(solution)/shard_map/ppermute | solution.py:153
  75.9 3.2 %collective-permute-start.20 = (f32[32,128]{1,0:T(8,128)S(1)}, f32[32,128]{1,0:T(8,128)S(1)}, u32[]{:S(2)}, u32[]{:S(2)}) collective-permute-start(f32[32,128]{1,0:T(8,128)S(1)} %shard_map.131), channel_id=1, source_target_pairs={{0,64},{64,0},{128,192},{192,128},{1,65},{65,1},{129,193},{193,129... | collective-permute-start | bytes 49160 | tf_op jit(solution)/shard_map/ppermute | solution.py:206
  79.9 5.3 %collective-permute-start.21 = (f32[32,128]{1,0:T(8,128)S(1)}, f32[32,128]{1,0:T(8,128)S(1)}, u32[]{:S(2)}, u32[]{:S(2)}) collective-permute-start(f32[32,128]{1,0:T(8,128)S(1)} %add.275.here), channel_id=1, source_target_pairs={{0,128},{64,192},{128,0},{192,64},{1,129},{65,193},{129,1},{193,65... | collective-permute-start | bytes 49160 | tf_op jit(solution)/shard_map/ppermute | solution.py:206
  86.4 1.4 %shard_map.132 = (f32[128,512]{1,0:T(8,128)}, f32[128,512]{1,0:T(8,128)}, f32[32,128]{1,0:T(8,128)}) custom-call(f32[32,128]{1,0:T(8,128)S(1)} %add.275.here, f32[32,128]{1,0:T(8,128)S(1)} %collective-permute-done.21.there, f32[128,512]{1,0:T(8,128)S(1)} %copy-done.4, f32[128,512]{1,0:T(8,128)S(1)} %copy-done.7, f32[32,128]{1,0:T(8,128)S(1)} %copy-done.8, ...), custom_call_target="tpu_custom_call" | custom-call | tf_op jit(solution)/shard_map/pallas_call | solution.py:196
  (59 shorter events, 13.5 us)
Async XLA Ops:
  5.4 13.2 %collective-permute-start.10 = (f16[2,4,256,128]{3,2,1,0:T(8,128)(2,1)S(1)}, f16[2,4,256,128]{3,2,1,0:T(8,128)(2,1)S(1)}, u32[]{:S(2)}, u32[]{:S(2)}) collective-permute-start(f16[2,4,256,128]{3,2,1,0:T(8,128)(2,1)S(1)} %convert_element_type.291), channel_id=1, source_target_pairs={{0,16},{1,17},{2,18},{3,19},{4,20},{5,21},{6,22},{7,23},{8,24},{9,... | collective-permute-start | bytes 1572872 | tf_op jit(solution)/shard_map/ppermute | solution.py:35
  7.6 12.9 %collective-permute-start.12 = (f16[2,4,256,128]{3,2,1,0:T(8,128)(2,1)S(1)}, f16[2,4,256,128]{3,2,1,0:T(8,128)(2,1)S(1)}, u32[]{:S(2)}, u32[]{:S(2)}) collective-permute-start(f16[2,4,256,128]{3,2,1,0:T(8,128)(2,1)S(1)} %convert_element_type.295), channel_id=1, source_target_pairs={{0,48},{1,49},{2,50},{3,51},{4,52},{5,53},{6,54},{7,55},{8,56},{9,... | collective-permute-start | bytes 1572872 | tf_op jit(solution)/shard_map/ppermute | solution.py:35
  9.3 13.3 %collective-permute-start = (f16[2,4,256,128]{3,2,1,0:T(8,128)(2,1)S(1)}, f16[2,4,256,128]{3,2,1,0:T(8,128)(2,1)S(1)}, u32[]{:S(2)}, u32[]{:S(2)}) collective-permute-start(f16[2,4,256,128]{3,2,1,0:T(8,128)(2,1)S(1)} %convert_element_type.256), channel_id=1, source_target_pairs={{0,4},{1,5},{2,6},{3,7},{4,8},{5,9},{6,10},{7,11},{8,12},{9,13},{1... | collective-permute-start | bytes 1572872 | tf_op jit(solution)/shard_map/ppermute | solution.py:35
  10.6 14.8 %collective-permute-start.2 = (f16[2,4,256,128]{3,2,1,0:T(8,128)(2,1)S(1)}, f16[2,4,256,128]{3,2,1,0:T(8,128)(2,1)S(1)}, u32[]{:S(2)}, u32[]{:S(2)}) collective-permute-start(f16[2,4,256,128]{3,2,1,0:T(8,128)(2,1)S(1)} %convert_element_type.260), channel_id=1, source_target_pairs={{0,12},{1,13},{2,14},{3,15},{4,0},{5,1},{6,2},{7,3},{8,4},{9,5},{1... | collective-permute-start | bytes 1572872 | tf_op jit(solution)/shard_map/ppermute | solution.py:35
  18.9 23.7 %collective-permute-start.11 = (f16[4,4,256,128]{3,2,1,0:T(8,128)(2,1)S(1)}, f16[4,4,256,128]{3,2,1,0:T(8,128)(2,1)S(1)}, u32[]{:S(2)}, u32[]{:S(2)}) collective-permute-start(f16[4,4,256,128]{3,2,1,0:T(8,128)(2,1)S(1)} %add_convert_fusion.1), channel_id=1, source_target_pairs={{0,16},{1,17},{2,18},{3,19},{4,20},{5,21},{6,22},{7,23},{8,24},{9,... | collective-permute-start | bytes 3145736 | tf_op jit(solution)/shard_map/ppermute | solution.py:35
  20.8 22.8 %collective-permute-start.13 = (f16[4,4,256,128]{3,2,1,0:T(8,128)(2,1)S(1)}, f16[4,4,256,128]{3,2,1,0:T(8,128)(2,1)S(1)}, u32[]{:S(2)}, u32[]{:S(2)}) collective-permute-start(f16[4,4,256,128]{3,2,1,0:T(8,128)(2,1)S(1)} %add_convert_fusion), channel_id=1, source_target_pairs={{0,48},{1,49},{2,50},{3,51},{4,52},{5,53},{6,54},{7,55},{8,56},{9,... | collective-permute-start | bytes 3145736 | tf_op jit(solution)/shard_map/ppermute | solution.py:35
  22.9 27.0 %collective-permute-start.1 = (f16[4,4,256,128]{3,2,1,0:T(8,128)(2,1)S(1)}, f16[4,4,256,128]{3,2,1,0:T(8,128)(2,1)S(1)}, u32[]{:S(2)}, u32[]{:S(2)}) collective-permute-start(f16[4,4,256,128]{3,2,1,0:T(8,128)(2,1)S(1)} %add_convert_fusion.3), channel_id=1, source_target_pairs={{0,4},{1,5},{2,6},{3,7},{4,8},{5,9},{6,10},{7,11},{8,12},{9,13},{1... | collective-permute-start | bytes 3145736 | tf_op jit(solution)/shard_map/ppermute | solution.py:35
  25.8 24.2 %collective-permute-start.3 = (f16[4,4,256,128]{3,2,1,0:T(8,128)(2,1)S(1)}, f16[4,4,256,128]{3,2,1,0:T(8,128)(2,1)S(1)}, u32[]{:S(2)}, u32[]{:S(2)}) collective-permute-start(f16[4,4,256,128]{3,2,1,0:T(8,128)(2,1)S(1)} %add_convert_fusion.2), channel_id=1, source_target_pairs={{0,12},{1,13},{2,14},{3,15},{4,0},{5,1},{6,2},{7,3},{8,4},{9,5},{1... | collective-permute-start | bytes 3145736 | tf_op jit(solution)/shard_map/ppermute | solution.py:35
  44.1 10.4 %collective-permute-start.14 = (f16[4,256,128]{2,1,0:T(8,128)(2,1)S(1)}, f16[4,256,128]{2,1,0:T(8,128)(2,1)S(1)}, u32[]{:S(2)}, u32[]{:S(2)}) collective-permute-start(f16[4,256,128]{2,1,0:T(8,128)(2,1)S(1)} %get-tuple-element.35), channel_id=1, source_target_pairs={{0,4},{1,5},{2,6},{3,7},{4,8},{5,9},{6,10},{7,11},{8,12},{9,13},{1... | collective-permute-start | bytes 786440 | tf_op jit(solution)/shard_map/ppermute | solution.py:35
  46.9 8.3 %collective-permute-start.15 = (f16[4,256,128]{2,1,0:T(8,128)(2,1)S(1)}, f16[4,256,128]{2,1,0:T(8,128)(2,1)S(1)}, u32[]{:S(2)}, u32[]{:S(2)}) collective-permute-start(f16[4,256,128]{2,1,0:T(8,128)(2,1)S(1)} %get-tuple-element.37), channel_id=1, source_target_pairs={{0,12},{1,13},{2,14},{3,15},{4,0},{5,1},{6,2},{7,3},{8,4},{9,5},{1... | collective-permute-start | bytes 786440 | tf_op jit(solution)/shard_map/ppermute | solution.py:35
  48.3 12.7 %collective-permute-start.16 = (f16[4,256,128]{2,1,0:T(8,128)(2,1)S(1)}, f16[4,256,128]{2,1,0:T(8,128)(2,1)S(1)}, u32[]{:S(2)}, u32[]{:S(2)}) collective-permute-start(f16[4,256,128]{2,1,0:T(8,128)(2,1)S(1)} %get-tuple-element.36), channel_id=1, source_target_pairs={{0,8},{1,9},{2,10},{3,11},{4,12},{5,13},{6,14},{7,15},{8,0},{9,1},... | collective-permute-start | bytes 786440 | tf_op jit(solution)/shard_map/ppermute | solution.py:35
  50.4 24.6 %copy-start.2 = (f32[1,128,512]{2,1,0:T(8,128)S(1)}, f32[1,128,512]{2,1,0:T(8,128)}, u32[]{:S(2)}) copy-start(f32[1,128,512]{2,1,0:T(8,128)} %param.12) | copy-start | bytes 786436
  50.4 24.6 %copy-start.3 = (f32[1,128,512]{2,1,0:T(8,128)S(1)}, f32[1,128,512]{2,1,0:T(8,128)}, u32[]{:S(2)}) copy-start(f32[1,128,512]{2,1,0:T(8,128)} %param.13) | copy-start | bytes 786436
  50.5 15.1 %collective-permute-start.4 = (f16[4,256,128]{2,1,0:T(8,128)(2,1)S(1)}, f16[4,256,128]{2,1,0:T(8,128)(2,1)S(1)}, u32[]{:S(2)}, u32[]{:S(2)}) collective-permute-start(f16[4,256,128]{2,1,0:T(8,128)(2,1)S(1)} %get-tuple-element.39), channel_id=1, source_target_pairs={{0,16},{1,17},{2,18},{3,19},{4,20},{5,21},{6,22},{7,23},{8,24},{9,... | collective-permute-start | bytes 786440 | tf_op jit(solution)/shard_map/ppermute | solution.py:35
  50.6 15.2 %collective-permute-start.5 = (f16[4,256,128]{2,1,0:T(8,128)(2,1)S(1)}, f16[4,256,128]{2,1,0:T(8,128)(2,1)S(1)}, u32[]{:S(2)}, u32[]{:S(2)}) collective-permute-start(f16[4,256,128]{2,1,0:T(8,128)(2,1)S(1)} %get-tuple-element.41), channel_id=1, source_target_pairs={{0,48},{1,49},{2,50},{3,51},{4,52},{5,53},{6,54},{7,55},{8,56},{9,... | collective-permute-start | bytes 786440 | tf_op jit(solution)/shard_map/ppermute | solution.py:35
  54.4 11.4 %collective-permute-start.6 = (f16[4,256,128]{2,1,0:T(8,128)(2,1)S(1)}, f16[4,256,128]{2,1,0:T(8,128)(2,1)S(1)}, u32[]{:S(2)}, u32[]{:S(2)}) collective-permute-start(f16[4,256,128]{2,1,0:T(8,128)(2,1)S(1)} %get-tuple-element.40), channel_id=1, source_target_pairs={{0,32},{1,33},{2,34},{3,35},{4,36},{5,37},{6,38},{7,39},{8,40},{9,... | collective-permute-start | bytes 786440 | tf_op jit(solution)/shard_map/ppermute | solution.py:35
  61.1 8.3 %collective-permute-start.17 = (f16[256,128]{1,0:T(8,128)(2,1)S(1)}, f16[256,128]{1,0:T(8,128)(2,1)S(1)}, u32[]{:S(2)}, u32[]{:S(2)}) collective-permute-start(f16[256,128]{1,0:T(8,128)(2,1)S(1)} %get-tuple-element.43), channel_id=1, source_target_pairs={{0,2},{1,3},{2,0},{3,1},{4,6},{5,7},{6,4},{7,5},{8,10},{9,11},{10,... | collective-permute-start | bytes 196616 | tf_op jit(solution)/shard_map/ppermute | solution.py:153
  64.2 5.2 %collective-permute-start.18 = (f16[256,128]{1,0:T(8,128)(2,1)S(1)}, f16[256,128]{1,0:T(8,128)(2,1)S(1)}, u32[]{:S(2)}, u32[]{:S(2)}) collective-permute-start(f16[256,128]{1,0:T(8,128)(2,1)S(1)} %get-tuple-element.45), channel_id=1, source_target_pairs={{0,3},{1,2},{2,1},{3,0},{4,7},{5,6},{6,5},{7,4},{8,11},{9,10},{10,... | collective-permute-start | bytes 196616 | tf_op jit(solution)/shard_map/ppermute | solution.py:153
  65.6 4.4 %collective-permute-start.19 = (f16[256,128]{1,0:T(8,128)(2,1)S(1)}, f16[256,128]{1,0:T(8,128)(2,1)S(1)}, u32[]{:S(2)}, u32[]{:S(2)}) collective-permute-start(f16[256,128]{1,0:T(8,128)(2,1)S(1)} %get-tuple-element.44), channel_id=1, source_target_pairs={{0,1},{1,0},{2,3},{3,2},{4,5},{5,4},{6,7},{7,6},{8,9},{9,8},{10,11... | collective-permute-start | bytes 196616 | tf_op jit(solution)/shard_map/ppermute | solution.py:153
  65.9 7.8 %collective-permute-start.7 = (f16[256,128]{1,0:T(8,128)(2,1)S(1)}, f16[256,128]{1,0:T(8,128)(2,1)S(1)}, u32[]{:S(2)}, u32[]{:S(2)}) collective-permute-start(f16[256,128]{1,0:T(8,128)(2,1)S(1)} %get-tuple-element.46), channel_id=1, source_target_pairs={{0,2},{1,3},{2,0},{3,1},{4,6},{5,7},{6,4},{7,5},{8,10},{9,11},{10,... | collective-permute-start | bytes 196616 | tf_op jit(solution)/shard_map/ppermute | solution.py:153
  67.9 5.8 %collective-permute-start.8 = (f16[256,128]{1,0:T(8,128)(2,1)S(1)}, f16[256,128]{1,0:T(8,128)(2,1)S(1)}, u32[]{:S(2)}, u32[]{:S(2)}) collective-permute-start(f16[256,128]{1,0:T(8,128)(2,1)S(1)} %get-tuple-element.48), channel_id=1, source_target_pairs={{0,3},{1,2},{2,1},{3,0},{4,7},{5,6},{6,5},{7,4},{8,11},{9,10},{10,... | collective-permute-start | bytes 196616 | tf_op jit(solution)/shard_map/ppermute | solution.py:153
  69.4 5.5 %collective-permute-start.9 = (f16[256,128]{1,0:T(8,128)(2,1)S(1)}, f16[256,128]{1,0:T(8,128)(2,1)S(1)}, u32[]{:S(2)}, u32[]{:S(2)}) collective-permute-start(f16[256,128]{1,0:T(8,128)(2,1)S(1)} %get-tuple-element.47), channel_id=1, source_target_pairs={{0,1},{1,0},{2,3},{3,2},{4,5},{5,4},{6,7},{7,6},{8,9},{9,8},{10,11... | collective-permute-start | bytes 196616 | tf_op jit(solution)/shard_map/ppermute | solution.py:153
  75.9 4.0 %collective-permute-start.20 = (f32[32,128]{1,0:T(8,128)S(1)}, f32[32,128]{1,0:T(8,128)S(1)}, u32[]{:S(2)}, u32[]{:S(2)}) collective-permute-start(f32[32,128]{1,0:T(8,128)S(1)} %shard_map.131), channel_id=1, source_target_pairs={{0,64},{64,0},{128,192},{192,128},{1,65},{65,1},{129,193},{193,129... | collective-permute-start | bytes 49160 | tf_op jit(solution)/shard_map/ppermute | solution.py:206
  79.9 6.5 %collective-permute-start.21 = (f32[32,128]{1,0:T(8,128)S(1)}, f32[32,128]{1,0:T(8,128)S(1)}, u32[]{:S(2)}, u32[]{:S(2)}) collective-permute-start(f32[32,128]{1,0:T(8,128)S(1)} %add.275.here), channel_id=1, source_target_pairs={{0,128},{64,192},{128,0},{192,64},{1,129},{65,193},{129,1},{193,65... | collective-permute-start | bytes 49160 | tf_op jit(solution)/shard_map/ppermute | solution.py:206
  (7 other events, 124.3 us)

commit v6 on v5

--- a/solution.py
+++ b/solution.py
@@ -145,7 +145,7 @@
         up = narrow(up + wide(lax.pad(below, zero, ((0, 2, 0),) + pads)))
         down = narrow(down + wide(lax.pad(above, zero, ((2, 0, 0),) + pads)))
         terms = own[h][0], along(h, up, 1), along(h, down, -1)
-        sent = [across(h, narrow(block_sum(terms, d)), d) for d in (1, 3, 2)]
+        sent = [across(h, narrow(block_sum(terms, d)), d) for d in ((2, 1, 3), (1, 3, 2))[h]]
         terms = [block_sum(terms, 0)] + sent
         sent = []
         for flip in (2, 3, 1):
@@ -179,25 +179,42 @@
     )
 
 
-def outer_kernel(here, there, base, moment, rows, cols, new_base, new_outer, band_ref):
+def outer_kernel(here, there, base, moment, rows, cols, new_base, new_outer, band_ref, *scratch):
+    base_part, outer_part, band_part, sems = scratch
     band = (here[...] + there[...]) / 4.0
-    band_ref[...] = band
+    band_part[...] = band
+    copies = [pltpu.make_async_copy(band_part, band_ref, sems.at[0])]
+    copies[0].start()
     inner = lax.dot_general(
         rows[...], band, (((0,), (0,)), ((), ())), precision=HIGHEST,
         preferred_element_type=jnp.float32,
     )
-    smooth = jnp.dot(inner, cols[...], precision=HIGHEST, preferred_element_type=jnp.float32)
-    outer = 0.9 * moment[...] + smooth
-    new_outer[...] = outer
-    new_base[...] = base[...] - 0.7 * (smooth + 0.9 * outer)
-
-
-def on_chip(kernel, shapes, *args):
+    half = moment.shape[1] // 2
+    for k in range(2):
+        at, small = slice(k * half, (k + 1) * half), slice(k * half // 4, (k + 1) * half // 4)
+        smooth = jnp.dot(
+            inner[:, small], cols[small, at], precision=HIGHEST,
+            preferred_element_type=jnp.float32,
+        )
+        outer = 0.9 * moment[:, at] + smooth
+        outer_part[:, at] = outer
+        base_part[:, at] = base[:, at] - 0.7 * (smooth + 0.9 * outer)
+        for part, whole in ((outer_part, new_outer), (base_part, new_base)):
+            copy = pltpu.make_async_copy(part.at[:, at], whole.at[:, at], sems.at[len(copies)])
+            copy.start()
+            copies.append(copy)
+    for copy in copies:
+        copy.wait()
+
+
+def on_chip(kernel, shapes, *args, copies=0):
     return pl.pallas_call(
         kernel,
         in_specs=[pl.BlockSpec(memory_space=pltpu.VMEM)] * len(args),
-        out_specs=[pl.BlockSpec(memory_space=pltpu.VMEM)] * len(shapes),
+        out_specs=[pl.BlockSpec(memory_space=pl.ANY if copies else pltpu.VMEM)] * len(shapes),
         out_shape=[jax.ShapeDtypeStruct(shape, jnp.float32) for shape in shapes],
+        scratch_shapes=[pltpu.VMEM(shape, jnp.float32) for shape in shapes if copies]
+        + [pltpu.SemaphoreType.DMA((copies,))] * (copies > 0),
         compiler_params=pltpu.CompilerParams(vmem_limit_bytes=8 << 20),
     )(*args)
 
@@ -216,7 +233,7 @@
     there = flipped_island(chip, 2)
     first, second = on_chip(moment_kernel, [full, full], *state)
     new_base, new_outer, band = on_chip(
-        outer_kernel, [full, full, small], chip, there, base, outer_moment, rows, cols
+        outer_kernel, [full, full, small], chip, there, base, outer_moment, rows, cols, copies=5
     )
     return (new_base, new_outer, band, first[None], second[None])
 

time: 88.3 us -> 88.4 us (level)
  no operation moved by 1% of the time
where the time goes in v6:
time: 88.4 us; the launch traced here: 88 us
  starting transfers between devices  40.3 us (46%)
  waiting for transfers between devices  26.6 us (30%)
  Pallas kernels  16.2 us (18%)
  other arithmetic  2.77 us (3%)
  local copies, waits for them, and re-layouts  1.09 us (1%)
  between operations  1.04 us (1%)
    ppermute x14, starting transfers between devices, shift(): return lax.ppermute(value, 'fsdp', pairs)  23.6 us
    ppermute x14, waiting for transfers between devices, shift(): return lax.ppermute(value, 'fsdp', pairs)  20.2 us
    pallas_call x3, Pallas kernels, products(): pl.pallas_call(functools.partial(product_kernel, plan), in_specs=[pl.Bloc...  12.9 us
    ppermute x2, starting transfers between devices, flipped_island(): return lax.ppermute(value, 'island', [(k, k ^ flip) for k in range(4)])  8.5 us
    ppermute x6, starting transfers between devices, scattered_grad(): sent.append(lax.ppermute(narrow(block_sum(terms, flip)), 'fsdp', pairs))  8.16 us
    ppermute x6, waiting for transfers between devices, scattered_grad(): sent.append(lax.ppermute(narrow(block_sum(terms, flip)), 'fsdp', pairs))  5.39 us
    pallas_call x3, Pallas kernels, on_chip(): pl.pallas_call(kernel, in_specs=[pl.BlockSpec(memory_space=pltpu.VMEM)] *...  3.25 us
    convert_element_type x10, other arithmetic, narrow(): return value.astype(jnp.float16)  2.36 us
  transfers between devices with their start and end apart: 22, of which 11 were waited for; matrix products, arithmetic and copies ran while one was open for 3% of the time, Pallas kernels for 12%

profile of v6, /device:TPU:1, one launch (start us, length us, event | category | flops | bytes accessed | tf_op | source)
XLA Modules:
  0.0 88.0 jit_solution(3260989095832125887)
XLA Ops:
  1.7 3.6 %shard_map.130 = (f32[2,4,256,128]{3,2,1,0:T(8,128)S(1)}, f32[2,4,256,128]{3,2,1,0:T(8,128)S(1)}, f32[2,4,256,128]{3,2,1,0:T(8,128)S(1)}, f32[2,4,256,128]{3,2,1,0:T(8,128)S(1)}) custom-call(bf16[512,8192]{1,0:T(8,128)(2,1)} %a_ref.5, bf16[512,512]{1,0:T(8,128)(2,1)S(1)} %copy-done), custom_call_target="tpu_custom_call" | custom-call | flops 1073741824 | bytes 3670016 | tf_op jit(solution)/shard_map/pallas_call | solution.py:94
  5.4 2.2 %collective-permute-start.10 = (f16[2,4,256,128]{3,2,1,0:T(8,128)(2,1)S(1)}, f16[2,4,256,128]{3,2,1,0:T(8,128)(2,1)S(1)}, u32[]{:S(2)}, u32[]{:S(2)}) collective-permute-start(f16[2,4,256,128]{3,2,1,0:T(8,128)(2,1)S(1)} %convert_element_type.291), channel_id=1, source_target_pairs={{0,16},{1,17},{2,18},{3,19},{4,20},{5,21},{6,22},{7,23},{8,24},{9,... | collective-permute-start | bytes 1572872 | tf_op jit(solution)/shard_map/ppermute | solution.py:35
  7.6 1.5 %collective-permute-start.12 = (f16[2,4,256,128]{3,2,1,0:T(8,128)(2,1)S(1)}, f16[2,4,256,128]{3,2,1,0:T(8,128)(2,1)S(1)}, u32[]{:S(2)}, u32[]{:S(2)}) collective-permute-start(f16[2,4,256,128]{3,2,1,0:T(8,128)(2,1)S(1)} %convert_element_type.295), channel_id=1, source_target_pairs={{0,48},{1,49},{2,50},{3,51},{4,52},{5,53},{6,54},{7,55},{8,56},{9,... | collective-permute-start | bytes 1572872 | tf_op jit(solution)/shard_map/ppermute | solution.py:35
  10.6 1.5 %collective-permute-start.2 = (f16[2,4,256,128]{3,2,1,0:T(8,128)(2,1)S(1)}, f16[2,4,256,128]{3,2,1,0:T(8,128)(2,1)S(1)}, u32[]{:S(2)}, u32[]{:S(2)}) collective-permute-start(f16[2,4,256,128]{3,2,1,0:T(8,128)(2,1)S(1)} %convert_element_type.260), channel_id=1, source_target_pairs={{0,12},{1,13},{2,14},{3,15},{4,0},{5,1},{6,2},{7,3},{8,4},{9,5},{1... | collective-permute-start | bytes 1572872 | tf_op jit(solution)/shard_map/ppermute | solution.py:35
  12.2 5.7 %shard_map.129 = (f32[4,4,256,128]{3,2,1,0:T(8,128)S(1)}, f32[4,4,256,128]{3,2,1,0:T(8,128)S(1)}, f32[4,4,256,128]{3,2,1,0:T(8,128)S(1)}, f32[4,4,256,128]{3,2,1,0:T(8,128)S(1)}) custom-call(bf16[512,8192]{1,0:T(8,128)(2,1)} %a_ref.5, bf16[512,512]{1,0:T(8,128)(2,1)S(1)} %copy-done.1), custom_call_target="tpu_custom_call" | custom-call | flops 2147483648 | bytes 6291456 | tf_op jit(solution)/shard_map/pallas_call | solution.py:94
  18.9 1.6 %collective-permute-start.11 = (f16[4,4,256,128]{3,2,1,0:T(8,128)(2,1)S(1)}, f16[4,4,256,128]{3,2,1,0:T(8,128)(2,1)S(1)}, u32[]{:S(2)}, u32[]{:S(2)}) collective-permute-start(f16[4,4,256,128]{3,2,1,0:T(8,128)(2,1)S(1)} %add_convert_fusion.1), channel_id=1, source_target_pairs={{0,16},{1,17},{2,18},{3,19},{4,20},{5,21},{6,22},{7,23},{8,24},{9,... | collective-permute-start | bytes 3145736 | tf_op jit(solution)/shard_map/ppermute | solution.py:35
  20.8 1.7 %collective-permute-start.13 = (f16[4,4,256,128]{3,2,1,0:T(8,128)(2,1)S(1)}, f16[4,4,256,128]{3,2,1,0:T(8,128)(2,1)S(1)}, u32[]{:S(2)}, u32[]{:S(2)}) collective-permute-start(f16[4,4,256,128]{3,2,1,0:T(8,128)(2,1)S(1)} %add_convert_fusion), channel_id=1, source_target_pairs={{0,48},{1,49},{2,50},{3,51},{4,52},{5,53},{6,54},{7,55},{8,56},{9,... | collective-permute-start | bytes 3145736 | tf_op jit(solution)/shard_map/ppermute | solution.py:35
  22.9 2.6 %collective-permute-start.1 = (f16[4,4,256,128]{3,2,1,0:T(8,128)(2,1)S(1)}, f16[4,4,256,128]{3,2,1,0:T(8,128)(2,1)S(1)}, u32[]{:S(2)}, u32[]{:S(2)}) collective-permute-start(f16[4,4,256,128]{3,2,1,0:T(8,128)(2,1)S(1)} %add_convert_fusion.3), channel_id=1, source_target_pairs={{0,4},{1,5},{2,6},{3,7},{4,8},{5,9},{6,10},{7,11},{8,12},{9,13},{1... | collective-permute-start | bytes 3145736 | tf_op jit(solution)/shard_map/ppermute | solution.py:35
  25.8 1.5 %collective-permute-start.3 = (f16[4,4,256,128]{3,2,1,0:T(8,128)(2,1)S(1)}, f16[4,4,256,128]{3,2,1,0:T(8,128)(2,1)S(1)}, u32[]{:S(2)}, u32[]{:S(2)}) collective-permute-start(f16[4,4,256,128]{3,2,1,0:T(8,128)(2,1)S(1)} %add_convert_fusion.2), channel_id=1, source_target_pairs={{0,12},{1,13},{2,14},{3,15},{4,0},{5,1},{6,2},{7,3},{8,4},{9,5},{1... | collective-permute-start | bytes 3145736 | tf_op jit(solution)/shard_map/ppermute | solution.py:35
  27.3 3.6 %shard_map.128 = (f32[4,4,256,128]{3,2,1,0:T(8,128)S(1)}, f32[4,4,256,128]{3,2,1,0:T(8,128)S(1)}) custom-call(bf16[512,8192]{1,0:T(8,128)(2,1)} %a_ref.5, bf16[512,512]{1,0:T(8,128)(2,1)S(1)} %copy-done.1), custom_call_target="tpu_custom_call" | custom-call | flops 1073741824 | bytes 3670016 | tf_op jit(solution)/shard_map/pallas_call | solution.py:94
  30.9 11.7 %collective-permute-done.11 = f16[4,4,256,128]{3,2,1,0:T(8,128)(2,1)S(1)} collective-permute-done((f16[4,4,256,128]{3,2,1,0:T(8,128)(2,1)S(1)}, f16[4,4,256,128]{3,2,1,0:T(8,128)(2,1)S(1)}, u32[]{:S(2)}, u32[]{:S(2)}) %collective-permute-start.11) | collective-permute-done | bytes 1048608 | tf_op jit(solution)/shard_map/ppermute | solution.py:35
  44.1 2.9 %collective-permute-start.14 = (f16[4,256,128]{2,1,0:T(8,128)(2,1)S(1)}, f16[4,256,128]{2,1,0:T(8,128)(2,1)S(1)}, u32[]{:S(2)}, u32[]{:S(2)}) collective-permute-start(f16[4,256,128]{2,1,0:T(8,128)(2,1)S(1)} %get-tuple-element.35), channel_id=1, source_target_pairs={{0,4},{1,5},{2,6},{3,7},{4,8},{5,9},{6,10},{7,11},{8,12},{9,13},{1... | collective-permute-start | bytes 786440 | tf_op jit(solution)/shard_map/ppermute | solution.py:35
  48.3 1.7 %collective-permute-start.16 = (f16[4,256,128]{2,1,0:T(8,128)(2,1)S(1)}, f16[4,256,128]{2,1,0:T(8,128)(2,1)S(1)}, u32[]{:S(2)}, u32[]{:S(2)}) collective-permute-start(f16[4,256,128]{2,1,0:T(8,128)(2,1)S(1)} %get-tuple-element.36), channel_id=1, source_target_pairs={{0,8},{1,9},{2,10},{3,11},{4,12},{5,13},{6,14},{7,15},{8,0},{9,1},... | collective-permute-start | bytes 786440 | tf_op jit(solution)/shard_map/ppermute | solution.py:35
  50.5 1.5 %collective-permute-start.4 = (f16[4,256,128]{2,1,0:T(8,128)(2,1)S(1)}, f16[4,256,128]{2,1,0:T(8,128)(2,1)S(1)}, u32[]{:S(2)}, u32[]{:S(2)}) collective-permute-start(f16[4,256,128]{2,1,0:T(8,128)(2,1)S(1)} %get-tuple-element.39), channel_id=1, source_target_pairs={{0,32},{1,33},{2,34},{3,35},{4,36},{5,37},{6,38},{7,39},{8,40},{9,... | collective-permute-start | bytes 786440 | tf_op jit(solution)/shard_map/ppermute | solution.py:35
  51.9 2.0 %collective-permute-start.5 = (f16[4,256,128]{2,1,0:T(8,128)(2,1)S(1)}, f16[4,256,128]{2,1,0:T(8,128)(2,1)S(1)}, u32[]{:S(2)}, u32[]{:S(2)}) collective-permute-start(f16[4,256,128]{2,1,0:T(8,128)(2,1)S(1)} %get-tuple-element.41), channel_id=1, source_target_pairs={{0,16},{1,17},{2,18},{3,19},{4,20},{5,21},{6,22},{7,23},{8,24},{9,... | collective-permute-start | bytes 786440 | tf_op jit(solution)/shard_map/ppermute | solution.py:35
  55.2 5.8 %collective-permute-done.16 = f16[4,256,128]{2,1,0:T(8,128)(2,1)S(1)} collective-permute-done((f16[4,256,128]{2,1,0:T(8,128)(2,1)S(1)}, f16[4,256,128]{2,1,0:T(8,128)(2,1)S(1)}, u32[]{:S(2)}, u32[]{:S(2)}) %collective-permute-start.16) | collective-permute-done | bytes 262176 | tf_op jit(solution)/shard_map/ppermute | solution.py:35
  61.1 3.1 %collective-permute-start.17 = (f16[256,128]{1,0:T(8,128)(2,1)S(1)}, f16[256,128]{1,0:T(8,128)(2,1)S(1)}, u32[]{:S(2)}, u32[]{:S(2)}) collective-permute-start(f16[256,128]{1,0:T(8,128)(2,1)S(1)} %get-tuple-element.43), channel_id=1, source_target_pairs={{0,2},{1,3},{2,0},{3,1},{4,6},{5,7},{6,4},{7,5},{8,10},{9,11},{10,... | collective-permute-start | bytes 196616 | tf_op jit(solution)/shard_map/ppermute | solution.py:153
  64.2 1.4 %collective-permute-start.18 = (f16[256,128]{1,0:T(8,128)(2,1)S(1)}, f16[256,128]{1,0:T(8,128)(2,1)S(1)}, u32[]{:S(2)}, u32[]{:S(2)}) collective-permute-start(f16[256,128]{1,0:T(8,128)(2,1)S(1)} %get-tuple-element.45), channel_id=1, source_target_pairs={{0,3},{1,2},{2,1},{3,0},{4,7},{5,6},{6,5},{7,4},{8,11},{9,10},{10,... | collective-permute-start | bytes 196616 | tf_op jit(solution)/shard_map/ppermute | solution.py:153
  65.9 2.0 %collective-permute-start.7 = (f16[256,128]{1,0:T(8,128)(2,1)S(1)}, f16[256,128]{1,0:T(8,128)(2,1)S(1)}, u32[]{:S(2)}, u32[]{:S(2)}) collective-permute-start(f16[256,128]{1,0:T(8,128)(2,1)S(1)} %get-tuple-element.46), channel_id=1, source_target_pairs={{0,2},{1,3},{2,0},{3,1},{4,6},{5,7},{6,4},{7,5},{8,10},{9,11},{10,... | collective-permute-start | bytes 196616 | tf_op jit(solution)/shard_map/ppermute | solution.py:153
  67.9 1.4 %collective-permute-start.8 = (f16[256,128]{1,0:T(8,128)(2,1)S(1)}, f16[256,128]{1,0:T(8,128)(2,1)S(1)}, u32[]{:S(2)}, u32[]{:S(2)}) collective-permute-start(f16[256,128]{1,0:T(8,128)(2,1)S(1)} %get-tuple-element.48), channel_id=1, source_target_pairs={{0,3},{1,2},{2,1},{3,0},{4,7},{5,6},{6,5},{7,4},{8,11},{9,10},{10,... | collective-permute-start | bytes 196616 | tf_op jit(solution)/shard_map/ppermute | solution.py:153
  70.1 3.7 %collective-permute-done.7 = f16[256,128]{1,0:T(8,128)(2,1)S(1)} collective-permute-done((f16[256,128]{1,0:T(8,128)(2,1)S(1)}, f16[256,128]{1,0:T(8,128)(2,1)S(1)}, u32[]{:S(2)}, u32[]{:S(2)}) %collective-permute-start.7) | collective-permute-done | bytes 65568 | tf_op jit(solution)/shard_map/ppermute | solution.py:153
  75.9 3.2 %collective-permute-start.20 = (f32[32,128]{1,0:T(8,128)S(1)}, f32[32,128]{1,0:T(8,128)S(1)}, u32[]{:S(2)}, u32[]{:S(2)}) collective-permute-start(f32[32,128]{1,0:T(8,128)S(1)} %shard_map.131), channel_id=1, source_target_pairs={{0,64},{64,0},{128,192},{192,128},{1,65},{65,1},{129,193},{193,129... | collective-permute-start | bytes 49160 | tf_op jit(solution)/shard_map/ppermute | solution.py:223
  79.9 5.3 %collective-permute-start.21 = (f32[32,128]{1,0:T(8,128)S(1)}, f32[32,128]{1,0:T(8,128)S(1)}, u32[]{:S(2)}, u32[]{:S(2)}) collective-permute-start(f32[32,128]{1,0:T(8,128)S(1)} %add.275.here), channel_id=1, source_target_pairs={{0,128},{64,192},{128,0},{192,64},{1,129},{65,193},{129,1},{193,65... | collective-permute-start | bytes 49160 | tf_op jit(solution)/shard_map/ppermute | solution.py:223
  86.4 1.4 %shard_map.132 = (f32[128,512]{1,0:T(8,128)}, f32[128,512]{1,0:T(8,128)}, f32[32,128]{1,0:T(8,128)}) custom-call(f32[32,128]{1,0:T(8,128)S(1)} %add.275.here, f32[32,128]{1,0:T(8,128)S(1)} %collective-permute-done.21.there, f32[128,512]{1,0:T(8,128)S(1)} %copy-done.4, f32[128,512]{1,0:T(8,128)S(1)} %copy-done.7, f32[32,128]{1,0:T(8,128)S(1)} %copy-done.8, ...), custom_call_target="tpu_custom_call" | custom-call | tf_op jit(solution)/shard_map/pallas_call | solution.py:211
  (59 shorter events, 14.3 us)
Async XLA Ops:
  5.4 13.2 %collective-permute-start.10 = (f16[2,4,256,128]{3,2,1,0:T(8,128)(2,1)S(1)}, f16[2,4,256,128]{3,2,1,0:T(8,128)(2,1)S(1)}, u32[]{:S(2)}, u32[]{:S(2)}) collective-permute-start(f16[2,4,256,128]{3,2,1,0:T(8,128)(2,1)S(1)} %convert_element_type.291), channel_id=1, source_target_pairs={{0,16},{1,17},{2,18},{3,19},{4,20},{5,21},{6,22},{7,23},{8,24},{9,... | collective-permute-start | bytes 1572872 | tf_op jit(solution)/shard_map/ppermute | solution.py:35
  7.6 12.9 %collective-permute-start.12 = (f16[2,4,256,128]{3,2,1,0:T(8,128)(2,1)S(1)}, f16[2,4,256,128]{3,2,1,0:T(8,128)(2,1)S(1)}, u32[]{:S(2)}, u32[]{:S(2)}) collective-permute-start(f16[2,4,256,128]{3,2,1,0:T(8,128)(2,1)S(1)} %convert_element_type.295), channel_id=1, source_target_pairs={{0,48},{1,49},{2,50},{3,51},{4,52},{5,53},{6,54},{7,55},{8,56},{9,... | collective-permute-start | bytes 1572872 | tf_op jit(solution)/shard_map/ppermute | solution.py:35
  9.3 13.3 %collective-permute-start = (f16[2,4,256,128]{3,2,1,0:T(8,128)(2,1)S(1)}, f16[2,4,256,128]{3,2,1,0:T(8,128)(2,1)S(1)}, u32[]{:S(2)}, u32[]{:S(2)}) collective-permute-start(f16[2,4,256,128]{3,2,1,0:T(8,128)(2,1)S(1)} %convert_element_type.256), channel_id=1, source_target_pairs={{0,4},{1,5},{2,6},{3,7},{4,8},{5,9},{6,10},{7,11},{8,12},{9,13},{1... | collective-permute-start | bytes 1572872 | tf_op jit(solution)/shard_map/ppermute | solution.py:35
  10.6 14.8 %collective-permute-start.2 = (f16[2,4,256,128]{3,2,1,0:T(8,128)(2,1)S(1)}, f16[2,4,256,128]{3,2,1,0:T(8,128)(2,1)S(1)}, u32[]{:S(2)}, u32[]{:S(2)}) collective-permute-start(f16[2,4,256,128]{3,2,1,0:T(8,128)(2,1)S(1)} %convert_element_type.260), channel_id=1, source_target_pairs={{0,12},{1,13},{2,14},{3,15},{4,0},{5,1},{6,2},{7,3},{8,4},{9,5},{1... | collective-permute-start | bytes 1572872 | tf_op jit(solution)/shard_map/ppermute | solution.py:35
  18.9 23.7 %collective-permute-start.11 = (f16[4,4,256,128]{3,2,1,0:T(8,128)(2,1)S(1)}, f16[4,4,256,128]{3,2,1,0:T(8,128)(2,1)S(1)}, u32[]{:S(2)}, u32[]{:S(2)}) collective-permute-start(f16[4,4,256,128]{3,2,1,0:T(8,128)(2,1)S(1)} %add_convert_fusion.1), channel_id=1, source_target_pairs={{0,16},{1,17},{2,18},{3,19},{4,20},{5,21},{6,22},{7,23},{8,24},{9,... | collective-permute-start | bytes 3145736 | tf_op jit(solution)/shard_map/ppermute | solution.py:35
  20.8 22.8 %collective-permute-start.13 = (f16[4,4,256,128]{3,2,1,0:T(8,128)(2,1)S(1)}, f16[4,4,256,128]{3,2,1,0:T(8,128)(2,1)S(1)}, u32[]{:S(2)}, u32[]{:S(2)}) collective-permute-start(f16[4,4,256,128]{3,2,1,0:T(8,128)(2,1)S(1)} %add_convert_fusion), channel_id=1, source_target_pairs={{0,48},{1,49},{2,50},{3,51},{4,52},{5,53},{6,54},{7,55},{8,56},{9,... | collective-permute-start | bytes 3145736 | tf_op jit(solution)/shard_map/ppermute | solution.py:35
  22.9 27.0 %collective-permute-start.1 = (f16[4,4,256,128]{3,2,1,0:T(8,128)(2,1)S(1)}, f16[4,4,256,128]{3,2,1,0:T(8,128)(2,1)S(1)}, u32[]{:S(2)}, u32[]{:S(2)}) collective-permute-start(f16[4,4,256,128]{3,2,1,0:T(8,128)(2,1)S(1)} %add_convert_fusion.3), channel_id=1, source_target_pairs={{0,4},{1,5},{2,6},{3,7},{4,8},{5,9},{6,10},{7,11},{8,12},{9,13},{1... | collective-permute-start | bytes 3145736 | tf_op jit(solution)/shard_map/ppermute | solution.py:35
  25.8 24.2 %collective-permute-start.3 = (f16[4,4,256,128]{3,2,1,0:T(8,128)(2,1)S(1)}, f16[4,4,256,128]{3,2,1,0:T(8,128)(2,1)S(1)}, u32[]{:S(2)}, u32[]{:S(2)}) collective-permute-start(f16[4,4,256,128]{3,2,1,0:T(8,128)(2,1)S(1)} %add_convert_fusion.2), channel_id=1, source_target_pairs={{0,12},{1,13},{2,14},{3,15},{4,0},{5,1},{6,2},{7,3},{8,4},{9,5},{1... | collective-permute-start | bytes 3145736 | tf_op jit(solution)/shard_map/ppermute | solution.py:35
  44.1 10.4 %collective-permute-start.14 = (f16[4,256,128]{2,1,0:T(8,128)(2,1)S(1)}, f16[4,256,128]{2,1,0:T(8,128)(2,1)S(1)}, u32[]{:S(2)}, u32[]{:S(2)}) collective-permute-start(f16[4,256,128]{2,1,0:T(8,128)(2,1)S(1)} %get-tuple-element.35), channel_id=1, source_target_pairs={{0,4},{1,5},{2,6},{3,7},{4,8},{5,9},{6,10},{7,11},{8,12},{9,13},{1... | collective-permute-start | bytes 786440 | tf_op jit(solution)/shard_map/ppermute | solution.py:35
  46.9 8.3 %collective-permute-start.15 = (f16[4,256,128]{2,1,0:T(8,128)(2,1)S(1)}, f16[4,256,128]{2,1,0:T(8,128)(2,1)S(1)}, u32[]{:S(2)}, u32[]{:S(2)}) collective-permute-start(f16[4,256,128]{2,1,0:T(8,128)(2,1)S(1)} %get-tuple-element.37), channel_id=1, source_target_pairs={{0,12},{1,13},{2,14},{3,15},{4,0},{5,1},{6,2},{7,3},{8,4},{9,5},{1... | collective-permute-start | bytes 786440 | tf_op jit(solution)/shard_map/ppermute | solution.py:35
  48.3 12.7 %collective-permute-start.16 = (f16[4,256,128]{2,1,0:T(8,128)(2,1)S(1)}, f16[4,256,128]{2,1,0:T(8,128)(2,1)S(1)}, u32[]{:S(2)}, u32[]{:S(2)}) collective-permute-start(f16[4,256,128]{2,1,0:T(8,128)(2,1)S(1)} %get-tuple-element.36), channel_id=1, source_target_pairs={{0,8},{1,9},{2,10},{3,11},{4,12},{5,13},{6,14},{7,15},{8,0},{9,1},... | collective-permute-start | bytes 786440 | tf_op jit(solution)/shard_map/ppermute | solution.py:35
  50.4 24.6 %copy-start.2 = (f32[1,128,512]{2,1,0:T(8,128)S(1)}, f32[1,128,512]{2,1,0:T(8,128)}, u32[]{:S(2)}) copy-start(f32[1,128,512]{2,1,0:T(8,128)} %param.12) | copy-start | bytes 786436
  50.4 24.6 %copy-start.3 = (f32[1,128,512]{2,1,0:T(8,128)S(1)}, f32[1,128,512]{2,1,0:T(8,128)}, u32[]{:S(2)}) copy-start(f32[1,128,512]{2,1,0:T(8,128)} %param.13) | copy-start | bytes 786436
  50.5 15.1 %collective-permute-start.4 = (f16[4,256,128]{2,1,0:T(8,128)(2,1)S(1)}, f16[4,256,128]{2,1,0:T(8,128)(2,1)S(1)}, u32[]{:S(2)}, u32[]{:S(2)}) collective-permute-start(f16[4,256,128]{2,1,0:T(8,128)(2,1)S(1)} %get-tuple-element.39), channel_id=1, source_target_pairs={{0,32},{1,33},{2,34},{3,35},{4,36},{5,37},{6,38},{7,39},{8,40},{9,... | collective-permute-start | bytes 786440 | tf_op jit(solution)/shard_map/ppermute | solution.py:35
  51.9 13.9 %collective-permute-start.5 = (f16[4,256,128]{2,1,0:T(8,128)(2,1)S(1)}, f16[4,256,128]{2,1,0:T(8,128)(2,1)S(1)}, u32[]{:S(2)}, u32[]{:S(2)}) collective-permute-start(f16[4,256,128]{2,1,0:T(8,128)(2,1)S(1)} %get-tuple-element.41), channel_id=1, source_target_pairs={{0,16},{1,17},{2,18},{3,19},{4,20},{5,21},{6,22},{7,23},{8,24},{9,... | collective-permute-start | bytes 786440 | tf_op jit(solution)/shard_map/ppermute | solution.py:35
  54.4 11.4 %collective-permute-start.6 = (f16[4,256,128]{2,1,0:T(8,128)(2,1)S(1)}, f16[4,256,128]{2,1,0:T(8,128)(2,1)S(1)}, u32[]{:S(2)}, u32[]{:S(2)}) collective-permute-start(f16[4,256,128]{2,1,0:T(8,128)(2,1)S(1)} %get-tuple-element.40), channel_id=1, source_target_pairs={{0,48},{1,49},{2,50},{3,51},{4,52},{5,53},{6,54},{7,55},{8,56},{9,... | collective-permute-start | bytes 786440 | tf_op jit(solution)/shard_map/ppermute | solution.py:35
  61.1 8.3 %collective-permute-start.17 = (f16[256,128]{1,0:T(8,128)(2,1)S(1)}, f16[256,128]{1,0:T(8,128)(2,1)S(1)}, u32[]{:S(2)}, u32[]{:S(2)}) collective-permute-start(f16[256,128]{1,0:T(8,128)(2,1)S(1)} %get-tuple-element.43), channel_id=1, source_target_pairs={{0,2},{1,3},{2,0},{3,1},{4,6},{5,7},{6,4},{7,5},{8,10},{9,11},{10,... | collective-permute-start | bytes 196616 | tf_op jit(solution)/shard_map/ppermute | solution.py:153
  64.2 5.2 %collective-permute-start.18 = (f16[256,128]{1,0:T(8,128)(2,1)S(1)}, f16[256,128]{1,0:T(8,128)(2,1)S(1)}, u32[]{:S(2)}, u32[]{:S(2)}) collective-permute-start(f16[256,128]{1,0:T(8,128)(2,1)S(1)} %get-tuple-element.45), channel_id=1, source_target_pairs={{0,3},{1,2},{2,1},{3,0},{4,7},{5,6},{6,5},{7,4},{8,11},{9,10},{10,... | collective-permute-start | bytes 196616 | tf_op jit(solution)/shard_map/ppermute | solution.py:153
  65.6 4.4 %collective-permute-start.19 = (f16[256,128]{1,0:T(8,128)(2,1)S(1)}, f16[256,128]{1,0:T(8,128)(2,1)S(1)}, u32[]{:S(2)}, u32[]{:S(2)}) collective-permute-start(f16[256,128]{1,0:T(8,128)(2,1)S(1)} %get-tuple-element.44), channel_id=1, source_target_pairs={{0,1},{1,0},{2,3},{3,2},{4,5},{5,4},{6,7},{7,6},{8,9},{9,8},{10,11... | collective-permute-start | bytes 196616 | tf_op jit(solution)/shard_map/ppermute | solution.py:153
  65.9 7.8 %collective-permute-start.7 = (f16[256,128]{1,0:T(8,128)(2,1)S(1)}, f16[256,128]{1,0:T(8,128)(2,1)S(1)}, u32[]{:S(2)}, u32[]{:S(2)}) collective-permute-start(f16[256,128]{1,0:T(8,128)(2,1)S(1)} %get-tuple-element.46), channel_id=1, source_target_pairs={{0,2},{1,3},{2,0},{3,1},{4,6},{5,7},{6,4},{7,5},{8,10},{9,11},{10,... | collective-permute-start | bytes 196616 | tf_op jit(solution)/shard_map/ppermute | solution.py:153
  67.9 5.8 %collective-permute-start.8 = (f16[256,128]{1,0:T(8,128)(2,1)S(1)}, f16[256,128]{1,0:T(8,128)(2,1)S(1)}, u32[]{:S(2)}, u32[]{:S(2)}) collective-permute-start(f16[256,128]{1,0:T(8,128)(2,1)S(1)} %get-tuple-element.48), channel_id=1, source_target_pairs={{0,3},{1,2},{2,1},{3,0},{4,7},{5,6},{6,5},{7,4},{8,11},{9,10},{10,... | collective-permute-start | bytes 196616 | tf_op jit(solution)/shard_map/ppermute | solution.py:153
  69.4 5.5 %collective-permute-start.9 = (f16[256,128]{1,0:T(8,128)(2,1)S(1)}, f16[256,128]{1,0:T(8,128)(2,1)S(1)}, u32[]{:S(2)}, u32[]{:S(2)}) collective-permute-start(f16[256,128]{1,0:T(8,128)(2,1)S(1)} %get-tuple-element.47), channel_id=1, source_target_pairs={{0,1},{1,0},{2,3},{3,2},{4,5},{5,4},{6,7},{7,6},{8,9},{9,8},{10,11... | collective-permute-start | bytes 196616 | tf_op jit(solution)/shard_map/ppermute | solution.py:153
  75.9 4.0 %collective-permute-start.20 = (f32[32,128]{1,0:T(8,128)S(1)}, f32[32,128]{1,0:T(8,128)S(1)}, u32[]{:S(2)}, u32[]{:S(2)}) collective-permute-start(f32[32,128]{1,0:T(8,128)S(1)} %shard_map.131), channel_id=1, source_target_pairs={{0,64},{64,0},{128,192},{192,128},{1,65},{65,1},{129,193},{193,129... | collective-permute-start | bytes 49160 | tf_op jit(solution)/shard_map/ppermute | solution.py:223
  79.9 6.5 %collective-permute-start.21 = (f32[32,128]{1,0:T(8,128)S(1)}, f32[32,128]{1,0:T(8,128)S(1)}, u32[]{:S(2)}, u32[]{:S(2)}) collective-permute-start(f32[32,128]{1,0:T(8,128)S(1)} %add.275.here), channel_id=1, source_target_pairs={{0,128},{64,192},{128,0},{192,64},{1,129},{65,193},{129,1},{193,65... | collective-permute-start | bytes 49160 | tf_op jit(solution)/shard_map/ppermute | solution.py:223
  (7 other events, 124.3 us)

commit v7 on v5

--- a/solution.py
+++ b/solution.py
@@ -123,6 +123,10 @@
     return out
 
 
+def crossing(value, flip):
+    return lax.ppermute(value, "fsdp", [(k, k ^ flip) for k in range(RING**3)])
+
+
 def scattered_grad(activations, out_grads):
     halves = (0, 1)
     far = products(activations, out_grads, FAR_UP, FAR_DOWN, vmem=49)
@@ -147,11 +151,14 @@
         terms = own[h][0], along(h, up, 1), along(h, down, -1)
         sent = [across(h, narrow(block_sum(terms, d)), d) for d in (1, 3, 2)]
         terms = [block_sum(terms, 0)] + sent
-        sent = []
-        for flip in (2, 3, 1):
-            pairs = [(k, k ^ flip) for k in range(RING**3)]
-            sent.append(lax.ppermute(narrow(block_sum(terms, flip)), "fsdp", pairs))
-        out = block_sum(terms, 0)
+        if h == 0:
+            sent = [crossing(narrow(block_sum(terms, flip)), flip) for flip in (2, 3, 1)]
+            out = block_sum(terms, 0)
+        else:
+            pair = narrow(jnp.stack([block_sum(terms, 1), block_sum(terms, 3)]))
+            pair = crossing(pair, 1)
+            sent = [pair[0], crossing(narrow(block_sum(terms, 2) + wide(pair[1])), 2)]
+            out = block_sum(terms, 0)
         for value in sent:
             out = out + wide(value)
         sums.append(out)

time: 88.3 us -> 88.2 us (level)
  starting transfers between devices: 39.6 us -> 42.1 us
  waiting for transfers between devices: 27.4 us -> 25 us
    ppermute x6 -> x5, waiting for transfers between devices: 5.39 us -> 2.89 us  [crossing(): lax.ppermute(value, 'fsdp', [(k, k ^ flip) for k in range(RING ** 3)])]
    ppermute x2, starting transfers between devices: 8.5 us -> 10.9 us  [flipped_island(): return lax.ppermute(value, 'island', [(k, k ^ flip) for k in range(4)])]
    ppermute x6 -> x5, starting transfers between devices: 8.16 us -> 8.31 us  [crossing(): lax.ppermute(value, 'fsdp', [(k, k ^ flip) for k in range(RING ** 3)])]
    convert_element_type x10 -> x11, other arithmetic: 2.36 us -> 2.41 us  [narrow(): return value.astype(jnp.float16)]
  transfers between devices with their start and end apart: 22 -> 21, of which waited for: 11 -> 11; matrix products, arithmetic and copies ran while one was open for 3% -> 3% of each run, Pallas kernels for 12% -> 12%
where the time goes in v7:
time: 88.2 us; the launch traced here: 88.1 us
  starting transfers between devices  42.1 us (48%)
  waiting for transfers between devices  25 us (28%)
  Pallas kernels  16.2 us (18%)
  other arithmetic  2.8 us (3%)
  local copies, waits for them, and re-layouts  1.09 us (1%)
  between operations  0.9 us (1%)
    ppermute x14, starting transfers between devices, shift(): return lax.ppermute(value, 'fsdp', pairs)  22.9 us
    ppermute x14, waiting for transfers between devices, shift(): return lax.ppermute(value, 'fsdp', pairs)  21.1 us
    pallas_call x3, Pallas kernels, products(): pl.pallas_call(functools.partial(product_kernel, plan), in_specs=[pl.Bloc...  12.9 us
    ppermute x2, starting transfers between devices, flipped_island(): return lax.ppermute(value, 'island', [(k, k ^ flip) for k in range(4)])  10.9 us
    ppermute x5, starting transfers between devices, crossing(): lax.ppermute(value, 'fsdp', [(k, k ^ flip) for k in range(RING ** 3)])  8.31 us
    pallas_call x3, Pallas kernels, on_chip(): pl.pallas_call(kernel, in_specs=[pl.BlockSpec(memory_space=pltpu.VMEM)] *...  3.27 us
    ppermute x5, waiting for transfers between devices, crossing(): lax.ppermute(value, 'fsdp', [(k, k ^ flip) for k in range(RING ** 3)])  2.89 us
    convert_element_type x11, other arithmetic, narrow(): return value.astype(jnp.float16)  2.41 us
  transfers between devices with their start and end apart: 21, of which 11 were waited for; matrix products, arithmetic and copies ran while one was open for 3% of the time, Pallas kernels for 12%

profile of v7, /device:TPU:1, one launch (start us, length us, event | category | flops | bytes accessed | tf_op | source)
XLA Modules:
  0.0 88.1 jit_solution(4551826617829433676)
XLA Ops:
  1.7 3.6 %shard_map.130 = (f32[2,4,256,128]{3,2,1,0:T(8,128)S(1)}, f32[2,4,256,128]{3,2,1,0:T(8,128)S(1)}, f32[2,4,256,128]{3,2,1,0:T(8,128)S(1)}, f32[2,4,256,128]{3,2,1,0:T(8,128)S(1)}) custom-call(bf16[512,8192]{1,0:T(8,128)(2,1)} %a_ref.5, bf16[512,512]{1,0:T(8,128)(2,1)S(1)} %copy-done), custom_call_target="tpu_custom_call" | custom-call | flops 1073741824 | bytes 3670016 | tf_op jit(solution)/shard_map/pallas_call | solution.py:94
  5.4 2.2 %collective-permute-start.10 = (f16[2,4,256,128]{3,2,1,0:T(8,128)(2,1)S(1)}, f16[2,4,256,128]{3,2,1,0:T(8,128)(2,1)S(1)}, u32[]{:S(2)}, u32[]{:S(2)}) collective-permute-start(f16[2,4,256,128]{3,2,1,0:T(8,128)(2,1)S(1)} %convert_element_type.298), channel_id=1, source_target_pairs={{0,16},{1,17},{2,18},{3,19},{4,20},{5,21},{6,22},{7,23},{8,24},{9,... | collective-permute-start | bytes 1572872 | tf_op jit(solution)/shard_map/ppermute | solution.py:35
  7.6 1.5 %collective-permute-start.12 = (f16[2,4,256,128]{3,2,1,0:T(8,128)(2,1)S(1)}, f16[2,4,256,128]{3,2,1,0:T(8,128)(2,1)S(1)}, u32[]{:S(2)}, u32[]{:S(2)}) collective-permute-start(f16[2,4,256,128]{3,2,1,0:T(8,128)(2,1)S(1)} %convert_element_type.302), channel_id=1, source_target_pairs={{0,48},{1,49},{2,50},{3,51},{4,52},{5,53},{6,54},{7,55},{8,56},{9,... | collective-permute-start | bytes 1572872 | tf_op jit(solution)/shard_map/ppermute | solution.py:35
  10.6 1.5 %collective-permute-start.2 = (f16[2,4,256,128]{3,2,1,0:T(8,128)(2,1)S(1)}, f16[2,4,256,128]{3,2,1,0:T(8,128)(2,1)S(1)}, u32[]{:S(2)}, u32[]{:S(2)}) collective-permute-start(f16[2,4,256,128]{3,2,1,0:T(8,128)(2,1)S(1)} %convert_element_type.267), channel_id=1, source_target_pairs={{0,12},{1,13},{2,14},{3,15},{4,0},{5,1},{6,2},{7,3},{8,4},{9,5},{1... | collective-permute-start | bytes 1572872 | tf_op jit(solution)/shard_map/ppermute | solution.py:35
  12.2 5.7 %shard_map.129 = (f32[4,4,256,128]{3,2,1,0:T(8,128)S(1)}, f32[4,4,256,128]{3,2,1,0:T(8,128)S(1)}, f32[4,4,256,128]{3,2,1,0:T(8,128)S(1)}, f32[4,4,256,128]{3,2,1,0:T(8,128)S(1)}) custom-call(bf16[512,8192]{1,0:T(8,128)(2,1)} %a_ref.5, bf16[512,512]{1,0:T(8,128)(2,1)S(1)} %copy-done.1), custom_call_target="tpu_custom_call" | custom-call | flops 2147483648 | bytes 6291456 | tf_op jit(solution)/shard_map/pallas_call | solution.py:94
  18.9 1.6 %collective-permute-start.11 = (f16[4,4,256,128]{3,2,1,0:T(8,128)(2,1)S(1)}, f16[4,4,256,128]{3,2,1,0:T(8,128)(2,1)S(1)}, u32[]{:S(2)}, u32[]{:S(2)}) collective-permute-start(f16[4,4,256,128]{3,2,1,0:T(8,128)(2,1)S(1)} %add_convert_fusion.1), channel_id=1, source_target_pairs={{0,16},{1,17},{2,18},{3,19},{4,20},{5,21},{6,22},{7,23},{8,24},{9,... | collective-permute-start | bytes 3145736 | tf_op jit(solution)/shard_map/ppermute | solution.py:35
  20.8 1.7 %collective-permute-start.13 = (f16[4,4,256,128]{3,2,1,0:T(8,128)(2,1)S(1)}, f16[4,4,256,128]{3,2,1,0:T(8,128)(2,1)S(1)}, u32[]{:S(2)}, u32[]{:S(2)}) collective-permute-start(f16[4,4,256,128]{3,2,1,0:T(8,128)(2,1)S(1)} %add_convert_fusion), channel_id=1, source_target_pairs={{0,48},{1,49},{2,50},{3,51},{4,52},{5,53},{6,54},{7,55},{8,56},{9,... | collective-permute-start | bytes 3145736 | tf_op jit(solution)/shard_map/ppermute | solution.py:35
  22.9 2.6 %collective-permute-start.1 = (f16[4,4,256,128]{3,2,1,0:T(8,128)(2,1)S(1)}, f16[4,4,256,128]{3,2,1,0:T(8,128)(2,1)S(1)}, u32[]{:S(2)}, u32[]{:S(2)}) collective-permute-start(f16[4,4,256,128]{3,2,1,0:T(8,128)(2,1)S(1)} %add_convert_fusion.3), channel_id=1, source_target_pairs={{0,4},{1,5},{2,6},{3,7},{4,8},{5,9},{6,10},{7,11},{8,12},{9,13},{1... | collective-permute-start | bytes 3145736 | tf_op jit(solution)/shard_map/ppermute | solution.py:35
  25.8 1.5 %collective-permute-start.3 = (f16[4,4,256,128]{3,2,1,0:T(8,128)(2,1)S(1)}, f16[4,4,256,128]{3,2,1,0:T(8,128)(2,1)S(1)}, u32[]{:S(2)}, u32[]{:S(2)}) collective-permute-start(f16[4,4,256,128]{3,2,1,0:T(8,128)(2,1)S(1)} %add_convert_fusion.2), channel_id=1, source_target_pairs={{0,12},{1,13},{2,14},{3,15},{4,0},{5,1},{6,2},{7,3},{8,4},{9,5},{1... | collective-permute-start | bytes 3145736 | tf_op jit(solution)/shard_map/ppermute | solution.py:35
  27.3 3.6 %shard_map.128 = (f32[4,4,256,128]{3,2,1,0:T(8,128)S(1)}, f32[4,4,256,128]{3,2,1,0:T(8,128)S(1)}) custom-call(bf16[512,8192]{1,0:T(8,128)(2,1)} %a_ref.5, bf16[512,512]{1,0:T(8,128)(2,1)S(1)} %copy-done.1), custom_call_target="tpu_custom_call" | custom-call | flops 1073741824 | bytes 3670016 | tf_op jit(solution)/shard_map/pallas_call | solution.py:94
  30.9 11.7 %collective-permute-done.11 = f16[4,4,256,128]{3,2,1,0:T(8,128)(2,1)S(1)} collective-permute-done((f16[4,4,256,128]{3,2,1,0:T(8,128)(2,1)S(1)}, f16[4,4,256,128]{3,2,1,0:T(8,128)(2,1)S(1)}, u32[]{:S(2)}, u32[]{:S(2)}) %collective-permute-start.11) | collective-permute-done | bytes 1048608 | tf_op jit(solution)/shard_map/ppermute | solution.py:35
  44.1 2.9 %collective-permute-start.14 = (f16[4,256,128]{2,1,0:T(8,128)(2,1)S(1)}, f16[4,256,128]{2,1,0:T(8,128)(2,1)S(1)}, u32[]{:S(2)}, u32[]{:S(2)}) collective-permute-start(f16[4,256,128]{2,1,0:T(8,128)(2,1)S(1)} %get-tuple-element.35), channel_id=1, source_target_pairs={{0,4},{1,5},{2,6},{3,7},{4,8},{5,9},{6,10},{7,11},{8,12},{9,13},{1... | collective-permute-start | bytes 786440 | tf_op jit(solution)/shard_map/ppermute | solution.py:35
  48.3 1.7 %collective-permute-start.16 = (f16[4,256,128]{2,1,0:T(8,128)(2,1)S(1)}, f16[4,256,128]{2,1,0:T(8,128)(2,1)S(1)}, u32[]{:S(2)}, u32[]{:S(2)}) collective-permute-start(f16[4,256,128]{2,1,0:T(8,128)(2,1)S(1)} %get-tuple-element.36), channel_id=1, source_target_pairs={{0,8},{1,9},{2,10},{3,11},{4,12},{5,13},{6,14},{7,15},{8,0},{9,1},... | collective-permute-start | bytes 786440 | tf_op jit(solution)/shard_map/ppermute | solution.py:35
  50.6 2.8 %collective-permute-start.5 = (f16[4,256,128]{2,1,0:T(8,128)(2,1)S(1)}, f16[4,256,128]{2,1,0:T(8,128)(2,1)S(1)}, u32[]{:S(2)}, u32[]{:S(2)}) collective-permute-start(f16[4,256,128]{2,1,0:T(8,128)(2,1)S(1)} %get-tuple-element.41), channel_id=1, source_target_pairs={{0,48},{1,49},{2,50},{3,51},{4,52},{5,53},{6,54},{7,55},{8,56},{9,... | collective-permute-start | bytes 786440 | tf_op jit(solution)/shard_map/ppermute | solution.py:35
  55.2 5.8 %collective-permute-done.16 = f16[4,256,128]{2,1,0:T(8,128)(2,1)S(1)} collective-permute-done((f16[4,256,128]{2,1,0:T(8,128)(2,1)S(1)}, f16[4,256,128]{2,1,0:T(8,128)(2,1)S(1)}, u32[]{:S(2)}, u32[]{:S(2)}) %collective-permute-start.16) | collective-permute-done | bytes 262176 | tf_op jit(solution)/shard_map/ppermute | solution.py:35
  61.1 1.7 %collective-permute-start.17 = (f16[2,256,128]{2,1,0:T(8,128)(2,1)S(1)}, f16[2,256,128]{2,1,0:T(8,128)(2,1)S(1)}, u32[]{:S(2)}, u32[]{:S(2)}) collective-permute-start(f16[2,256,128]{2,1,0:T(8,128)(2,1)S(1)} %pad_maximum_fusion), channel_id=1, source_target_pairs={{0,1},{1,0},{2,3},{3,2},{4,5},{5,4},{6,7},{7,6},{8,9},{9,8},{10,11... | collective-permute-start | bytes 393224 | tf_op jit(solution)/shard_map/ppermute | solution.py:127
  63.1 3.0 %collective-permute-start.7 = (f16[256,128]{1,0:T(8,128)(2,1)S(1)}, f16[256,128]{1,0:T(8,128)(2,1)S(1)}, u32[]{:S(2)}, u32[]{:S(2)}) collective-permute-start(f16[256,128]{1,0:T(8,128)(2,1)S(1)} %get-tuple-element.45), channel_id=1, source_target_pairs={{0,2},{1,3},{2,0},{3,1},{4,6},{5,7},{6,4},{7,5},{8,10},{9,11},{10,... | collective-permute-start | bytes 196616 | tf_op jit(solution)/shard_map/ppermute | solution.py:127
  66.1 1.4 %collective-permute-start.8 = (f16[256,128]{1,0:T(8,128)(2,1)S(1)}, f16[256,128]{1,0:T(8,128)(2,1)S(1)}, u32[]{:S(2)}, u32[]{:S(2)}) collective-permute-start(f16[256,128]{1,0:T(8,128)(2,1)S(1)} %get-tuple-element.47), channel_id=1, source_target_pairs={{0,3},{1,2},{2,1},{3,0},{4,7},{5,6},{6,5},{7,4},{8,11},{9,10},{10,... | collective-permute-start | bytes 196616 | tf_op jit(solution)/shard_map/ppermute | solution.py:127
  67.8 2.0 %collective-permute-start.18 = (f16[256,128]{1,0:T(8,128)(2,1)S(1)}, f16[256,128]{1,0:T(8,128)(2,1)S(1)}, u32[]{:S(2)}, u32[]{:S(2)}) collective-permute-start(f16[256,128]{1,0:T(8,128)(2,1)S(1)} %fusion.47), channel_id=1, source_target_pairs={{0,2},{1,3},{2,0},{3,1},{4,6},{5,7},{6,4},{7,5},{8,10},{9,11},{10,... | collective-permute-start | bytes 196616 | tf_op jit(solution)/shard_map/ppermute | solution.py:127
  69.8 1.5 %collective-permute-done.8 = f16[256,128]{1,0:T(8,128)(2,1)S(1)} collective-permute-done((f16[256,128]{1,0:T(8,128)(2,1)S(1)}, f16[256,128]{1,0:T(8,128)(2,1)S(1)}, u32[]{:S(2)}, u32[]{:S(2)}) %collective-permute-start.8) | collective-permute-done | bytes 65568 | tf_op jit(solution)/shard_map/ppermute | solution.py:127
  71.3 1.4 %collective-permute-done.9 = f16[256,128]{1,0:T(8,128)(2,1)S(1)} collective-permute-done((f16[256,128]{1,0:T(8,128)(2,1)S(1)}, f16[256,128]{1,0:T(8,128)(2,1)S(1)}, u32[]{:S(2)}, u32[]{:S(2)}) %collective-permute-start.9) | collective-permute-done | bytes 65568 | tf_op jit(solution)/shard_map/ppermute | solution.py:127
  73.8 5.4 %collective-permute-start.19 = (f32[32,128]{1,0:T(8,128)S(1)}, f32[32,128]{1,0:T(8,128)S(1)}, u32[]{:S(2)}, u32[]{:S(2)}) collective-permute-start(f32[32,128]{1,0:T(8,128)S(1)} %shard_map.131), channel_id=1, source_target_pairs={{0,64},{64,0},{128,192},{192,128},{1,65},{65,1},{129,193},{193,129... | collective-permute-start | bytes 49160 | tf_op jit(solution)/shard_map/ppermute | solution.py:213
  80.0 5.4 %collective-permute-start.20 = (f32[32,128]{1,0:T(8,128)S(1)}, f32[32,128]{1,0:T(8,128)S(1)}, u32[]{:S(2)}, u32[]{:S(2)}) collective-permute-start(f32[32,128]{1,0:T(8,128)S(1)} %add.269.here), channel_id=1, source_target_pairs={{0,128},{64,192},{128,0},{192,64},{1,129},{65,193},{129,1},{193,65... | collective-permute-start | bytes 49160 | tf_op jit(solution)/shard_map/ppermute | solution.py:213
  86.6 1.4 %shard_map.132 = (f32[128,512]{1,0:T(8,128)}, f32[128,512]{1,0:T(8,128)}, f32[32,128]{1,0:T(8,128)}) custom-call(f32[32,128]{1,0:T(8,128)S(1)} %add.269.here, f32[32,128]{1,0:T(8,128)S(1)} %collective-permute-done.20.there, f32[128,512]{1,0:T(8,128)S(1)} %copy-done.4, f32[128,512]{1,0:T(8,128)S(1)} %copy-done.7, f32[32,128]{1,0:T(8,128)S(1)} %copy-done.8, ...), custom_call_target="tpu_custom_call" | custom-call | tf_op jit(solution)/shard_map/pallas_call | solution.py:203
  (59 shorter events, 13.4 us)
Async XLA Ops:
  5.4 13.2 %collective-permute-start.10 = (f16[2,4,256,128]{3,2,1,0:T(8,128)(2,1)S(1)}, f16[2,4,256,128]{3,2,1,0:T(8,128)(2,1)S(1)}, u32[]{:S(2)}, u32[]{:S(2)}) collective-permute-start(f16[2,4,256,128]{3,2,1,0:T(8,128)(2,1)S(1)} %convert_element_type.298), channel_id=1, source_target_pairs={{0,16},{1,17},{2,18},{3,19},{4,20},{5,21},{6,22},{7,23},{8,24},{9,... | collective-permute-start | bytes 1572872 | tf_op jit(solution)/shard_map/ppermute | solution.py:35
  7.6 12.9 %collective-permute-start.12 = (f16[2,4,256,128]{3,2,1,0:T(8,128)(2,1)S(1)}, f16[2,4,256,128]{3,2,1,0:T(8,128)(2,1)S(1)}, u32[]{:S(2)}, u32[]{:S(2)}) collective-permute-start(f16[2,4,256,128]{3,2,1,0:T(8,128)(2,1)S(1)} %convert_element_type.302), channel_id=1, source_target_pairs={{0,48},{1,49},{2,50},{3,51},{4,52},{5,53},{6,54},{7,55},{8,56},{9,... | collective-permute-start | bytes 1572872 | tf_op jit(solution)/shard_map/ppermute | solution.py:35
  9.3 13.3 %collective-permute-start = (f16[2,4,256,128]{3,2,1,0:T(8,128)(2,1)S(1)}, f16[2,4,256,128]{3,2,1,0:T(8,128)(2,1)S(1)}, u32[]{:S(2)}, u32[]{:S(2)}) collective-permute-start(f16[2,4,256,128]{3,2,1,0:T(8,128)(2,1)S(1)} %convert_element_type.263), channel_id=1, source_target_pairs={{0,4},{1,5},{2,6},{3,7},{4,8},{5,9},{6,10},{7,11},{8,12},{9,13},{1... | collective-permute-start | bytes 1572872 | tf_op jit(solution)/shard_map/ppermute | solution.py:35
  10.6 14.8 %collective-permute-start.2 = (f16[2,4,256,128]{3,2,1,0:T(8,128)(2,1)S(1)}, f16[2,4,256,128]{3,2,1,0:T(8,128)(2,1)S(1)}, u32[]{:S(2)}, u32[]{:S(2)}) collective-permute-start(f16[2,4,256,128]{3,2,1,0:T(8,128)(2,1)S(1)} %convert_element_type.267), channel_id=1, source_target_pairs={{0,12},{1,13},{2,14},{3,15},{4,0},{5,1},{6,2},{7,3},{8,4},{9,5},{1... | collective-permute-start | bytes 1572872 | tf_op jit(solution)/shard_map/ppermute | solution.py:35
  18.9 23.7 %collective-permute-start.11 = (f16[4,4,256,128]{3,2,1,0:T(8,128)(2,1)S(1)}, f16[4,4,256,128]{3,2,1,0:T(8,128)(2,1)S(1)}, u32[]{:S(2)}, u32[]{:S(2)}) collective-permute-start(f16[4,4,256,128]{3,2,1,0:T(8,128)(2,1)S(1)} %add_convert_fusion.1), channel_id=1, source_target_pairs={{0,16},{1,17},{2,18},{3,19},{4,20},{5,21},{6,22},{7,23},{8,24},{9,... | collective-permute-start | bytes 3145736 | tf_op jit(solution)/shard_map/ppermute | solution.py:35
  20.8 22.8 %collective-permute-start.13 = (f16[4,4,256,128]{3,2,1,0:T(8,128)(2,1)S(1)}, f16[4,4,256,128]{3,2,1,0:T(8,128)(2,1)S(1)}, u32[]{:S(2)}, u32[]{:S(2)}) collective-permute-start(f16[4,4,256,128]{3,2,1,0:T(8,128)(2,1)S(1)} %add_convert_fusion), channel_id=1, source_target_pairs={{0,48},{1,49},{2,50},{3,51},{4,52},{5,53},{6,54},{7,55},{8,56},{9,... | collective-permute-start | bytes 3145736 | tf_op jit(solution)/shard_map/ppermute | solution.py:35
  22.9 27.0 %collective-permute-start.1 = (f16[4,4,256,128]{3,2,1,0:T(8,128)(2,1)S(1)}, f16[4,4,256,128]{3,2,1,0:T(8,128)(2,1)S(1)}, u32[]{:S(2)}, u32[]{:S(2)}) collective-permute-start(f16[4,4,256,128]{3,2,1,0:T(8,128)(2,1)S(1)} %add_convert_fusion.3), channel_id=1, source_target_pairs={{0,4},{1,5},{2,6},{3,7},{4,8},{5,9},{6,10},{7,11},{8,12},{9,13},{1... | collective-permute-start | bytes 3145736 | tf_op jit(solution)/shard_map/ppermute | solution.py:35
  25.8 24.2 %collective-permute-start.3 = (f16[4,4,256,128]{3,2,1,0:T(8,128)(2,1)S(1)}, f16[4,4,256,128]{3,2,1,0:T(8,128)(2,1)S(1)}, u32[]{:S(2)}, u32[]{:S(2)}) collective-permute-start(f16[4,4,256,128]{3,2,1,0:T(8,128)(2,1)S(1)} %add_convert_fusion.2), channel_id=1, source_target_pairs={{0,12},{1,13},{2,14},{3,15},{4,0},{5,1},{6,2},{7,3},{8,4},{9,5},{1... | collective-permute-start | bytes 3145736 | tf_op jit(solution)/shard_map/ppermute | solution.py:35
  44.1 10.4 %collective-permute-start.14 = (f16[4,256,128]{2,1,0:T(8,128)(2,1)S(1)}, f16[4,256,128]{2,1,0:T(8,128)(2,1)S(1)}, u32[]{:S(2)}, u32[]{:S(2)}) collective-permute-start(f16[4,256,128]{2,1,0:T(8,128)(2,1)S(1)} %get-tuple-element.35), channel_id=1, source_target_pairs={{0,4},{1,5},{2,6},{3,7},{4,8},{5,9},{6,10},{7,11},{8,12},{9,13},{1... | collective-permute-start | bytes 786440 | tf_op jit(solution)/shard_map/ppermute | solution.py:35
  46.9 8.3 %collective-permute-start.15 = (f16[4,256,128]{2,1,0:T(8,128)(2,1)S(1)}, f16[4,256,128]{2,1,0:T(8,128)(2,1)S(1)}, u32[]{:S(2)}, u32[]{:S(2)}) collective-permute-start(f16[4,256,128]{2,1,0:T(8,128)(2,1)S(1)} %get-tuple-element.37), channel_id=1, source_target_pairs={{0,12},{1,13},{2,14},{3,15},{4,0},{5,1},{6,2},{7,3},{8,4},{9,5},{1... | collective-permute-start | bytes 786440 | tf_op jit(solution)/shard_map/ppermute | solution.py:35
  48.3 12.7 %collective-permute-start.16 = (f16[4,256,128]{2,1,0:T(8,128)(2,1)S(1)}, f16[4,256,128]{2,1,0:T(8,128)(2,1)S(1)}, u32[]{:S(2)}, u32[]{:S(2)}) collective-permute-start(f16[4,256,128]{2,1,0:T(8,128)(2,1)S(1)} %get-tuple-element.36), channel_id=1, source_target_pairs={{0,8},{1,9},{2,10},{3,11},{4,12},{5,13},{6,14},{7,15},{8,0},{9,1},... | collective-permute-start | bytes 786440 | tf_op jit(solution)/shard_map/ppermute | solution.py:35
  50.4 22.4 %copy-start.2 = (f32[1,128,512]{2,1,0:T(8,128)S(1)}, f32[1,128,512]{2,1,0:T(8,128)}, u32[]{:S(2)}) copy-start(f32[1,128,512]{2,1,0:T(8,128)} %param.12) | copy-start | bytes 786436
  50.4 22.4 %copy-start.3 = (f32[1,128,512]{2,1,0:T(8,128)S(1)}, f32[1,128,512]{2,1,0:T(8,128)}, u32[]{:S(2)}) copy-start(f32[1,128,512]{2,1,0:T(8,128)} %param.13) | copy-start | bytes 786436
  50.5 12.3 %collective-permute-start.4 = (f16[4,256,128]{2,1,0:T(8,128)(2,1)S(1)}, f16[4,256,128]{2,1,0:T(8,128)(2,1)S(1)}, u32[]{:S(2)}, u32[]{:S(2)}) collective-permute-start(f16[4,256,128]{2,1,0:T(8,128)(2,1)S(1)} %get-tuple-element.39), channel_id=1, source_target_pairs={{0,16},{1,17},{2,18},{3,19},{4,20},{5,21},{6,22},{7,23},{8,24},{9,... | collective-permute-start | bytes 786440 | tf_op jit(solution)/shard_map/ppermute | solution.py:35
  50.6 12.2 %collective-permute-start.5 = (f16[4,256,128]{2,1,0:T(8,128)(2,1)S(1)}, f16[4,256,128]{2,1,0:T(8,128)(2,1)S(1)}, u32[]{:S(2)}, u32[]{:S(2)}) collective-permute-start(f16[4,256,128]{2,1,0:T(8,128)(2,1)S(1)} %get-tuple-element.41), channel_id=1, source_target_pairs={{0,48},{1,49},{2,50},{3,51},{4,52},{5,53},{6,54},{7,55},{8,56},{9,... | collective-permute-start | bytes 786440 | tf_op jit(solution)/shard_map/ppermute | solution.py:35
  54.4 8.6 %collective-permute-start.6 = (f16[4,256,128]{2,1,0:T(8,128)(2,1)S(1)}, f16[4,256,128]{2,1,0:T(8,128)(2,1)S(1)}, u32[]{:S(2)}, u32[]{:S(2)}) collective-permute-start(f16[4,256,128]{2,1,0:T(8,128)(2,1)S(1)} %get-tuple-element.40), channel_id=1, source_target_pairs={{0,32},{1,33},{2,34},{3,35},{4,36},{5,37},{6,38},{7,39},{8,40},{9,... | collective-permute-start | bytes 786440 | tf_op jit(solution)/shard_map/ppermute | solution.py:35
  61.1 6.6 %collective-permute-start.17 = (f16[2,256,128]{2,1,0:T(8,128)(2,1)S(1)}, f16[2,256,128]{2,1,0:T(8,128)(2,1)S(1)}, u32[]{:S(2)}, u32[]{:S(2)}) collective-permute-start(f16[2,256,128]{2,1,0:T(8,128)(2,1)S(1)} %pad_maximum_fusion), channel_id=1, source_target_pairs={{0,1},{1,0},{2,3},{3,2},{4,5},{5,4},{6,7},{7,6},{8,9},{9,8},{10,11... | collective-permute-start | bytes 393224 | tf_op jit(solution)/shard_map/ppermute | solution.py:127
  63.1 23.5 %copy-start.7 = (f32[128,512]{1,0:T(8,128)S(1)}, f32[128,512]{1,0:T(8,128)}, u32[]{:S(2)}) copy-start(f32[128,512]{1,0:T(8,128)} %moment.1) | copy-start | bytes 786436
  63.1 6.7 %collective-permute-start.7 = (f16[256,128]{1,0:T(8,128)(2,1)S(1)}, f16[256,128]{1,0:T(8,128)(2,1)S(1)}, u32[]{:S(2)}, u32[]{:S(2)}) collective-permute-start(f16[256,128]{1,0:T(8,128)(2,1)S(1)} %get-tuple-element.45), channel_id=1, source_target_pairs={{0,2},{1,3},{2,0},{3,1},{4,6},{5,7},{6,4},{7,5},{8,10},{9,11},{10,... | collective-permute-start | bytes 196616 | tf_op jit(solution)/shard_map/ppermute | solution.py:127
  66.1 5.2 %collective-permute-start.8 = (f16[256,128]{1,0:T(8,128)(2,1)S(1)}, f16[256,128]{1,0:T(8,128)(2,1)S(1)}, u32[]{:S(2)}, u32[]{:S(2)}) collective-permute-start(f16[256,128]{1,0:T(8,128)(2,1)S(1)} %get-tuple-element.47), channel_id=1, source_target_pairs={{0,3},{1,2},{2,1},{3,0},{4,7},{5,6},{6,5},{7,4},{8,11},{9,10},{10,... | collective-permute-start | bytes 196616 | tf_op jit(solution)/shard_map/ppermute | solution.py:127
  67.5 5.1 %collective-permute-start.9 = (f16[256,128]{1,0:T(8,128)(2,1)S(1)}, f16[256,128]{1,0:T(8,128)(2,1)S(1)}, u32[]{:S(2)}, u32[]{:S(2)}) collective-permute-start(f16[256,128]{1,0:T(8,128)(2,1)S(1)} %get-tuple-element.46), channel_id=1, source_target_pairs={{0,1},{1,0},{2,3},{3,2},{4,5},{5,4},{6,7},{7,6},{8,9},{9,8},{10,11... | collective-permute-start | bytes 196616 | tf_op jit(solution)/shard_map/ppermute | solution.py:127
  67.8 5.0 %collective-permute-start.18 = (f16[256,128]{1,0:T(8,128)(2,1)S(1)}, f16[256,128]{1,0:T(8,128)(2,1)S(1)}, u32[]{:S(2)}, u32[]{:S(2)}) collective-permute-start(f16[256,128]{1,0:T(8,128)(2,1)S(1)} %fusion.47), channel_id=1, source_target_pairs={{0,2},{1,3},{2,0},{3,1},{4,6},{5,7},{6,4},{7,5},{8,10},{9,11},{10,... | collective-permute-start | bytes 196616 | tf_op jit(solution)/shard_map/ppermute | solution.py:127
  73.8 6.2 %collective-permute-start.19 = (f32[32,128]{1,0:T(8,128)S(1)}, f32[32,128]{1,0:T(8,128)S(1)}, u32[]{:S(2)}, u32[]{:S(2)}) collective-permute-start(f32[32,128]{1,0:T(8,128)S(1)} %shard_map.131), channel_id=1, source_target_pairs={{0,64},{64,0},{128,192},{192,128},{1,65},{65,1},{129,193},{193,129... | collective-permute-start | bytes 49160 | tf_op jit(solution)/shard_map/ppermute | solution.py:213
  80.0 6.6 %collective-permute-start.20 = (f32[32,128]{1,0:T(8,128)S(1)}, f32[32,128]{1,0:T(8,128)S(1)}, u32[]{:S(2)}, u32[]{:S(2)}) collective-permute-start(f32[32,128]{1,0:T(8,128)S(1)} %add.269.here), channel_id=1, source_target_pairs={{0,128},{64,192},{128,0},{192,64},{1,129},{65,193},{129,1},{193,65... | collective-permute-start | bytes 49160 | tf_op jit(solution)/shard_map/ppermute | solution.py:213
  (6 other events, 95.4 us)
